TPU v7x, 32 devices: a whole 2x2x4 slice. The times are simulated.
32 devices in a mesh: section: 2 (over x), dp: 8 (over z, y), expert: 2 (over core).
Axes of the slice: x: 2, y: 2, z: 4, core: 2. Of those that a mesh axis runs over, the one named last changes fastest.
Arguments:
- tokens: bfloat16 [2, 2048, 1152], P(None, ('dp', 'expert')), may hold values from -6 to 6
- cotangent: bfloat16 [2, 2048, 1152], P(None, ('dp', 'expert')), may hold values from -6 to 6
- routes: int32 [2, 2, 2048], P('section', None, ('dp', 'expert')), may hold values from 0 to 7, as said below
- slots: int32 [2, 2, 2048], P('section', None, ('dp', 'expert')), may hold values from 0 to 11, as said below
- drops: int32 [2, 2, 2048], P('section', None, ('dp', 'expert')), may hold values from 0 to 1, as said below
- norm_gain: float32 [2, 1152], P('section', 'dp'), may hold values from 0.5 to 1.5
- w_in: float32 [2, 1152, 2, 2304], P('section', None, None, ('dp', 'expert')), may hold values from -0.1875 to 0.1875
- conv_w: float32 [2, 4, 2304], P('section', None, ('dp', 'expert')), may hold values from -3 to 3
- conv_b: float32 [2, 2304], P('section', ('dp', 'expert')), may hold values from -3 to 3
- x_proj: float32 [2, 2304, 104], P('section', ('dp', 'expert')), may hold values from -0.125 to 0.125
- dt_proj: float32 [2, 72, 2304], P('section', None, ('dp', 'expert')), may hold values from -0.75 to 0.75
- dt_bias: float32 [2, 2304], P('section', ('dp', 'expert')), may hold values from -6 to -1
- a_log: float32 [2, 16, 2304], P('section', None, ('dp', 'expert')), may hold values from -5 to 1
- skip: float32 [2, 2304], P('section', ('dp', 'expert')), may hold values from 0.5 to 1.5
- w_out: float32 [2, 2304, 1152], P('section', ('dp', 'expert')), may hold values from -0.375 to 0.375
- moe_gain: float32 [2, 1152], P('section', 'dp'), may hold values from 0.5 to 1.5
- router: float32 [2, 1152, 8], P('section', 'dp'), may hold values from -0.09375 to 0.09375
- w_up: float32 [2, 8, 1152, 3072], P('section', 'expert', 'dp'), may hold values from -0.1875 to 0.1875
- w_down: float32 [2, 8, 3072, 1152], P('section', 'expert', 'dp'), may hold values from -0.875 to 0.875
Outputs:
- segment_outputs: bfloat16 [2, 2, 2048, 1152], P('section', None, ('dp', 'expert'))
- input_grads: bfloat16 [2, 2, 2048, 1152], P('section', None, ('dp', 'expert'))
- norm_gain_grad: float32 [2, 1152], P('section', 'dp')
- w_in_grad: float32 [2, 1152, 2, 2304], P('section', None, None, ('dp', 'expert'))
- conv_w_grad: float32 [2, 4, 2304], P('section', None, ('dp', 'expert'))
- conv_b_grad: float32 [2, 2304], P('section', ('dp', 'expert'))
- x_proj_grad: float32 [2, 2304, 104], P('section', ('dp', 'expert'))
- dt_proj_grad: float32 [2, 72, 2304], P('section', None, ('dp', 'expert'))
- dt_bias_grad: float32 [2, 2304], P('section', ('dp', 'expert'))
- a_log_grad: float32 [2, 16, 2304], P('section', None, ('dp', 'expert'))
- skip_grad: float32 [2, 2304], P('section', ('dp', 'expert'))
- w_out_grad: float32 [2, 2304, 1152], P('section', ('dp', 'expert'))
- moe_gain_grad: float32 [2, 1152], P('section', 'dp')
- router_grad: float32 [2, 1152, 8], P('section', 'dp')
- w_up_grad: float32 [2, 8, 1152, 3072], P('section', 'expert', 'dp')
- w_down_grad: float32 [2, 8, 3072, 1152], P('section', 'expert', 'dp')
Inputs may be any that keep to these rules, and one draw needn't show every extreme that they name: `routes`: each token's one expert. Within each aligned block of 128 tokens, the tokens of one expert that are kept have the distinct slots 0, 1, 2 and so on in token order; dropped tokens have slot 0. `drops`: 1 exactly for the tokens of an aligned block of 128 tokens that come after the first 12 tokens of their expert in that block.
All inputs are finite; a program needn't handle non-finite values.
Results may differ from a plain program's by a relative error of at most 0.023.
The roundings to bfloat16 on the way count: a program that leaves them out, or rounds other values in their place, can miss the bound.
Values may be sent and summed in bfloat16 or wider, within the bound.
A program may use at most 448 MiB of HBM per device.

v0:
```python
import jax
import jax.numpy as jnp
from jax import lax
from jax.sharding import PartitionSpec as P

EXPERTS = 8
CAP = 12


epsilon = 1e-05
highest = lax.Precision.HIGHEST


def prefix(shard, axis, join, neutral):
    count = lax.axis_size(axis)
    place = lax.axis_index(axis)
    ahead = count - 1 - place
    gathered = jax.tree.map(
        lambda a, kind: lax.all_gather(a.astype(kind), axis), shard, (jnp.bfloat16, jnp.bfloat16)
    )
    state = jax.tree.map(lambda a, e: jnp.zeros_like(a) + jnp.asarray(e, a.dtype), shard, neutral)

    def one(hop, state):
        source = count - 1 - hop
        return join(
            state,
            jax.tree.map(
                lambda a, own: lax.dynamic_index_in_dim(a, source, 0, False).astype(own.dtype),
                gathered,
                shard,
            ),
        )

    return lax.fori_loop(0, ahead, one, state)


def from_behind(shard, axis, by):
    count = lax.axis_size(axis)
    pairs = [(i, i + by) for i in range(count) if 0 <= i + by < count]
    return lax.ppermute(shard, axis, pairs)


def entering(shard, axis, combine, identity):
    count, here = (lax.axis_size(axis), lax.axis_index(axis))
    everything = jax.tree.map(lambda part: lax.all_gather(part, axis), shard)
    start = jax.tree.map(
        lambda part, zero: jnp.broadcast_to(jnp.asarray(zero, part.dtype), part.shape),
        shard,
        identity,
    )

    def hop(k, before):
        reached = k < here
        new = combine(before, jax.tree.map(lambda part: part[k], everything))
        return jax.tree.map(lambda a, b: jnp.where(reached, a, b), new, before)

    return lax.fori_loop(0, count, hop, start)


def normalize(values, gain):
    return values * lax.rsqrt(jnp.mean(values * values, axis=-1, keepdims=True) + epsilon) * gain


def compose(early, late):
    return (early[0] * late[0], late[0] * early[1] + late[1])


def wide_total(values):
    return lax.psum(values, "expert")


def narrow_total(values):
    return lax.psum(values, "expert")


def to_experts(buffer):
    return lax.all_to_all(buffer, "expert", split_axis=0, concat_axis=1, tiled=True)


def from_experts(buffer):
    return lax.all_to_all(buffer, "expert", split_axis=1, concat_axis=0, tiled=True)


def store(bank, index, valid, value):
    return jax.tree.map(
        lambda held, fresh: held.at[index].set(jnp.where(valid, fresh, held[index])), bank, value
    )


def share_grads(grads):
    (
        grad_norm,
        grad_in,
        grad_conv,
        grad_conv_bias,
        grad_xproj,
        grad_dtproj,
        grad_dtbias,
        grad_alog,
        grad_skip,
        grad_out,
        grad_moe,
        grad_router,
    ) = grads
    return (
        lax.psum_scatter(
            grad_norm.astype(jnp.bfloat16), "dp", scatter_dimension=0, tiled=True
        ).astype(jnp.float32),
        lax.psum_scatter(
            grad_in.astype(jnp.bfloat16), "dp", scatter_dimension=2, tiled=True
        ).astype(jnp.float32),
        lax.psum_scatter(
            grad_conv.astype(jnp.bfloat16), "dp", scatter_dimension=1, tiled=True
        ).astype(jnp.float32),
        lax.psum_scatter(
            grad_conv_bias.astype(jnp.bfloat16), "dp", scatter_dimension=0, tiled=True
        ).astype(jnp.float32),
        lax.psum_scatter(
            grad_xproj.astype(jnp.bfloat16), "dp", scatter_dimension=0, tiled=True
        ).astype(jnp.float32),
        lax.psum_scatter(
            grad_dtproj.astype(jnp.bfloat16), "dp", scatter_dimension=1, tiled=True
        ).astype(jnp.float32),
        lax.psum_scatter(
            grad_dtbias.astype(jnp.bfloat16), "dp", scatter_dimension=0, tiled=True
        ).astype(jnp.float32),
        lax.psum_scatter(
            grad_alog.astype(jnp.bfloat16), "dp", scatter_dimension=1, tiled=True
        ).astype(jnp.float32),
        lax.psum_scatter(
            grad_skip.astype(jnp.bfloat16), "dp", scatter_dimension=0, tiled=True
        ).astype(jnp.float32),
        lax.psum_scatter(
            grad_out.astype(jnp.bfloat16), "dp", scatter_dimension=0, tiled=True
        ).astype(jnp.float32),
        lax.psum_scatter(
            grad_moe.astype(jnp.bfloat16), "dp", scatter_dimension=0, tiled=True
        ).astype(jnp.float32),
        lax.psum_scatter(
            grad_router.astype(jnp.bfloat16), "dp", scatter_dimension=0, tiled=True
        ).astype(jnp.float32),
    )


def convolve(conv_in, rim, conv_w, conv_b):
    taps = conv_w.shape[0]
    length = conv_in.shape[0]
    padded = jnp.concatenate([rim, conv_in], 0)
    weights = conv_w.astype(jnp.float32)
    summed = conv_b.astype(jnp.float32)[None] + weights[0] * padded[0:length]
    for tap in range(1, taps):
        summed = summed + weights[tap] * padded[tap : tap + length]
    return (summed, padded)


def selective_inputs(projected, dt_proj, dt_bias, a_log):
    rank = dt_proj.shape[0]
    states = a_log.shape[0]
    dt_low = projected[:, :rank].astype(jnp.bfloat16)
    input_map = projected[:, rank : rank + states]
    output_map = projected[:, rank + states :]
    dt_raw = jnp.dot(dt_low, dt_proj, preferred_element_type=jnp.float32)
    step_size = jax.nn.softplus(dt_raw + dt_bias.astype(jnp.float32)[None])
    rates = -jnp.exp(a_log.astype(jnp.float32))
    return (dt_low, dt_raw, step_size, input_map, output_map, rates)


def split_blocks(values, span):
    return values.reshape((values.shape[0] // span, span) + values.shape[1:])


def block_span(length):
    return min(length, max(16, length // 16))


def local_states(step_size, input_map, output_map, signal, rates, start):
    length, width = step_size.shape
    span = block_span(length)

    def advance(state, pieces):
        step_blk, in_blk, out_blk, sig_blk = pieces
        first = state
        outputs = []
        for tick in range(span):
            decay = jnp.exp(step_blk[tick][None] * rates)
            state = decay * state + (step_blk[tick] * sig_blk[tick])[None] * in_blk[tick][:, None]
            outputs.append(jnp.sum(state * out_blk[tick][:, None], 0))
        return (state, (jnp.stack(outputs, 0), first))

    pieces = (
        split_blocks(step_size, span),
        split_blocks(input_map, span),
        split_blocks(output_map, span),
        split_blocks(signal, span),
    )
    final, (outputs, starts) = lax.scan(advance, start, pieces)
    return (outputs.reshape(length, width), final, starts)


def scan_backward(step_size, input_map, output_map, signal, rates, starts, d_out):
    length, width = step_size.shape
    span = block_span(length)
    sums = jnp.cumsum(step_size, 0)
    leak = jnp.einsum(
        "tn,tne->ne",
        output_map,
        jnp.exp(rates[None] * sums[:, None, :]) * d_out[:, None, :],
        precision=highest,
    )
    inflow = prefix(
        (jnp.exp(rates * sums[-1][None]), leak),
        "dp",
        compose,
        (jnp.ones_like(rates), jnp.zeros_like(rates)),
    )[1]

    def retreat(carry, pieces):
        step_blk, in_blk, out_blk, sig_blk, dy_blk, state = pieces
        decays = []
        states = []
        current = state
        for tick in range(span):
            decay = jnp.exp(step_blk[tick][None] * rates)
            current = (
                decay * current + (step_blk[tick] * sig_blk[tick])[None] * in_blk[tick][:, None]
            )
            decays.append(decay)
            states.append(current)
        grad = carry
        d_step = [None] * span
        d_signal = [None] * span
        d_in = [None] * span
        d_outmap = [None] * span
        d_rates = jnp.zeros_like(rates)
        for tick in reversed(range(span)):
            grad = grad + dy_blk[tick][None, :] * out_blk[tick][:, None]
            before = states[tick - 1] if tick > 0 else state
            through_in = jnp.sum(grad * in_blk[tick][:, None], 0)
            flow = grad * before * decays[tick]
            d_step[tick] = jnp.sum(flow * rates, 0) + sig_blk[tick] * through_in
            d_signal[tick] = step_blk[tick] * through_in
            d_in[tick] = jnp.sum(grad * (step_blk[tick] * sig_blk[tick])[None], 1)
            d_outmap[tick] = jnp.sum(dy_blk[tick][None] * states[tick], 1)
            d_rates = d_rates + flow * step_blk[tick][None]
            grad = decays[tick] * grad
        return (
            grad,
            (
                jnp.stack(d_step, 0),
                jnp.stack(d_signal, 0),
                jnp.stack(d_in, 0),
                jnp.stack(d_outmap, 0),
                d_rates,
            ),
        )

    pieces = (
        split_blocks(step_size, span),
        split_blocks(input_map, span),
        split_blocks(output_map, span),
        split_blocks(signal, span),
        split_blocks(d_out, span),
        starts,
    )
    unused, (d_step, d_signal, d_in, d_outmap, d_rates) = lax.scan(
        retreat, inflow, pieces, reverse=True
    )
    return (
        d_step.reshape(length, width),
        d_signal.reshape(length, width),
        d_in.reshape(length, -1),
        d_outmap.reshape(length, -1),
        jnp.sum(d_rates, 0),
    )


def route(resid_own, gain_moe, router, chosen, placed, dropped):
    normed = normalize(resid_own, gain_moe.astype(jnp.float32))
    logits = jnp.dot(normed, router.astype(jnp.float32), precision=highest)
    probs = jax.nn.softmax(logits, axis=-1)
    keep = (1 - dropped).astype(jnp.float32)
    pick = (chosen[:, None] == jnp.arange(EXPERTS)[None]).astype(jnp.float32)
    gate = jnp.sum(probs * pick, -1) * keep
    flat = chosen * CAP + placed
    table = ((flat[:, None] == jnp.arange(EXPERTS * CAP)[None]) & (dropped[:, None] == 0)).astype(
        jnp.bfloat16
    )
    return (normed, probs, pick, keep, gate, table)


def segment_forward(own_rows, chosen, placed, dropped, weights):
    (
        gain_in,
        w_in,
        conv_w,
        conv_b,
        x_proj,
        dt_proj,
        dt_bias,
        a_log,
        skip,
        w_out,
        gain_moe,
        router,
        w_up,
        w_down,
    ) = weights
    rows_all = lax.all_gather(own_rows, "expert", axis=0, tiled=True)
    inputs = rows_all.astype(jnp.float32)
    normed_in = normalize(inputs, gain_in.astype(jnp.float32)).astype(jnp.bfloat16)
    mixed_in = jnp.einsum("ld,dke->lke", normed_in, w_in, preferred_element_type=jnp.float32)
    conv_in = mixed_in[:, 0]
    taps = conv_w.shape[0]
    rim = from_behind(conv_in[conv_in.shape[0] - taps + 1 :], "dp", 1)
    summed, padded = convolve(conv_in, rim, conv_w, conv_b)
    signal = jax.nn.silu(summed).astype(jnp.bfloat16)
    projected = narrow_total(jnp.dot(signal, x_proj, preferred_element_type=jnp.float32))
    dt_low, dt_raw, step_size, input_map, output_map, rates = selective_inputs(
        projected, dt_proj, dt_bias, a_log
    )
    signal_wide = signal.astype(jnp.float32)
    zero_state = jnp.zeros(rates.shape, jnp.float32)
    local_out, final, unused = local_states(
        step_size, input_map, output_map, signal_wide, rates, zero_state
    )
    sums = jnp.cumsum(step_size, 0)
    carried = entering(
        (jnp.exp(rates * sums[-1][None]), final), "dp", compose, (jnp.ones_like(rates), zero_state)
    )[1]
    reach = jnp.exp(rates[None] * sums[:, None, :]) * carried[None]
    scan_out = local_out + jnp.einsum("tn,tne->te", output_map, reach, precision=highest)
    gated = (
        (scan_out + skip.astype(jnp.float32)[None] * signal_wide) * jax.nn.silu(mixed_in[:, 1])
    ).astype(jnp.bfloat16)
    resid = inputs + wide_total(jnp.dot(gated, w_out, preferred_element_type=jnp.float32))
    count = own_rows.shape[0]
    start = lax.axis_index("expert") * count
    resid_own = lax.dynamic_slice_in_dim(resid, start, count, 0)
    normed_own, probs, pick, keep, gate, table = route(
        resid_own, gain_moe, router, chosen, placed, dropped
    )
    buffer = jnp.einsum(
        "ts,td->sd", table, normed_own.astype(jnp.bfloat16), preferred_element_type=jnp.float32
    )
    arrived = to_experts(buffer.astype(jnp.bfloat16).reshape(EXPERTS, CAP, -1))
    hidden_pre = jnp.einsum("erd,edf->erf", arrived, w_up, preferred_element_type=jnp.float32)
    hidden = jax.nn.gelu(hidden_pre).astype(jnp.bfloat16)
    produced = jnp.einsum(
        "erf,efd->erd", hidden, w_down, preferred_element_type=jnp.float32
    ).astype(jnp.bfloat16)
    returned = from_experts(produced).reshape(EXPERTS * CAP, -1)
    combined = jnp.dot(table, returned, preferred_element_type=jnp.float32) * gate[:, None]
    result = (resid_own + combined).astype(jnp.bfloat16)
    return (
        result,
        (rows_all, mixed_in, rim, projected, carried, resid, arrived, hidden_pre, returned),
    )


def segment_backward(upstream, kept, chosen, placed, dropped, weights, valid):
    (
        gain_in,
        w_in,
        conv_w,
        conv_b,
        x_proj,
        dt_proj,
        dt_bias,
        a_log,
        skip,
        w_out,
        gain_moe,
        router,
        w_up,
        w_down,
    ) = weights
    rows_all, mixed_in, rim, projected, carried, resid, arrived, hidden_pre, returned = kept
    count = upstream.shape[0]
    start = lax.axis_index("expert") * count
    resid_own = lax.dynamic_slice_in_dim(resid, start, count, 0)
    normed_own, probs, pick, keep, gate, table = route(
        resid_own, gain_moe, router, chosen, placed, dropped
    )
    picked = jnp.dot(table, returned, preferred_element_type=jnp.float32)
    d_gate = jnp.sum(upstream * picked, -1)
    d_slots = jnp.einsum(
        "ts,td->sd", table.astype(jnp.float32), upstream * gate[:, None], precision=highest
    )
    d_produced = to_experts(d_slots.astype(jnp.bfloat16).reshape(EXPERTS, CAP, -1))
    d_produced = jnp.where(valid, d_produced, jnp.zeros_like(d_produced))
    hidden = jax.nn.gelu(hidden_pre).astype(jnp.bfloat16)
    d_hidden = jnp.einsum("erd,efd->erf", d_produced, w_down, preferred_element_type=jnp.float32)
    d_pre = jax.vjp(jax.nn.gelu, hidden_pre)[1](d_hidden)[0].astype(jnp.bfloat16)
    d_arrived = jnp.einsum("erf,edf->erd", d_pre, w_up, preferred_element_type=jnp.float32).astype(
        jnp.bfloat16
    )
    d_sent = from_experts(d_arrived).reshape(EXPERTS * CAP, -1)
    d_choice = d_gate[:, None] * pick * keep[:, None]
    d_logits = probs * (d_choice - jnp.sum(probs * d_choice, -1, keepdims=True))
    d_normed_own = jnp.dot(table, d_sent, preferred_element_type=jnp.float32) + jnp.dot(
        d_logits, router.astype(jnp.float32).T, precision=highest
    )
    up_all, d_normed_all, d_logits_all = (
        lax.all_gather(upstream.astype(jnp.bfloat16), "expert", axis=0, tiled=True).astype(
            upstream.dtype
        ),
        lax.all_gather(d_normed_own.astype(jnp.bfloat16), "expert", axis=0, tiled=True).astype(
            d_normed_own.dtype
        ),
        lax.all_gather(d_logits.astype(jnp.bfloat16), "expert", axis=0, tiled=True).astype(
            d_logits.dtype
        ),
    )
    normed_all, norm_moe_back = jax.vjp(normalize, resid, gain_moe.astype(jnp.float32))
    d_resid_norm, grad_moe = norm_moe_back(d_normed_all)
    grad_router = jnp.dot(normed_all.T, d_logits_all, precision=highest)
    d_resid = up_all + d_resid_norm
    inputs = rows_all.astype(jnp.float32)
    normed_wide, norm_in_back = jax.vjp(normalize, inputs, gain_in.astype(jnp.float32))
    normed_in = normed_wide.astype(jnp.bfloat16)
    conv_in = mixed_in[:, 0]
    gate_in = mixed_in[:, 1]
    summed, padded = convolve(conv_in, rim, conv_w, conv_b)
    signal_act, signal_back = jax.vjp(jax.nn.silu, summed)
    signal = signal_act.astype(jnp.bfloat16)
    signal_wide = signal.astype(jnp.float32)
    dt_low, dt_raw, step_size, input_map, output_map, rates = selective_inputs(
        projected, dt_proj, dt_bias, a_log
    )
    scan_out, unused, starts = local_states(
        step_size, input_map, output_map, signal_wide, rates, carried
    )
    skip_wide = skip.astype(jnp.float32)
    total_out = scan_out + skip_wide[None] * signal_wide
    gate_act, gate_back = jax.vjp(jax.nn.silu, gate_in)
    gated = (total_out * gate_act).astype(jnp.bfloat16)
    d_mixer = d_resid.astype(jnp.bfloat16)
    grad_out = jnp.einsum("le,ld->ed", gated, d_mixer, preferred_element_type=jnp.float32)
    d_gated = jnp.einsum("ld,ed->le", d_mixer, w_out, preferred_element_type=jnp.float32)
    d_total = d_gated * gate_act
    d_gate_in = gate_back(d_gated * total_out)[0]
    grad_skip = jnp.sum(d_total * signal_wide, 0)
    d_step, d_signal, d_input_map, d_output_map, d_rates = scan_backward(
        step_size, input_map, output_map, signal_wide, rates, starts, d_total
    )
    d_signal = d_signal + d_total * skip_wide[None]
    d_raw = d_step * jax.nn.sigmoid(dt_raw + dt_bias.astype(jnp.float32)[None])
    grad_dt_bias = jnp.sum(d_raw, 0)
    d_raw_low = d_raw.astype(jnp.bfloat16)
    grad_dt_proj = jnp.einsum("lr,le->re", dt_low, d_raw_low, preferred_element_type=jnp.float32)
    d_low = jnp.einsum("le,re->lr", d_raw_low, dt_proj, preferred_element_type=jnp.float32)
    d_projected = narrow_total(jnp.concatenate([d_low, d_input_map, d_output_map], 1)).astype(
        jnp.bfloat16
    )
    grad_x_proj = jnp.einsum("le,lw->ew", signal, d_projected, preferred_element_type=jnp.float32)
    d_signal = d_signal + jnp.einsum(
        "lw,ew->le", d_projected, x_proj, preferred_element_type=jnp.float32
    )
    d_summed = signal_back(d_signal)[0]
    taps = conv_w.shape[0]
    length = conv_in.shape[0]
    ahead = from_behind(d_summed[: taps - 1], "dp", -1)
    extended = jnp.concatenate([d_summed, ahead], 0)
    weights_conv = conv_w.astype(jnp.float32)
    d_conv_in = weights_conv[taps - 1] * extended[0:length]
    for tap in range(taps - 1):
        d_conv_in = (
            d_conv_in + weights_conv[tap] * extended[taps - 1 - tap : taps - 1 - tap + length]
        )
    grad_conv = jnp.stack(
        [jnp.sum(d_summed * padded[tap : tap + length], 0) for tap in range(taps)], 0
    )
    grad_conv_bias = jnp.sum(d_summed, 0)
    d_mixed = jnp.stack([d_conv_in, d_gate_in], 1).astype(jnp.bfloat16)
    grad_in = jnp.einsum("ld,lke->dke", normed_in, d_mixed, preferred_element_type=jnp.float32)
    d_normed_in = wide_total(
        jnp.einsum("lke,dke->ld", d_mixed, w_in, preferred_element_type=jnp.float32)
    )
    d_inputs, grad_norm = norm_in_back(d_normed_in)
    d_own = lax.dynamic_slice_in_dim(d_resid + d_inputs, start, count, 0).astype(jnp.bfloat16)
    grads = (
        grad_norm,
        grad_in,
        grad_conv,
        grad_conv_bias,
        grad_x_proj,
        grad_dt_proj,
        grad_dt_bias,
        d_rates * rates,
        grad_skip,
        grad_out,
        grad_moe,
        grad_router,
    )
    return (d_own, grads, (hidden, d_produced, arrived, d_pre))


def shards(
    tokens,
    cotangent,
    routes,
    slots,
    drops,
    norm_gain,
    w_in,
    conv_w,
    conv_b,
    x_proj,
    dt_proj,
    dt_bias,
    a_log,
    skip,
    w_out,
    moe_gain,
    router,
    w_up,
    w_down,
):
    low_norm = norm_gain[0].astype(jnp.bfloat16)
    low_in = w_in[0].astype(jnp.bfloat16)
    low_conv = conv_w[0].astype(jnp.bfloat16)
    low_conv_bias = conv_b[0].astype(jnp.bfloat16)
    low_xproj = x_proj[0].astype(jnp.bfloat16)
    low_dtproj = dt_proj[0].astype(jnp.bfloat16)
    low_dtbias = dt_bias[0].astype(jnp.bfloat16)
    low_alog = a_log[0].astype(jnp.bfloat16)
    low_skip = skip[0].astype(jnp.bfloat16)
    low_out = w_out[0].astype(jnp.bfloat16)
    low_moe = moe_gain[0].astype(jnp.bfloat16)
    low_router = router[0].astype(jnp.bfloat16)
    low_up = w_up[0].astype(jnp.bfloat16)
    low_down = w_down[0].astype(jnp.bfloat16)
    weights = (
        lax.all_gather(low_norm, "dp", axis=0, tiled=True),
        lax.all_gather(low_in, "dp", axis=2, tiled=True),
        lax.all_gather(low_conv, "dp", axis=1, tiled=True),
        lax.all_gather(low_conv_bias, "dp", axis=0, tiled=True),
        lax.all_gather(low_xproj, "dp", axis=0, tiled=True),
        lax.all_gather(low_dtproj, "dp", axis=1, tiled=True),
        lax.all_gather(low_dtbias, "dp", axis=0, tiled=True),
        lax.all_gather(low_alog, "dp", axis=1, tiled=True),
        lax.all_gather(low_skip, "dp", axis=0, tiled=True),
        lax.all_gather(low_out, "dp", axis=0, tiled=True),
        lax.all_gather(low_moe, "dp", axis=0, tiled=True),
        lax.all_gather(low_router, "dp", axis=0, tiled=True),
        lax.all_gather(low_up, "dp", axis=1, tiled=True),
        lax.all_gather(low_down, "dp", axis=1, tiled=True),
    )
    segment = lax.axis_index("section")
    segments = lax.axis_size("section")
    micro = tokens.shape[0]
    chosen_all = routes[0]
    placed_all = slots[0]
    dropped_all = drops[0]
    outputs_bank = jnp.zeros(tokens.shape, jnp.bfloat16)
    back_bank = jnp.zeros(tokens.shape, jnp.bfloat16)
    incoming = jnp.zeros(tokens.shape[1:], jnp.bfloat16)
    bank = None
    for step in range(micro + segments - 1):
        index = step - segment
        valid = (index >= 0) & (index < micro)
        which = jnp.clip(index, 0, micro - 1)
        fresh = tokens[min(step, micro - 1)]
        own_rows = jnp.where(segment == 0, fresh, incoming)
        chosen = lax.dynamic_index_in_dim(chosen_all, which, 0, keepdims=False)
        placed = lax.dynamic_index_in_dim(placed_all, which, 0, keepdims=False)
        dropped = lax.dynamic_index_in_dim(dropped_all, which, 0, keepdims=False)
        result, kept = segment_forward(own_rows, chosen, placed, dropped, weights)
        if bank is None:
            bank = jax.tree.map(lambda value: jnp.zeros((micro,) + value.shape, value.dtype), kept)
        bank = store(bank, which, valid, kept)
        outputs_bank = store(outputs_bank, which, valid, result)
        incoming = from_behind(result, "section", 1)
    incoming_grad = jnp.zeros(tokens.shape[1:], jnp.bfloat16)
    totals = None
    expert_pieces = []
    for step in range(micro + segments - 1):
        index = step - (segments - 1 - segment)
        valid = (index >= 0) & (index < micro)
        which = jnp.clip(index, 0, micro - 1)
        above = cotangent[min(step, micro - 1)]
        upstream = jnp.where(segment == segments - 1, above, incoming_grad).astype(jnp.float32)
        chosen = lax.dynamic_index_in_dim(chosen_all, which, 0, keepdims=False)
        placed = lax.dynamic_index_in_dim(placed_all, which, 0, keepdims=False)
        dropped = lax.dynamic_index_in_dim(dropped_all, which, 0, keepdims=False)
        kept = jax.tree.map(
            lambda held: lax.dynamic_index_in_dim(held, which, 0, keepdims=False), bank
        )
        d_own, grads, pieces = segment_backward(
            upstream, kept, chosen, placed, dropped, weights, valid
        )
        expert_pieces.append(pieces)
        grads = jax.tree.map(lambda value: jnp.where(valid, value, 0.0), grads)
        if totals is None:
            totals = grads
        else:
            totals = jax.tree.map(lambda held, fresh: held + fresh, totals, grads)
        back_bank = store(back_bank, which, valid, d_own)
        incoming_grad = from_behind(d_own, "section", -1)
    shares = share_grads(totals)
    hidden_rows = jnp.concatenate([piece[0] for piece in expert_pieces], 1)
    d_out_rows = jnp.concatenate([piece[1] for piece in expert_pieces], 1)
    in_rows = jnp.concatenate([piece[2] for piece in expert_pieces], 1)
    d_pre_rows = jnp.concatenate([piece[3] for piece in expert_pieces], 1)
    grad_up = jnp.einsum("erd,erf->edf", in_rows, d_pre_rows, preferred_element_type=jnp.float32)
    grad_down = jnp.einsum(
        "erf,erd->efd", hidden_rows, d_out_rows, preferred_element_type=jnp.float32
    )
    up_share, down_share = (
        lax.psum_scatter(
            grad_up.astype(jnp.bfloat16), "dp", scatter_dimension=1, tiled=True
        ).astype(jnp.float32),
        lax.psum_scatter(
            grad_down.astype(jnp.bfloat16), "dp", scatter_dimension=1, tiled=True
        ).astype(jnp.float32),
    )
    return (
        (outputs_bank[None], back_bank[None])
        + tuple((piece[None] for piece in shares))
        + (up_share[None], down_share[None])
    )


def solution(mesh):
    return jax.shard_map(
        shards,
        mesh=mesh,
        in_specs=(
            P(None, ("dp", "expert"), None),
            P(None, ("dp", "expert"), None),
            P("section", None, ("dp", "expert")),
            P("section", None, ("dp", "expert")),
            P("section", None, ("dp", "expert")),
            P("section", "dp"),
            P("section", None, None, ("dp", "expert")),
            P("section", None, ("dp", "expert")),
            P("section", ("dp", "expert")),
            P("section", ("dp", "expert"), None),
            P("section", None, ("dp", "expert")),
            P("section", ("dp", "expert")),
            P("section", None, ("dp", "expert")),
            P("section", ("dp", "expert")),
            P("section", ("dp", "expert"), None),
            P("section", "dp"),
            P("section", "dp", None),
            P("section", "expert", "dp", None),
            P("section", "expert", "dp", None),
        ),
        out_specs=(
            P("section", None, ("dp", "expert"), None),
            P("section", None, ("dp", "expert"), None),
            P("section", "dp"),
            P("section", None, None, ("dp", "expert")),
            P("section", None, ("dp", "expert")),
            P("section", ("dp", "expert")),
            P("section", ("dp", "expert"), None),
            P("section", None, ("dp", "expert")),
            P("section", ("dp", "expert")),
            P("section", None, ("dp", "expert")),
            P("section", ("dp", "expert")),
            P("section", ("dp", "expert"), None),
            P("section", "dp"),
            P("section", "dp", None),
            P("section", "expert", "dp", None),
            P("section", "expert", "dp", None),
        ),
        check_vma=False,
    )
```

profile of v0, /device:TPU:0, one launch (start us, length us, event | category | flops | bytes accessed | tf_op | source)
XLA Modules:
  0.0 6442.0 jit_solution(10212059581836235964)
XLA Ops:
  12.9 40.3 all-reduce.11
  53.4 33.9 all-gather.2
  251.3 109.9 %while.279 = (s32[]{:T(128)}, f32[16,1152]{1,0:T(8,128)S(1)}, f32[16,16,1152]{2,1,0:T(8,128)S(1)}, f32[16,16,1152]{2,1,0:T(8,128)}, f32[16,1152]{1,0:T(8,128)S(1...) while((s32[]{:T(128)}, f32[16,1152]{1,0:T(8,128)S(1)}, ...), condition=%wide.region_20.21_spmd.clone, body=%wide.region_3.20_spmd.clone.sunk | while | flops 2617362 | bytes 2615528 | solution.py:196
  458.3 67.7 %all-gather.16 = bf16[1,1152,8]{2,0,1:T(2,128)(2,1)S(1)} all-gather(bf16[1,144,8]{2,0,1:T(2,128)(2,1)S(1)} %copy.340), channel_id=18, replica_groups=mesh['section'=2,'dp'=8,'expert'=2] {'dp'}, dimensions={1}, use_global_device_ids=true | all-gather | bytes 20736 | tf_op jit(solution)/shard_map/all_gather | solution.py:545
  554.0 456.1 %all-gather.37.cloned.1.call-done = bf16[1,4,1152,3072]{3,2,1,0:T(8,128)(2,1)} async-done(((bf16[1,4,144,3072]{3,2,1,0:T(8,128)(2,1)}), bf16[1,4,1152,3072]{3,2,1,0:T(8,128)(2,1)}) %all-gather.37.cloned.1.call-update) | async-done | bytes 28311568 | tf_op jit(solution)/shard_map/all_gather | solution.py:546
  1027.9 523.1 %all-gather.39.cloned.1.call-done = bf16[1,4,3072,1152]{3,2,1,0:T(8,128)(2,1)} async-done(((bf16[1,4,384,1152]{3,2,1,0:T(8,128)(2,1)}), bf16[1,4,3072,1152]{3,2,1,0:T(8,128)(2,1)}) %all-gather.39.cloned.1.call-update) | async-done | bytes 28311568 | tf_op jit(solution)/shard_map/all_gather | solution.py:547
  1633.5 274.7 %while.281 = (s32[]{:T(128)}, f32[16,1152]{1,0:T(8,128)S(1)}, f32[16,16,1152]{2,1,0:T(8,128)}, f32[16,16,1152]{2,1,0:T(8,128)}, f32[16,1152]{1,0:T(8,128)S(1)}, ...) while((s32[]{:T(128)}, f32[16,1152]{1,0:T(8,128)S(1)}, ...), condition=%wide.region_50.51_spmd.clone, body=%wide.region_33.0_spmd.clone.sunk | while | flops 2617362 | bytes 2728276 | solution.py:196
  1915.8 33.7 all-gather.17
  1949.5 34.2 all-gather.18
  2151.5 154.8 %while.283 = (s32[]{:T(128)}, f32[16,1152]{1,0:T(8,128)S(1)}, f32[16,16,1152]{2,1,0:T(8,128)}, f32[16,16,1152]{2,1,0:T(8,128)}, f32[16,1152]{1,0:T(8,128)S(1)}, ...) while((s32[]{:T(128)}, f32[16,1152]{1,0:T(8,128)S(1)}, ...), condition=%wide.region_80.81_spmd.clone, body=%wide.region_63.80_spmd.clone.sunk | while | flops 2617362 | bytes 2616948 | solution.py:196
  2363.8 34.1 all-gather.20
  2708.1 150.0 %while.271 = (s32[]{:T(128)}, f32[16,1152]{1,0:T(8,128)S(1)}, f32[16,16,1152]{2,1,0:T(8,128)}, f32[16,16,1152]{2,1,0:T(8,128)}, f32[16,16,1152]{2,1,0:T(8,128)},...) while((s32[]{:T(128)}, f32[16,1152]{1,0:T(8,128)S(1)}, ...), condition=%wide.region_123.124_spmd, body=%wide.region_106.123_spmd.sunk | while | flops 2654225 | bytes 2624933 | solution.py:196
  2862.8 514.3 %while.272 = (s32[]{:T(128)}, f32[16,1152]{1,0:T(8,128)S(1)}, f32[16,16,1152]{2,1,0:T(8,128)}, f32[16,16,1152]{2,1,0:T(8,128)}, f32[16,16,16]{2,1,0:T(8,128)}, /...) while((s32[]{:T(128)}, f32[16,1152]{1,0:T(8,128)S(1)}, ...), condition=%wide.region_189.190_spmd, body=%wide.region_124.189_spmd.sunk | while | flops 8164882 | bytes 5807977 | solution.py:265
  3580.5 120.3 %while.274 = (s32[]{:T(128)}, f32[16,1152]{1,0:T(8,128)S(1)}, f32[16,16,1152]{2,1,0:T(8,128)}, f32[16,16,1152]{2,1,0:T(8,128)}, f32[16,16,1152]{2,1,0:T(8,128)},...) while((s32[]{:T(128)}, f32[16,1152]{1,0:T(8,128)S(1)}, ...), condition=%wide.region_224.225_spmd, body=%wide.region_207.224_spmd.sunk | while | flops 2654225 | bytes 2624933 | solution.py:196
  3705.5 486.6 %while.275 = (s32[]{:T(128)}, f32[16,1152]{1,0:T(8,128)S(1)}, f32[16,16,1152]{2,1,0:T(8,128)}, f32[16,16,1152]{2,1,0:T(8,128)}, f32[16,16,16]{2,1,0:T(8,128)}, /...) while((s32[]{:T(128)}, f32[16,1152]{1,0:T(8,128)S(1)}, ...), condition=%wide.region_290.291_spmd, body=%wide.region_225.290_spmd.sunk | while | flops 8164882 | bytes 5789517 | solution.py:265
  4382.1 121.9 %while.277 = (s32[]{:T(128)}, f32[16,1152]{1,0:T(8,128)S(1)}, f32[16,16,1152]{2,1,0:T(8,128)}, f32[16,16,1152]{2,1,0:T(8,128)}, f32[16,16,1152]{2,1,0:T(8,128)},...) while((s32[]{:T(128)}, f32[16,1152]{1,0:T(8,128)S(1)}, ...), condition=%wide.region_325.326_spmd, body=%wide.region_308.325_spmd.sunk | while | flops 2654225 | bytes 2624933 | solution.py:196
  4508.6 492.3 %while.278 = (s32[]{:T(128)}, f32[16,1152]{1,0:T(8,128)S(1)}, f32[16,16,1152]{2,1,0:T(8,128)}, f32[16,16,1152]{2,1,0:T(8,128)}, f32[16,16,16]{2,1,0:T(8,128)}, /...) while((s32[]{:T(128)}, f32[16,1152]{1,0:T(8,128)S(1)}, ...), condition=%wide.region_391.392_spmd, body=%wide.region_326.391_spmd.sunk | while | flops 8164882 | bytes 5789517 | solution.py:265
  5138.4 59.8 reduce-scatter.32.cloned.1.call-done
  5199.6 59.8 reduce-scatter.30.cloned.1.call-done
  5260.9 59.7 reduce-scatter.20.cloned.1.call-done
  5344.4 38.1 all-reduce.10
  5419.4 105.7 %reduce-scatter.18.cloned.1.call-done = bf16[1152,2,144]{0,2,1:T(8,128)(2,1)} async-done(((bf16[1152,2,1152]{0,2,1:T(8,128)(2,1)}), bf16[1152,2,144]{0,2,1:T(8,128)(2,1)}) %reduce-scatter.18.cloned.1.call-update) | async-done | bytes 663568 | tf_op jit(solution)/shard_map/reduce_scatter | solution.py:109
  5527.4 450.1 %reduce-scatter.24.cloned.1.call-done = bf16[4,144,3072]{2,1,0:T(8,128)(2,1)} async-done(((bf16[4,1152,3072]{2,1,0:T(8,128)(2,1)}), bf16[4,144,3072]{2,1,0:T(8,128)(2,1)}) %reduce-scatter.24.cloned.1.call-update) | async-done | bytes 3538960 | tf_op jit(solution)/shard_map/reduce_scatter | solution.py:610
  5983.4 445.9 %reduce-scatter.26.cloned.1.call-done = bf16[4,384,1152]{2,1,0:T(8,128)(2,1)} async-done(((bf16[4,3072,1152]{2,1,0:T(8,128)(2,1)}), bf16[4,384,1152]{2,1,0:T(8,128)(2,1)}) %reduce-scatter.26.cloned.1.call-update) | async-done | bytes 3538960 | tf_op jit(solution)/shard_map/reduce_scatter | solution.py:613
  (8371 shorter events, 3974.5 us)
Async XLA Ops:
  7.3 140.1 %all-gather.33.cloned.1.call-start = ((), (), s32[]{:S(2)}) async-start(), calls=%async_computation.35 | async-start | bytes 5971968 | tf_op jit(solution)/shard_map/all_gather | solution.py:535
  10.2 236.3 %all-reduce.22.cloned.1.call-start = ((), (), s32[]{:S(2)}) async-start(), calls=%async_computation.21 | async-start | bytes 212992 | tf_op jit(solution)/shard_map/psum | solution.py:73
  177.0 265.9 %all-gather.35.cloned.1.call-start = ((), (), s32[]{:S(2)}) async-start(), calls=%async_computation.36 | async-start | bytes 2985984 | tf_op jit(solution)/shard_map/all_gather | solution.py:543
  177.9 363.9 %all-reduce.24.cloned.1.call-start = ((), (), s32[]{:S(2)}) async-start(), calls=%async_computation.22 | async-start | bytes 2359296 | tf_op jit(solution)/shard_map/psum | solution.py:69
  446.7 563.4 %all-gather.37.cloned.1.call-start = ((), (), s32[]{:S(2)}) async-start(), calls=%async_computation.37 | async-start | bytes 31850496 | tf_op jit(solution)/shard_map/all_gather | solution.py:546
  452.1 1098.9 %all-gather.39.cloned.1.call-start = ((), (), s32[]{:S(2)}) async-start(), calls=%async_computation.38 | async-start | bytes 31850496 | tf_op jit(solution)/shard_map/all_gather | solution.py:547
  549.5 1076.9 %all-reduce.26.cloned.1.call-start = ((), (), s32[]{:S(2)}) async-start(), calls=%async_computation.23 | async-start | bytes 212992 | tf_op jit(solution)/shard_map/psum | solution.py:73
  1573.5 12.2 collective-permute-start.1
  1607.6 423.4 %all-reduce.28.cloned.1.call-start = ((), (), s32[]{:S(2)}) async-start(), calls=%async_computation.24 | async-start | bytes 2359296 | tf_op jit(solution)/shard_map/psum | solution.py:69
  2009.7 123.7 %all-reduce.30.cloned.1.call-start = ((), (), s32[]{:S(2)}) async-start(), calls=%async_computation.25 | async-start | bytes 212992 | tf_op jit(solution)/shard_map/psum | solution.py:73
  2100.1 11.6 collective-permute-start.4
  2114.4 424.8 %all-reduce.32.cloned.1.call-start = ((), (), s32[]{:S(2)}) async-start(), calls=%async_computation.26 | async-start | bytes 2359296 | tf_op jit(solution)/shard_map/psum | solution.py:69
  2424.0 1007.0 %all-reduce.34.cloned.1.call-start = ((), (), s32[]{:S(2)}) async-start(), calls=%async_computation.27 | async-start | bytes 2359296 | tf_op jit(solution)/shard_map/psum | solution.py:69
  3411.2 824.6 %all-reduce.36.cloned.1.call-start = ((), (), s32[]{:S(2)}) async-start(), calls=%async_computation.28 | async-start | bytes 2359296 | tf_op jit(solution)/shard_map/psum | solution.py:69
  4217.2 885.7 %reduce-scatter.28.cloned.1.call-start = ((), (), s32[]{:S(2)}) async-start(), calls=%async_computation.39 | async-start | bytes 331776
  5020.3 116.7 %reduce-scatter.34.cloned.1.call-start = ((), (), s32[]{:S(2)}) async-start(), calls=%async_computation.42 | async-start | bytes 331776
  5025.8 172.4 %reduce-scatter.32.cloned.1.call-start = ((), (), s32[]{:S(2)}) async-start(), calls=%async_computation.41 | async-start | bytes 331776
  5027.2 232.3 %reduce-scatter.30.cloned.1.call-start = ((), (), s32[]{:S(2)}) async-start(), calls=%async_computation.40 | async-start | bytes 331776
  5028.7 292.0 %reduce-scatter.20.cloned.1.call-start = ((), (), s32[]{:S(2)}) async-start(), calls=%async_computation.31 | async-start | bytes 331776 | tf_op jit(solution)/shard_map/reduce_scatter | solution.py:118
  5032.5 309.3 %all-reduce.38.cloned.1.call-start = ((), (), s32[]{:S(2)}) async-start(), calls=%async_computation.29 | async-start | bytes 2359296 | tf_op jit(solution)/shard_map/psum | solution.py:69
  5042.7 374.8 %reduce-scatter.22.cloned.1.call-start = ((), (), s32[]{:S(2)}) async-start(), calls=%async_computation.32 | async-start | bytes 2985984 | tf_op jit(solution)/shard_map/reduce_scatter | solution.py:133
  5050.1 475.0 %reduce-scatter.18.cloned.1.call-start = ((), (), s32[]{:S(2)}) async-start(), calls=%async_computation.30 | async-start | bytes 5971968 | tf_op jit(solution)/shard_map/reduce_scatter | solution.py:109
  5061.0 916.5 %reduce-scatter.24.cloned.1.call-start = ((), (), s32[]{:S(2)}) async-start(), calls=%async_computation.33 | async-start | bytes 31850496 | tf_op jit(solution)/shard_map/reduce_scatter | solution.py:610
  5078.2 1351.1 %reduce-scatter.26.cloned.1.call-start = ((), (), s32[]{:S(2)}) async-start(), calls=%async_computation.34 | async-start | bytes 31850496 | tf_op jit(solution)/shard_map/reduce_scatter | solution.py:613
  (806 other events, 15197.6 us)
Sparse Core Ops, SparseCore 0:
  10.8 102.7 all-gather.32
  177.1 18.9 all-reduce.21
  198.8 59.7 all-gather.34
  446.8 18.3 all-reduce.23
  466.7 543.3 all-gather.36
  1011.6 539.3 all-gather.38
  1607.7 18.5 all-reduce.25
  2009.8 21.1 all-reduce.27
  2114.5 18.8 all-reduce.29
  2424.1 21.1 all-reduce.31
  3411.3 19.6 all-reduce.33
  4217.4 18.4 all-reduce.35
  5020.4 55.2 reduce-scatter.27
  5079.2 57.6 reduce-scatter.33
  5140.4 57.6 reduce-scatter.31
  5201.7 57.6 reduce-scatter.29
  5262.9 57.6 reduce-scatter.19
  5323.0 18.7 all-reduce.37
  5346.0 71.5 reduce-scatter.21
  5422.1 102.9 reduce-scatter.17
  5529.6 447.8 reduce-scatter.23
  5981.4 447.8 reduce-scatter.25
where the time goes:
time: 6540 us; the launch traced here: 6440 us
  waiting for transfers between devices  2330 us (36%)
  local copies, waits for them, and re-layouts  1470 us (22%)
  other arithmetic  1370 us (21%)
  blocking collectives  760 us (12%)
  matrix products  427 us (7%)
    all_gather x1, waiting for transfers between devices, shards(): lax.all_gather(low_down, 'dp', axis=1, tiled=True)  523 us
    all_gather x1, waiting for transfers between devices, shards(): lax.all_gather(low_up, 'dp', axis=1, tiled=True)  456 us
    reduce_scatter x1, waiting for transfers between devices, shards(): lax.psum_scatter(grad_up.astype(jnp.bfloat16), 'dp', scatter_dimension=1,...  450 us
    reduce_scatter x1, waiting for transfers between devices, shards(): lax.psum_scatter(grad_down.astype(jnp.bfloat16), 'dp', scatter_dimension=...  446 us
    reduce_sum x480, other arithmetic, advance(): outputs.append(jnp.sum(state * out_blk[tick][:, None], 0))  213 us
    reduce_sum x192, other arithmetic, retreat(): d_step[tick] = jnp.sum(flow * rates, 0) + sig_blk[tick] * through_in  212 us
    all_gather x6, blocking collectives, entering(): everything = jax.tree.map(lambda part: lax.all_gather(part, axis), shard)  199 us
    all_gather x6, blocking collectives, prefix(): lax.all_gather(a.astype(kind), axis)  199 us

commit v1 on v0

v1 whole, which is shorter than its diff:
```python
import functools

import jax
import jax.numpy as jnp
from jax import lax
from jax.experimental import pallas as pl
from jax.experimental.pallas import tpu as pltpu
from jax.sharding import PartitionSpec as P

EXPERTS = 8
CAP = 12
LANES = 128
CHUNK = 8
HALO = 16
LOG2E = 1.4426950408889634
MESH = pl.DeviceIdType.MESH
MIB = 2**20

epsilon = 1e-05
highest = lax.Precision.HIGHEST
f32 = jnp.float32
bf16 = jnp.bfloat16


def tiles_of(width):
    return [slice(i * LANES, (i + 1) * LANES) for i in range(width // LANES)]


def lanes_at(block, width):
    return pl.ds(pl.multiple_of(block * width, LANES), width)


def scan_final(step_ref, drive_ref, bb_ref, a_ref, state, total, width):
    states = a_ref.shape[0]
    tiles = tiles_of(width)
    each = state.shape[2] // width

    def block(b, unused):
        lanes = lanes_at(b, width)
        rates = [a_ref[:, lanes][:, t] for t in tiles]

        def body(i, carry):
            base = pl.multiple_of(i * CHUNK, CHUNK)
            step = step_ref[pl.ds(base, CHUNK), lanes]
            drive = drive_ref[pl.ds(base, CHUNK), lanes]
            carry, sums = list(carry[0]), carry[1]
            for k in range(CHUNK):
                in_map = bb_ref[base + k]
                for j, t in enumerate(tiles):
                    decay = jnp.exp2(step[k : k + 1, t] * rates[j])
                    carry[j] = decay * carry[j] + drive[k : k + 1, t] * in_map
            return tuple(carry), sums + step

        zeros = tuple(jnp.zeros((states, LANES), f32) for _ in tiles)
        final, sums = lax.fori_loop(
            0, step_ref.shape[0] // CHUNK, body, (zeros, jnp.zeros((CHUNK, width), f32))
        )
        side, at = lax.div(b, each), lanes_at(lax.rem(b, each), width)
        state[side, :, at] = jnp.concatenate(final, 1)
        total[side, :, at] = jnp.sum(sums, 0, keepdims=True)
        return unused

    lax.fori_loop(0, 2 * each, block, 0)


def scan_leak(step_ref, dy_ref, cb_ref, a_ref, state, total, width):
    states = a_ref.shape[0]
    tiles = tiles_of(width)
    each = state.shape[2] // width
    count = step_ref.shape[0] // CHUNK

    def block(b, unused):
        lanes = lanes_at(b, width)
        rates = [a_ref[:, lanes][:, t] for t in tiles]

        def body(i, carry):
            base = pl.multiple_of((count - 1 - i) * CHUNK, CHUNK)
            step = step_ref[pl.ds(base, CHUNK), lanes]
            dys = dy_ref[pl.ds(base, CHUNK), lanes]
            carry, sums = list(carry[0]), carry[1]
            for k in reversed(range(CHUNK)):
                out_map = cb_ref[base + k]
                for j, t in enumerate(tiles):
                    decay = jnp.exp2(step[k : k + 1, t] * rates[j])
                    carry[j] = decay * (carry[j] + dys[k : k + 1, t] * out_map)
            return tuple(carry), sums + step

        zeros = tuple(jnp.zeros((states, LANES), f32) for _ in tiles)
        final, sums = lax.fori_loop(0, count, body, (zeros, jnp.zeros((CHUNK, width), f32)))
        side, at = lax.div(b, each), lanes_at(lax.rem(b, each), width)
        state[side, :, at] = jnp.concatenate(final, 1)
        total[side, :, at] = jnp.sum(sums, 0, keepdims=True)
        return unused

    lax.fori_loop(0, 2 * each, block, 0)


def scan_outputs(step_ref, drive_ref, bb_ref, cb_ref, a_ref, entering, y_ref, starts_ref, width):
    tiles = tiles_of(width)
    each = entering.shape[2] // width

    def block(b, unused):
        lanes = lanes_at(b, width)
        rates = [a_ref[:, lanes][:, t] for t in tiles]

        def body(i, carry):
            base = pl.multiple_of(i * CHUNK, CHUNK)
            step = step_ref[pl.ds(base, CHUNK), lanes]
            drive = drive_ref[pl.ds(base, CHUNK), lanes]
            carry = list(carry)
            starts_ref[i, :, lanes] = jnp.concatenate(carry, 1)
            rows = [[] for _ in tiles]
            for k in range(CHUNK):
                in_map = bb_ref[base + k]
                out_map = cb_ref[base + k]
                for j, t in enumerate(tiles):
                    decay = jnp.exp2(step[k : k + 1, t] * rates[j])
                    carry[j] = decay * carry[j] + drive[k : k + 1, t] * in_map
                    rows[j].append(jnp.sum(carry[j] * out_map, 0, keepdims=True))
            y_ref[pl.ds(base, CHUNK), lanes] = jnp.concatenate(
                [jnp.concatenate(row, 0) for row in rows], 1
            )
            return tuple(carry)

        first = entering[lax.div(b, each), :, lanes_at(lax.rem(b, each), width)]
        lax.fori_loop(0, step_ref.shape[0] // CHUNK, body, tuple(first[:, t] for t in tiles))
        return unused

    lax.fori_loop(0, 2 * each, block, 0)


def scan_back(
    step_ref, drive_ref, dy_ref, bb_ref, cb_ref, a_ref, starts_ref, inflow, through_ref, flow_ref, db_ref,
    dc_ref, da_ref, width,
):
    tiles = tiles_of(width)
    each = inflow.shape[2] // width
    count = step_ref.shape[0] // CHUNK
    db_ref[...] = jnp.zeros_like(db_ref)
    dc_ref[...] = jnp.zeros_like(dc_ref)

    def block(b, unused):
        lanes = lanes_at(b, width)
        rates = [a_ref[:, lanes][:, t] for t in tiles]

        def body(i, carry):
            grads, d_rates = list(carry[0]), list(carry[1])
            chunk = count - 1 - i
            base = pl.multiple_of(chunk * CHUNK, CHUNK)
            step = step_ref[pl.ds(base, CHUNK), lanes]
            drive = drive_ref[pl.ds(base, CHUNK), lanes]
            dys = dy_ref[pl.ds(base, CHUNK), lanes]
            start = starts_ref[chunk, :, lanes]
            d_in, d_out = [None] * CHUNK, [None] * CHUNK
            all_through, all_flows = [], []
            for j, t in enumerate(tiles):
                current = start[:, t]
                decays, states = [], [current]
                for k in range(CHUNK):
                    decay = jnp.exp2(step[k : k + 1, t] * rates[j])
                    current = decay * current + drive[k : k + 1, t] * bb_ref[base + k]
                    decays.append(decay)
                    states.append(current)
                grad = grads[j]
                through, flows = [None] * CHUNK, [None] * CHUNK
                for k in reversed(range(CHUNK)):
                    dy = dys[k : k + 1, t]
                    grad = grad + dy * cb_ref[base + k]
                    through[k] = jnp.sum(grad * bb_ref[base + k], 0, keepdims=True)
                    piece = grad * drive[k : k + 1, t]
                    d_in[k] = piece if d_in[k] is None else d_in[k] + piece
                    piece = dy * states[k + 1]
                    d_out[k] = piece if d_out[k] is None else d_out[k] + piece
                    grad = decays[k] * grad
                    flow = grad * states[k]
                    flows[k] = jnp.sum(flow * rates[j], 0, keepdims=True)
                    d_rates[j] = d_rates[j] + flow * step[k : k + 1, t]
                grads[j] = grad
                all_through.append(jnp.concatenate(through, 0))
                all_flows.append(jnp.concatenate(flows, 0))
            through_ref[pl.ds(base, CHUNK), lanes] = jnp.concatenate(all_through, 1)
            flow_ref[pl.ds(base, CHUNK), lanes] = jnp.concatenate(all_flows, 1)
            for k in range(CHUNK):
                db_ref[base + k] += d_in[k]
                dc_ref[base + k] += d_out[k]
            return tuple(grads), tuple(d_rates)

        first = inflow[lax.div(b, each), :, lanes_at(lax.rem(b, each), width)]
        zeros = tuple(jnp.zeros((a_ref.shape[0], LANES), f32) for _ in tiles)
        d_rates = lax.fori_loop(0, count, body, (tuple(first[:, t] for t in tiles), zeros))[1]
        da_ref[:, lanes] = jnp.concatenate(d_rates, 1)
        return unused

    lax.fori_loop(0, 2 * each, block, 0)


def block_width(width, most):
    while width % most:
        most -= LANES
    return most


def shape_of(*shape, dtype=f32):
    return jax.ShapeDtypeStruct(shape, dtype)


def place_of(index, count):
    return jnp.where(
        lax.rem(index, 2) == 0, lax.div(index, 2), count - 1 - lax.div(index, 2)
    )


def index_at(place, count):
    place = lax.rem(place + 2 * count, count)
    return jnp.where(place < (count + 1) // 2, 2 * place, 2 * (count - 1 - place) + 1)


def greet(devices):
    barrier = pltpu.get_barrier_semaphore()
    for device in devices:
        pl.semaphore_signal(barrier, inc=1, device_id=device, device_id_type=MESH)
    pl.semaphore_wait(barrier, len(devices))


def remote(src, dst, send, recv, device):
    return pltpu.make_async_remote_copy(
        src_ref=src, dst_ref=dst, send_sem=send, recv_sem=recv, device_id=device,
        device_id_type=MESH,
    )


def here(count):
    section, dp, core = (lax.axis_index(name) for name in ("section", "dp", "expert"))
    place = place_of(dp, count)
    right = (section, index_at(place + 1, count), core)
    left = (section, index_at(place - 1, count), core)
    return dp, core, place, right, left, (section, dp, 1 - core)


def dp_peers(count):
    section, dp, core = (lax.axis_index(name) for name in ("section", "dp", "expert"))
    return [(section, lax.rem(dp + by, count), core) for by in range(1, count)]


def comm_params(identity, vmem=48):
    return pltpu.CompilerParams(
        collective_id=identity, has_side_effects=True, vmem_limit_bytes=vmem * MIB
    )


anywhere = pl.BlockSpec(memory_space=pl.ANY)
in_vmem = pl.BlockSpec(memory_space=pltpu.VMEM)
dma = pltpu.SemaphoreType.DMA


def gelu_parts(x):
    scale, cubic = 0.7978845608028654, 0.044715
    square = x * x
    t = jnp.tanh(scale * x * (1.0 + cubic * square))
    act = 0.5 * x * (1.0 + t)
    slope = 0.5 * (1.0 + t) + 0.5 * x * (1.0 - t * t) * scale * (1.0 + 3.0 * cubic * square)
    return act, slope


def own_expert(rows, each_rows, hidden):
    each = each_rows // CAP
    row = lax.broadcasted_iota(jnp.int32, (rows, 1), 0)
    for _ in range(rows // each_rows - 1):
        row = jnp.where(row >= each_rows, row - each_rows, row)
    column = lax.broadcasted_iota(jnp.int32, (1, hidden), 1)
    row_expert, column_expert = jnp.zeros_like(row), jnp.zeros_like(column)
    for e in range(1, each):
        row_expert = row_expert + (row >= e * CAP).astype(jnp.int32)
        column_expert = column_expert + (column >= e * (hidden // each)).astype(jnp.int32)
    return row_expert == column_expert


def mm(a, b, dims):
    return lax.dot_general(a, b, (dims, ((), ())), preferred_element_type=f32)


class Round:
    def __init__(self, count, own, held, work, part, out, scratch):
        self.own, self.held, self.work, self.part, self.out = own, held, work, part, out
        self.slots, (self.total, self.pair_in, self.pair_sems) = scratch[:4], scratch[4:7]
        self.sems, self.back_sems, self.local_sem = scratch[7:9], scratch[9:11], scratch[11]
        self.count, self.reach = count, count // 2
        self.dp, self.core, self.place, right, left, self.partner = here(count)
        self.towards = (right, left)

    def source(self, way, k):
        return index_at(self.place - k if way == 0 else self.place + k, self.count)

    def hop(self, way, k, half, src=None):
        sem = self.sems[way]
        slot = self.held.at[self.source(way, k), self.core if half == 0 else 1 - self.core]
        return remote(
            slot if src is None else src, slot, sem.at[0, k, half], sem.at[1, k, half],
            self.towards[way],
        )

    def first(self, half):
        return self.own.at[self.core] if half == 0 else None

    def swap(self):
        return remote(
            self.own.at[1 - self.core], self.held.at[self.dp, self.core], self.pair_sems.at[0, 0],
            self.pair_sems.at[1, 0], self.partner,
        )

    def keep(self):
        return pltpu.make_async_copy(
            self.own.at[self.core], self.held.at[self.dp, self.core], self.local_sem
        )

    def begin(self):
        self.swap().start()
        self.keep().start()
        for way in range(2):
            if self.reach > 1 or way == 0:
                self.hop(way, 0, 0, self.first(0)).start()

    def begin_other(self):
        self.swap().wait_recv()
        for way in range(2):
            if self.reach > 1 or way == 1:
                self.hop(way, 0, 1).start()
        self.keep().wait()

    def further(self, k):
        for half in range(2):
            for way in range(2):
                self.hop(way, k - 1, half).wait_recv()
                if half == way:
                    self.hop(way, k, half).start()
                else:

                    @pl.when(k < self.reach - 1)
                    def _(way=way, half=half):
                        self.hop(way, k, half).start()

    def arrive(self):
        for way in range(2):
            self.hop(way, self.reach - 1, way).wait_recv()

    def back(self, way, k, half):
        sem = self.back_sems[way]
        return remote(
            self.slots[way].at[k, half], self.slots[way + 2].at[k, half], sem.at[0, k, half],
            sem.at[1, k, half], self.towards[way],
        )

    def begin_back(self):
        for way in range(2):
            self.slots[way + 2][0, 1 - way] = jnp.zeros(self.slots[0].shape[2:], bf16)
            self.slots[way][0, way] = self.part[self.source(way, self.reach), way]
            self.back(way, 0, way).start()

    def nearer(self, k):
        for half in range(2):
            for way in range(2):
                owner = self.source(1 - way, self.reach - k)
                piece = self.part[owner, half].astype(f32)
                if half == way:
                    self.back(way, k - 1, half).wait_recv()
                else:

                    @pl.when(k > 1)
                    def _(way=way, half=half):
                        self.back(way, k - 1, half).wait_recv()

                before = self.slots[way + 2][k - 1, half].astype(f32)
                self.slots[way][k, half] = (piece + before).astype(bf16)
                self.back(way, k, half).start()

    def swap_back(self):
        return remote(
            self.total.at[1 - self.core], self.pair_in, self.pair_sems.at[0, 1], self.pair_sems.at[1, 1],
            self.partner,
        )

    def sum_up(self):
        for half in range(2):
            value = self.part[self.dp, half].astype(f32)
            for way in range(2):
                if self.reach > 1 or half == way:
                    self.back(way, self.reach - 1, half).wait_recv()
                    value = value + self.slots[way + 2][self.reach - 1, half].astype(f32)
            self.total[half] = value.astype(bf16)
        self.swap_back().start()

    def end(self):
        self.out[self.core] = self.total[self.core]
        self.swap_back().wait_recv()
        self.out[1 - self.core] = self.pair_in[...]
        self.swap().wait_send()
        self.swap_back().wait_send()

    def finish(self, k):
        for half in range(2):
            for way in range(2):
                if half == way:
                    self.hop(way, k, half, self.first(half)).wait_send()
                    self.back(way, k, half).wait_send()
                else:

                    @pl.when(k < self.reach - 1)
                    def _(way=way, half=half):
                        self.hop(way, k, half, self.first(half)).wait_send()

                    @pl.when(k > 0)
                    def _(way=way, half=half):
                        self.back(way, k, half).wait_send()


def go_round(rounds):
    reach = rounds[0].reach

    def steps(from_step, step):
        def body(k, unused):
            step(k)
            return unused

        lax.fori_loop(from_step, reach, body, 0)

    for one in rounds:
        one.begin()
    for one in rounds:
        one.begin_other()
    for one in rounds:
        one.work([one.dp])

    def further(k):
        for one in rounds:
            one.further(k)
        for one in rounds:
            one.work([one.source(0, k), one.source(1, k)])

    steps(1, further)
    for one in rounds:
        one.arrive()
        one.work([one.source(0, reach)])
        one.begin_back()

    def nearer(k):
        for one in rounds:
            one.nearer(k)

    steps(1, nearer)
    for one in rounds:
        one.sum_up()
    for one in rounds:
        one.end()

    def finish(k):
        for one in rounds:
            one.finish(k)

    steps(0, finish)


def rows_of(held, sources):
    pieces = [held[s].reshape(-1, held.shape[-1]) for s in sources]
    return pieces[0] if len(pieces) == 1 else jnp.concatenate(pieces, 0)


def put_rows(ref, sources, value):
    size = value.shape[0] // len(sources)
    for i, s in enumerate(sources):
        ref[s] = value[i * size : (i + 1) * size].reshape(ref.shape[1:]).astype(ref.dtype)


def block_at(section, index, count):
    index = lax.rem(index + 2 * count, 2 * count)
    return section, lax.div(index, 2), lax.rem(index, 2)


def experts_kernel(count, ahead, behind, cross, *refs):
    refs = list(refs)

    def take(number):
        taken = refs[:number]
        del refs[:number]
        return taken

    if ahead:
        own, resid, table, gate = take(4)
    if behind:
        below = take(1)[0] if cross else None
        above, table_back, gate_back, arrived_hbm = take(4)
    up_hbm, down_hbm = take(2)
    if ahead:
        out, result = take(2)
        next_rows, next_halo = take(2) if cross else (None, None)
        (arrived_out,) = take(1)
    if behind:
        upstream_out, out_back, given_out, hidden_out, slope_out = take(5)
    up, down, load_sems = take(3)
    section = lax.axis_index("section")
    dp, core, place, right, left, partner = here(count)
    block = 2 * dp + core
    across, before, after = (block_at(1 - section, block + by, count) for by in (0, -1, 1))
    greet([right, left, partner] + [across] * cross + [before] * (cross and ahead))
    loads = [
        pltpu.make_async_copy(up_hbm, up, load_sems.at[0]),
        pltpu.make_async_copy(down_hbm, down, load_sems.at[1]),
    ]
    rounds = []
    if ahead:
        held, part = take(2)
        landed, landed_halo, cross_sems = take(3) if cross else (None, None, None)
        scratch = take(12)
        (save_sem,) = take(1)

        def work(sources):
            pre = mm(rows_of(held, sources), up[...], ((1,), (0,)))
            mask = own_expert(pre.shape[0], held.shape[2], pre.shape[1])
            hidden = jnp.where(mask, gelu_parts(pre)[0], 0.0).astype(bf16)
            put_rows(part, sources, mm(hidden, down[...], ((1,), (0,))))

        rounds.append(Round(count, own, held, work, part, out, scratch))
    if behind:
        own_back, held_back, arrived, hidden_all, slope_all, part_back = take(6)
        landed_back, cross_back = take(2) if cross else (None, None)
        scratch_back = take(12)
        (back_sems,) = take(1)
        loads.append(pltpu.make_async_copy(arrived_hbm, arrived, back_sems.at[0]))

        def work_back(sources):
            pre = mm(rows_of(arrived, sources), up[...], ((1,), (0,)))
            mask = own_expert(pre.shape[0], held_back.shape[2], pre.shape[1])
            act, slope = gelu_parts(pre)
            put_rows(hidden_all, sources, jnp.where(mask, act, 0.0))
            d_hidden = mm(rows_of(held_back, sources), down[...], ((1,), (1,)))
            d_pre = jnp.where(mask, d_hidden * slope, 0.0).astype(bf16)
            put_rows(slope_all, sources, d_pre)
            put_rows(part_back, sources, mm(d_pre, up[...], ((1,), (1,))))

        rounds.append(Round(count, own_back, held_back, work_back, part_back, out_back, scratch_back))
    if behind:
        if cross:
            crossing = remote(below, landed_back, cross_back.at[0], cross_back.at[1], across)
            crossing.start()
    for load in loads:
        load.start()
    if behind:
        upstream = above[...].astype(f32)
        if cross:
            crossing.wait_recv()
            upstream = jnp.where(section == 1, upstream, landed_back[...].astype(f32))
        upstream_out[...] = upstream.astype(bf16)
        slots_grad = mm(table_back[...], (upstream * gate_back[...]).astype(bf16), ((1,), (0,)))
        own_back[...] = slots_grad.astype(bf16).reshape(own_back.shape)
    waiting = list(loads)
    for one in rounds:

        def work_first(sources, work=one.work):
            while waiting:
                waiting.pop().wait()
            work(sources)

        one.work = work_first
    go_round(rounds)
    saves = []
    if ahead:
        saves.append(pltpu.make_async_copy(held, arrived_out, save_sem))
    if behind:
        for n, (src, dst) in enumerate(
            ((held_back, given_out), (hidden_all, hidden_out), (slope_all, slope_out))
        ):
            saves.append(pltpu.make_async_copy(src, dst, back_sems.at[1 + n]))
    for save in saves:
        save.start()
    if ahead:
        returned = out[...].reshape(-1, out.shape[2])
        combined = mm(table[...], returned, ((1,), (0,))) * gate[...]
        result[...] = (resid[...] + combined).astype(bf16)
    if ahead and cross:
        length, halo = result.shape[0], next_halo.shape[0]
        copies = [
            remote(result, landed, cross_sems.at[0, 0], cross_sems.at[1, 0], across),
            remote(
                result.at[length - halo : length], landed_halo, cross_sems.at[0, 1], cross_sems.at[1, 1], after
            ),
        ]
        for copy in copies:
            copy.start()
        for copy in copies:
            copy.wait_recv()
        next_rows[...] = landed[...]
        next_halo[...] = jnp.where(block > 0, landed_halo[...].astype(f32), 0.0).astype(bf16)
        for copy in copies:
            copy.wait_send()
    if behind and cross:
        crossing.wait_send()
    for save in saves:
        save.wait()


def experts(up, down, ahead, behind, cross):
    count = lax.axis_size("dp")
    reach = count // 2
    width = (ahead[1] if ahead else behind[-4]).shape[1]
    length = (ahead[1] if ahead else behind[-4]).shape[0]
    rows = (2, EXPERTS * CAP // 2, width)
    gathered = (count,) + rows
    units = (count, 2 * rows[1], up.shape[1])
    around = (
        [pltpu.VMEM((reach,) + rows, bf16)] * 4
        + [pltpu.VMEM(rows, bf16), pltpu.VMEM(rows[1:], bf16), dma((2, 2))]
        + [dma((2, reach, 2))] * 4
        + [dma(())]
    )
    in_specs, out_specs, shapes, scratch = [], [], [], []
    if ahead:
        landing = [(length, width), (HALO, width)] if cross else []
        in_specs += [in_vmem] * 4
        out_specs += [in_vmem] * (2 + len(landing)) + [anywhere]
        shapes += [rows, (length, width)] + landing + [gathered]
        scratch += [pltpu.VMEM(gathered, bf16)] * 2 + [pltpu.VMEM(shape, bf16) for shape in landing]
        scratch += [dma((2, 2))] * cross + around + [dma(())]
    if behind:
        in_specs += [in_vmem] * (len(behind) - 1) + [anywhere]
        out_specs += [in_vmem] * 2 + [anywhere] * 3
        shapes += [(length, width), rows, gathered, units, units]
        scratch += [pltpu.VMEM(rows, bf16)] + [pltpu.VMEM(gathered, bf16)] * 2
        scratch += [pltpu.VMEM(units, bf16)] * 2 + [pltpu.VMEM(gathered, bf16)]
        scratch += [pltpu.VMEM((length, width), bf16), dma((2,))] if cross else []
        scratch += around + [dma((4,))]
    number = 7 if ahead and behind else 1 if ahead else 2
    number += 0 if cross or number == 7 else 7
    return pl.pallas_call(
        functools.partial(experts_kernel, count, bool(ahead), bool(behind), cross),
        in_specs=in_specs + [anywhere] * 2,
        out_specs=out_specs,
        out_shape=[shape_of(*shape, dtype=bf16) for shape in shapes],
        scratch_shapes=[pltpu.VMEM(up.shape, bf16), pltpu.VMEM(down.shape, bf16), dma((2,))] + scratch,
        compiler_params=comm_params(number, 60),
        name="experts_both" if number == 7 else "experts_forward" if ahead else "experts_backward",
    )(*(ahead or ()), *(behind or ()), up, down)


def grid_here(count):
    section, dp, core = (lax.axis_index(name) for name in ("section", "dp", "expert"))
    a, b = lax.div(dp, 2), lax.rem(dp, 2)
    line = count // 2

    def at(place):
        return section, 2 * lax.rem(place + line, line) + b, core

    return a, b, core, at(a + 1), at(a - 1), (section, 2 * a + 1 - b, core), (section, dp, 1 - core)


def greet_lines(count):
    greet_all(count)


def weights_gather_kernel(count, parts, wide_up, wide_down, *refs):
    own, refs = refs[:parts], refs[parts:]
    (up_out, low_down), out, refs = refs[:2], refs[2 : parts + 2], refs[parts + 2 :]
    buffer_up, buffer_down, rounded_up, rounded_down, load_sems, up_sems = refs[:6]
    after_sems, before_sems, side_sems, pair_sems, local_sems = refs[6:]
    a, b, core, after, before, beside, partner = grid_here(count)
    line = count // 2
    greet_lines(count)

    def slot(p, place, which):
        return out[p].at[core, 2 * place + which]

    def source(p, place, k):
        return own[p] if isinstance(k, int) and k == 0 else slot(p, place, b)

    def along(way, k, p):
        place = a - k if way == 0 else a + k
        sems = after_sems if way == 0 else before_sems
        return remote(
            source(p, place, k), slot(p, place, b), sems.at[0, k, p], sems.at[1, k, p],
            after if way == 0 else before,
        )

    def aside(place, k, p):
        return remote(
            source(p, place, k), slot(p, place, b), side_sems.at[0, place, p], side_sems.at[1, place, p],
            beside,
        )

    def across(place, which, k, p):
        src = source(p, place, k) if which is b else slot(p, place, which)
        number = 2 * place + which
        return remote(
            src, slot(p, place, which), pair_sems.at[0, number, p], pair_sems.at[1, number, p], partner
        )

    def has(way, k):
        return a - k >= 0 if way == 0 else a + k < line

    def goes(way):
        return a + 1 < line if way == 0 else a >= 1

    for p in range(parts):
        aside(a, 0, p).start()
        for way in range(2):

            @pl.when(goes(way))
            def _(way=way, p=p):
                along(way, 0, p).start()

    keeps = [
        pltpu.make_async_copy(own[p], slot(p, a, b), local_sems.at[p]) for p in range(parts)
    ]
    for p in range(parts):
        across(a, b, 0, p).start()
        keeps[p].start()
    loads = [
        pltpu.make_async_copy(wide_up, buffer_up, load_sems.at[0]),
        pltpu.make_async_copy(wide_down, buffer_down, load_sems.at[1]),
    ]
    save = pltpu.make_async_copy(rounded_down, low_down, load_sems.at[2])
    for load in loads:
        load.start()
    loads[0].wait()
    each, depth, hidden = wide_up.shape
    cut = hidden // count
    for piece in range(count):
        for e in range(each):
            rounded_up[piece, :, e * cut : (e + 1) * cut] = buffer_up[
                e, :, piece * cut : (piece + 1) * cut
            ].astype(bf16)
    end = exchange(count, rounded_up, up_out, up_sems, load_sems.at[3])
    loads[1].wait()

    def rounding(e, unused):
        rounded_down[e] = buffer_down[e].astype(bf16)
        return unused

    lax.fori_loop(0, each, rounding, 0)
    save.start()

    def came_aside(place, p):
        aside(place, None, p).wait_recv()
        across(place, 1 - b, None, p).start()

    def arrivals(k, unused):
        for p in range(parts):
            for way in range(2):

                @pl.when(has(way, k))
                def _(way=way, p=p):
                    place = a - k if way == 0 else a + k
                    along(way, k - 1, p).wait_recv()

                    @pl.when(goes(way))
                    def _():
                        along(way, k, p).start()

                    aside(place, None, p).start()
                    across(place, b, None, p).start()

        for p in range(parts):

            @pl.when(k == 1)
            def _(p=p):
                came_aside(a, p)

            for way in range(2):

                @pl.when((k > 1) & has(way, k - 1))
                def _(way=way, p=p):
                    came_aside(a - k + 1 if way == 0 else a + k - 1, p)

        return unused

    lax.fori_loop(1, line, arrivals, 0)
    for p in range(parts):
        if line == 1:
            came_aside(a, p)
        for way in range(2):

            @pl.when((line > 1) & has(way, line - 1))
            def _(way=way, p=p):
                came_aside(a - line + 1 if way == 0 else a + line - 1, p)

    for p in range(parts):
        keeps[p].wait()

    def finish(place, unused):
        for p in range(parts):
            for which in range(2):
                copy = across(place, which, None, p)
                copy.wait_recv()
                copy.wait_send()
            aside(place, None, p).wait_send()
        return unused

    lax.fori_loop(0, line, finish, 0)

    def sent(k, unused):
        for p in range(parts):
            for way in range(2):

                @pl.when(has(way, k) & goes(way))
                def _(way=way, p=p):
                    along(way, k, p).wait_send()

        return unused

    lax.fori_loop(0, line, sent, 0)
    save.wait()
    end()


def weights_gather(up, down, own):
    count = lax.axis_size("dp")
    reach = count // 2
    parts = len(own)
    pieces = (count, up.shape[1], up.shape[0] * up.shape[2] // count)
    return pl.pallas_call(
        functools.partial(weights_gather_kernel, count, parts),
        in_specs=[anywhere] * (parts + 2),
        out_specs=[anywhere] * (parts + 2),
        out_shape=[shape_of(*pieces, dtype=bf16), shape_of(*down.shape, dtype=bf16)]
        + [shape_of(2, count, *part.shape, dtype=part.dtype) for part in own],
        scratch_shapes=[
            pltpu.VMEM(up.shape, f32),
            pltpu.VMEM(down.shape, f32),
            pltpu.VMEM(pieces, bf16),
            pltpu.VMEM(down.shape, bf16),
            dma((4,)),
            dma((2, count - 1)),
            dma((2, reach, parts)),
            dma((2, reach, parts)),
            dma((2, reach, parts)),
            dma((2, count, parts)),
            dma((parts,)),
        ],
        compiler_params=comm_params(3),
        name="weights_gather",
    )(up, down, *own)


def grads_reduce_kernel(count, parts, pieces, *refs):
    part, pieces_out, refs = refs[:parts], refs[parts], refs[parts + 1 :]
    out, refs = refs[:parts], refs[parts:]
    sides, refs = refs[:parts], refs[parts:]
    outs = (refs[:parts], refs[parts : 2 * parts])
    ins = (refs[2 * parts : 3 * parts], refs[3 * parts : 4 * parts])
    after_sems, before_sems, side_sems, piece_sems, local_sem = refs[4 * parts :]
    a, b, core, after, before, beside, partner = grid_here(count)
    line = count // 2
    greet(dp_peers(count))

    def aside(place, p):
        return remote(
            part[p].at[2 * place + 1 - b], sides[p].at[place], side_sems.at[0, place, p],
            side_sems.at[1, place, p], beside,
        )

    def along(way, place, p):
        sems = after_sems if way == 0 else before_sems
        return remote(
            outs[way][p].at[place], ins[way][p].at[place], sems.at[0, place, p], sems.at[1, place, p],
            after if way == 0 else before,
        )

    def far(way, k):
        return line - 1 - k if way == 0 else k

    def starts(k, unused):
        for p in range(parts):
            for way in range(2):

                @pl.when((way == 0) | (far(0, k) != far(1, k)))
                def _(way=way, p=p):
                    aside(far(way, k), p).start()

        return unused

    lax.fori_loop(0, (line + 1) // 2, starts, 0)
    end = exchange(count, pieces, pieces_out, piece_sems, local_sem)

    def both_lines(place, p):
        aside(place, p).wait_recv()
        return part[p][2 * place + b].astype(f32) + sides[p][place].astype(f32)

    def passing(k, unused):
        for p in range(parts):
            for way in range(2):
                place = far(way, k)

                @pl.when(place > a if way == 0 else place < a)
                def _(way=way, place=place, p=p):
                    value = both_lines(place, p)
                    outs[way][p][place] = value.astype(bf16)

                    @pl.when(a > 0 if way == 0 else a < line - 1)
                    def _():
                        along(way, place, p).wait_recv()
                        value = outs[way][p][place].astype(f32) + ins[way][p][place].astype(f32)
                        outs[way][p][place] = value.astype(bf16)

                    along(way, place, p).start()

        return unused

    lax.fori_loop(0, line - 1, passing, 0)
    for p in range(parts):
        out[p][...] = both_lines(a, p)
        for way in range(2):

            @pl.when(a > 0 if way == 0 else a < line - 1)
            def _(way=way, p=p):
                along(way, a, p).wait_recv()
                out[p][...] = out[p][...] + ins[way][p][a].astype(f32)

    def finish(place, unused):
        for p in range(parts):
            aside(place, p).wait_send()
            for way in range(2):

                @pl.when(place > a if way == 0 else place < a)
                def _(way=way, p=p):
                    along(way, place, p).wait_send()

        return unused

    lax.fori_loop(0, line, finish, 0)
    end()


def grads_reduce(pieces, parts):
    count = lax.axis_size("dp")
    reach = count // 2
    number = len(parts)
    slots = [pltpu.VMEM((reach,) + part.shape[1:], bf16) for part in parts]
    return pl.pallas_call(
        functools.partial(grads_reduce_kernel, count, number),
        in_specs=[anywhere] + [in_vmem] * number,
        out_specs=[anywhere] + [in_vmem] * number,
        out_shape=[shape_of(*pieces.shape, dtype=bf16)]
        + [shape_of(*part.shape[1:]) for part in parts],
        scratch_shapes=slots * 5
        + [dma((2, reach, number))] * 3
        + [dma((2, count - 1)), dma(())],
        compiler_params=comm_params(4, 60),
        name="grads_reduce",
    )(pieces, *parts)


def join(
    count, forward, state_ref, total_ref, rates, out_ref, other_state, other_total, mine, mine_total, states,
    totals, back, back_in, pair_sems, sems,
):
    section, dp, core = (lax.axis_index(name) for name in ("section", "dp", "expert"))
    partner = (section, dp, 1 - core)
    swap = [
        remote(state_ref.at[1 - core], other_state, pair_sems.at[0, 0], pair_sems.at[1, 0], partner),
        remote(total_ref.at[1 - core], other_total, pair_sems.at[0, 1], pair_sems.at[1, 1], partner),
    ]
    for copy in swap:
        copy.start()
    own_state, own_total = state_ref[core], total_ref[core]
    for copy in swap:
        copy.wait_recv()
    leads = core == (0 if forward else 1)
    first_state = jnp.where(leads, own_state, other_state[...])
    first_total = jnp.where(leads, own_total, other_total[...])
    second_state = jnp.where(leads, other_state[...], own_state)
    second_total = jnp.where(leads, other_total[...], own_total)
    mine[...] = (jnp.exp2(rates * second_total) * first_state + second_state).astype(bf16)
    mine_total[...] = first_total + second_total
    copies = []
    for d, peer in enumerate(dp_peers(count)):
        for n, (src, dst) in enumerate(((mine, states), (mine_total, totals))):
            copy = remote(src, dst.at[dp], sems.at[0, d, n], sems.at[1, d, n], peer)
            copy.start()
            copies.append(copy)
    states[dp] = mine[...]
    totals[dp] = mine_total[...]
    for copy in copies:
        copy.wait_recv()

    entering = jnp.zeros_like(own_state)
    for k in range(count):
        source = k if forward else count - 1 - k
        reached = (source < dp) if forward else (source > dp)
        fresh = jnp.exp2(rates * totals[source]) * entering + states[source].astype(f32)
        entering = jnp.where(reached, fresh, entering)
    after = jnp.exp2(rates * first_total) * entering + first_state
    back[...] = jnp.where(leads, after, entering)
    swap_back = remote(back, back_in, pair_sems.at[0, 2], pair_sems.at[1, 2], partner)
    swap_back.start()
    out_ref[core] = jnp.where(leads, entering, after)
    swap_back.wait_recv()
    out_ref[1 - core] = back_in[...]
    for copy in swap + copies + [swap_back]:
        copy.wait_send()


def join_scratch(count, states, half):
    one, sums = pltpu.VMEM((states, half), f32), pltpu.VMEM((1, half), f32)
    return [
        pltpu.VMEM((2, states, half), f32),
        pltpu.VMEM((2, 1, half), f32),
        pltpu.VMEM((2, states, half), f32),
        one,
        sums,
        pltpu.VMEM((states, half), bf16),
        sums,
        pltpu.VMEM((count, states, half), bf16),
        pltpu.VMEM((count, 1, half), f32),
        one,
        one,
        dma((2, 3)),
        dma((2, count - 1, 2)),
    ]


def own_lanes(a_ref, half):
    return a_ref[:, lanes_at(lax.axis_index("expert"), half)]


def greet_all(count):
    section, dp, core = (lax.axis_index(name) for name in ("section", "dp", "expert"))
    greet(dp_peers(count) + [(section, dp, 1 - core)])


def exchange(count, pieces_ref, out_ref, sems, local_sem):
    dp = lax.axis_index("dp")
    keep = pltpu.make_async_copy(pieces_ref.at[dp], out_ref.at[dp], local_sem)
    keep.start()
    copies = []
    for by, peer in enumerate(dp_peers(count)):
        copy = remote(pieces_ref.at[peer[1]], out_ref.at[dp], sems.at[0, by], sems.at[1, by], peer)
        copy.start()
        copies.append(copy)

    def end():
        keep.wait()
        for copy in copies:
            copy.wait()

    return end


def mixer_forward_kernel(
    count, step_ref, drive_ref, bb_ref, cb_ref, a_ref, y_ref, starts_ref, state, total, entering, *rest
):
    half = state.shape[2]
    width = block_width(half, 384)
    scan_final(step_ref, drive_ref, bb_ref, a_ref, state, total, width)
    greet_all(count)
    join(count, True, state, total, own_lanes(a_ref, half), entering, *rest)
    scan_outputs(step_ref, drive_ref, bb_ref, cb_ref, a_ref, entering, y_ref, starts_ref, width)


def mixer_forward(step, drive, in_map, out_map, rates):
    count = lax.axis_size("dp")
    (length, width), states = step.shape, rates.shape[0]
    return pl.pallas_call(
        functools.partial(mixer_forward_kernel, count),
        in_specs=[in_vmem] * 5,
        out_specs=[in_vmem] * 2,
        out_shape=[shape_of(length, width), shape_of(length // CHUNK, states, width)],
        scratch_shapes=join_scratch(count, states, width // 2),
        compiler_params=comm_params(5),
        name="mixer_forward",
    )(step, drive, in_map, out_map, rates)


def mixer_backward_kernel(
    count, step_ref, drive_ref, dy_ref, bb_ref, cb_ref, a_ref, starts_ref, through_ref, flow_ref, db_ref, dc_ref,
    da_ref, state, total, inflow, *rest,
):
    half = state.shape[2]
    width = block_width(half, 384)
    scan_leak(step_ref, dy_ref, cb_ref, a_ref, state, total, width)
    greet_all(count)
    join(count, False, state, total, own_lanes(a_ref, half), inflow, *rest)
    scan_back(
        step_ref, drive_ref, dy_ref, bb_ref, cb_ref, a_ref, starts_ref, inflow, through_ref, flow_ref, db_ref,
        dc_ref, da_ref, width,
    )


def mixer_backward(step, drive, dy, in_map, out_map, rates, starts):
    count = lax.axis_size("dp")
    (length, width), states = step.shape, rates.shape[0]
    wide, maps = shape_of(length, width), shape_of(*in_map.shape)
    return pl.pallas_call(
        functools.partial(mixer_backward_kernel, count),
        in_specs=[in_vmem] * 7,
        out_specs=[in_vmem] * 5,
        out_shape=[wide, wide, maps, maps, shape_of(states, width)],
        scratch_shapes=join_scratch(count, states, width // 2),
        compiler_params=comm_params(6),
        name="mixer_backward",
    )(step, drive, dy, in_map, out_map, rates, starts)


def dot(a, b, dims, dtype=f32):
    return lax.dot_general(a, b, (dims, ((), ())), preferred_element_type=f32).astype(dtype)


def nn(a, b, dtype=f32):
    return dot(a, b, ((1,), (0,)), dtype)


def nt(a, b, dtype=f32):
    return dot(a, b, ((1,), (1,)), dtype)


def tn(a, b, dtype=f32):
    return dot(a, b, ((0,), (0,)), dtype)


def normalize(values, gain):
    return values * lax.rsqrt(jnp.mean(values * values, axis=-1, keepdims=True) + epsilon) * gain


def sums(value):
    return jnp.sum(value, 0)


def normalize_back(values, gain, upstream):
    scale = lax.rsqrt(jnp.mean(values * values, axis=-1, keepdims=True) + epsilon)
    unit = values * scale
    inner = upstream * gain
    d_values = scale * (inner - unit * jnp.mean(inner * unit, axis=-1, keepdims=True))
    return d_values, sums(upstream * unit)


def from_behind(shard, axis, by):
    count = 1
    for name in (axis,) if isinstance(axis, str) else axis:
        count *= lax.axis_size(name)
    pairs = [(i, i + by) for i in range(count) if 0 <= i + by < count]
    return lax.ppermute(shard, axis, pairs)


def swap_pair(value):
    return lax.ppermute(value, "expert", [(0, 1), (1, 0)])


def spread(values):
    return jnp.broadcast_to(values[:, :, None], values.shape + (LANES,))


def routing(resid, moe_gain, router, chosen, placed, dropped):
    normed = normalize(resid, moe_gain)
    probs = jax.nn.softmax(jnp.dot(normed, router, precision=highest), axis=-1)
    keep = (1 - dropped).astype(f32)
    pick = (chosen[:, None] == jnp.arange(EXPERTS)[None]).astype(f32)
    gate = jnp.sum(probs * pick, -1) * keep
    flat = chosen * CAP + placed
    table = ((flat[:, None] == jnp.arange(EXPERTS * CAP)[None]) & (dropped[:, None] == 0)).astype(
        bf16
    )
    return normed, probs, pick, keep, gate, table


def by_core(buffer):
    return buffer.reshape(2, -1, buffer.shape[1])


def mixed(xz, weights):
    width = weights["w_out"].shape[0]
    taps = weights["conv_w"].shape[0]
    length = xz.shape[0] - HALO
    padded = xz[HALO - taps + 1 :, :width]
    summed = weights["conv_b"]
    for tap in range(taps):
        summed = summed + weights["conv_w"][tap : tap + 1] * padded[tap : tap + length]
    return padded, summed, xz[HALO:, width:]


def selective(projected, weights):
    rank = weights["dt_proj"].shape[0]
    states = weights["rates"].shape[0]
    dt_low = projected[:, :rank].astype(bf16)
    dt_raw = nn(dt_low, weights["dt_proj"]) + weights["dt_bias"]
    in_map = projected[:, rank : rank + states]
    out_map = projected[:, rank + states : rank + 2 * states]
    return dt_low, dt_raw, jax.nn.softplus(dt_raw), spread(in_map), spread(out_map)


def forward(rows, halo, chosen, placed, dropped, weights):
    inputs = jnp.concatenate([halo, rows], 0).astype(f32)
    normed = normalize(inputs, weights["norm_gain"]).astype(bf16)
    xz = nt(normed, weights["w_in"])
    padded, summed, gate_in = mixed(xz, weights)
    signal = jax.nn.silu(summed).astype(bf16)
    projected = nn(signal, weights["x_proj"])
    dt_low, dt_raw, step, in_map, out_map = selective(projected, weights)
    wide = signal.astype(f32)
    drive = step * wide
    rates = weights["rates"] * LOG2E
    scanned, starts = mixer_forward(step, drive, in_map, out_map, rates)
    gated = ((scanned + weights["skip"] * wide) * jax.nn.silu(gate_in)).astype(bf16)
    resid = rows.astype(f32) + nn(gated, weights["w_out"])
    normed_moe, probs, pick, keep, gate, table = routing(
        resid, weights["moe_gain"], weights["router"], chosen, placed, dropped
    )
    buffer = tn(table, normed_moe.astype(bf16), bf16)
    ahead = (by_core(buffer), resid, table, gate[:, None])
    kept = dict(
        rows=rows, halo=halo, xz=xz, projected=projected, scanned=scanned, starts=starts, resid=resid,
    )
    return ahead, kept


def backward_routing(kept, chosen, placed, dropped, weights):
    return routing(
        kept["resid"], weights["moe_gain"], weights["router"], chosen, placed, dropped
    )


def backward_experts(routed, returned, upstream, d_sent, weights):
    normed_moe, probs, pick, keep, gate, table = routed
    d_sent = d_sent.reshape(-1, d_sent.shape[2])
    returned = returned.reshape(d_sent.shape)
    upstream = upstream.astype(f32)
    d_gate = jnp.sum(upstream * nn(table, returned), -1)
    d_choice = d_gate[:, None] * pick * keep[:, None]
    d_logits = probs * (d_choice - jnp.sum(probs * d_choice, -1, keepdims=True))
    d_normed = nn(table, d_sent) + jnp.dot(d_logits, weights["router"].T, precision=highest)
    return upstream, d_normed, d_logits


def backward_mixer(upstream, kept, d_normed, d_logits, weights):
    resid = kept["resid"]
    normed_moe = normalize(resid, weights["moe_gain"])
    grad_router = lax.dot_general(
        normed_moe, d_logits, (((0,), (0,)), ((), ())), precision=highest
    )
    d_norm, grad_moe = normalize_back(resid, weights["moe_gain"], d_normed)
    d_resid = upstream + d_norm

    inputs = kept["rows"].astype(f32)
    normed = normalize(inputs, weights["norm_gain"]).astype(bf16)
    xz = kept["xz"]
    padded, summed, gate_in = mixed(xz, weights)
    signal_act, signal_back = jax.vjp(jax.nn.silu, summed)
    signal = signal_act.astype(bf16)
    wide = signal.astype(f32)
    dt_low, dt_raw, step, in_map, out_map = selective(kept["projected"], weights)
    drive = step * wide
    rates = weights["rates"] * LOG2E
    skip = weights["skip"]
    total_out = kept["scanned"] + skip * wide
    gate_act, gate_back = jax.vjp(jax.nn.silu, gate_in)
    gated = (total_out * gate_act).astype(bf16)
    d_mixer = d_resid.astype(bf16)
    d_gated = nt(d_mixer, weights["w_out"])
    d_total = d_gated * gate_act
    d_gate_in = gate_back(d_gated * total_out)[0]
    grad_skip = sums(d_total * wide)
    through, flow, d_in_map, d_out_map, d_rates = mixer_backward(
        step, drive, d_total, in_map, out_map, rates, kept["starts"]
    )
    d_step = flow / LOG2E + through * wide
    d_signal = step * through + d_total * skip
    d_raw = d_step * jax.nn.sigmoid(dt_raw)
    grad_dt_bias = sums(d_raw)
    d_raw_low = d_raw.astype(bf16)
    d_low = nt(d_raw_low, weights["dt_proj"])
    d_projected = jnp.concatenate(
        [d_low, jnp.sum(d_in_map, -1), jnp.sum(d_out_map, -1)], 1
    ).astype(bf16)
    d_signal = d_signal + nt(d_projected, weights["x_proj"])
    d_summed = signal_back(d_signal)[0]
    taps = weights["conv_w"].shape[0]
    length = d_summed.shape[0]
    ahead = from_behind(d_summed[:8], ("dp", "expert"), -1)
    extended = jnp.concatenate([d_summed, ahead], 0)
    d_conv_in = jnp.zeros_like(d_summed)
    for tap in range(taps):
        begin = taps - 1 - tap
        d_conv_in = d_conv_in + weights["conv_w"][tap : tap + 1] * extended[begin : begin + length]
    grad_conv = [
        sums(d_summed * padded[tap : tap + length]) for tap in range(taps)
    ]
    d_xz = jnp.concatenate([d_conv_in, d_gate_in], 1).astype(bf16)
    d_normed_in = nn(d_xz, weights["w_in"])
    d_inputs, grad_norm = normalize_back(inputs, weights["norm_gain"], d_normed_in)
    result = (d_resid + d_inputs).astype(bf16)
    half = signal.shape[1] // 2

    def sides(value):
        return value[:, :half], value[:, half:]

    lanes = (-(d_projected.shape[1] + dt_low.shape[1])) % LANES
    common = jnp.concatenate(
        [normed, d_mixer, d_projected, dt_low, jnp.zeros((length, lanes), bf16)], 1
    )
    width = signal.shape[1]
    cut = [sides(v) for v in (d_xz[:, :width], d_xz[:, width:], gated, signal, d_raw_low)]
    core = lax.axis_index("expert")
    own, theirs = (
        jnp.concatenate([jnp.where(core == side, a, b) for a, b in cut], 1) for side in (0, 1)
    )
    got_common, got = swap_pair(common), swap_pair(theirs)
    activations = (
        jnp.concatenate([common, got_common], 0), jnp.concatenate([own, got], 0),
    )
    vectors = (
        grad_conv + [sums(d_summed), grad_dt_bias, grad_skip], d_rates * weights["rates"],
        [grad_norm, grad_moe], grad_router,
    )
    return result, activations, vectors


def gather_weights(
    norm_gain, w_in, conv_w, conv_b, x_proj, dt_proj, dt_bias, a_log, skip, w_out, moe_gain, router,
    w_up, w_down,
):
    count = lax.axis_size("dp")
    share = x_proj.shape[1]
    model = w_out.shape[2]
    low_in = jnp.transpose(w_in[0].astype(bf16), (1, 2, 0))
    pieces = [
        x_proj[0], dt_proj[0].T, conv_w[0].T, conv_b[0][:, None], dt_bias[0][:, None],
        skip[0][:, None], a_log[0].T, norm_gain[0][:, None], moe_gain[0][:, None], router[0],
    ]
    sizes = [piece.shape[1] for piece in pieces]
    pad = (-sum(sizes)) % LANES
    small = jnp.concatenate(pieces + [jnp.zeros((share, pad), f32)], 1).astype(bf16)
    up, low_down, in_x, in_z, out, small = weights_gather(
        w_up[0], w_down[0], [low_in[0], low_in[1], w_out[0].astype(bf16), small]
    )
    width = 2 * count * share
    w_in_all = jnp.concatenate([in_x.reshape(width, model), in_z.reshape(width, model)], 0)
    table = small.reshape(width, -1)
    rows = table.astype(f32).T
    at = 0
    found = []
    for size in sizes:
        found.append(rows[at : at + size])
        at += size
    unused, dt_proj, conv_w, conv_b, dt_bias, a_skip, a_log, norm_gain, moe_gain, router = found
    weights = dict(
        w_in=w_in_all,
        w_out=out.reshape(width, model),
        x_proj=table[:, : sizes[0]],
        dt_proj=dt_proj.astype(bf16),
        conv_w=conv_w,
        conv_b=conv_b,
        dt_bias=dt_bias,
        skip=a_skip,
        rates=-jnp.exp(a_log),
        norm_gain=norm_gain[:, :model],
        moe_gain=moe_gain[:, :model],
        router=router[:, :model].T,
        w_up=up.reshape(-1, up.shape[2]),
        w_down=low_down.reshape(-1, model),
    )
    return weights, sizes


def mixer_grads(activations, vectors, sizes, up, count):
    common, own = activations
    channel, d_rates, feature, grad_router = vectors

    def added(pieces):
        return [piece[None] for piece in pieces]

    channel = jnp.concatenate(added(channel) + [d_rates], 0)
    feature = jnp.concatenate(added(feature) + [grad_router.T], 0)
    half = own.shape[1] // 5
    share = half // count
    model = feature.shape[1]
    core = lax.axis_index("expert")
    normed, d_mixer = common[:, :model], common[:, model : 2 * model]
    d_projected = common[:, 2 * model : 2 * model + sizes[0]]
    dt_low = common[:, 2 * model + sizes[0] : 2 * model + sizes[0] + sizes[1]]
    d_x, d_z, gated, signal, d_raw = (own[:, i * half : (i + 1) * half] for i in range(5))
    grad_x = tn(d_x, normed, bf16).reshape(count, share, model)
    grad_z = tn(d_z, normed, bf16).reshape(count, share, model)
    grad_out = tn(gated, d_mixer, bf16).reshape(count, share, model)
    grad_proj = tn(signal, d_projected)
    grad_dt = tn(d_raw, dt_low)
    sides = (channel[:, :half], channel[:, half:])

    def packed(which):
        return jnp.concatenate([which, feature], 0)

    own_vectors = packed(jnp.where(core == 0, sides[0], sides[1]))
    got = swap_pair(packed(jnp.where(core == 0, sides[1], sides[0])))
    total = (own_vectors + got).T
    pad = (-sum(sizes)) % LANES
    small = jnp.concatenate([grad_proj, grad_dt, total, jnp.zeros((half, pad), f32)], 1)
    small = small.astype(bf16).reshape(count, share, -1)
    up, grad_x, grad_z, grad_out, small = grads_reduce(up, [grad_x, grad_z, grad_out, small])
    at = 0
    found = []
    for size in sizes:
        found.append(small[:, at : at + size])
        at += size
    x_proj, dt_proj, conv_w, conv_b, dt_bias, skip, a_log, norm_gain, moe_gain, router = found
    return (
        norm_gain[:, 0],
        jnp.transpose(jnp.stack([grad_x, grad_z], 0), (2, 0, 1)),
        conv_w.T,
        conv_b[:, 0],
        x_proj,
        dt_proj.T,
        dt_bias[:, 0],
        a_log.T,
        skip[:, 0],
        grad_out,
        moe_gain[:, 0],
        router,
        up_grad(up),
    )


def rows_flat(value):
    return value.reshape(-1, value.shape[-1])


def down_grad(first, second):
    hidden, d_produced = (
        jnp.concatenate([rows_flat(a), rows_flat(b)], 0)
        for a, b in zip(first, second, strict=True)
    )
    return tn(hidden, d_produced).reshape(EXPERTS // 2, -1, d_produced.shape[1])


def up_pieces(first, second, count):
    arrived, d_pre = (
        jnp.concatenate([rows_flat(a), rows_flat(b)], 0)
        for a, b in zip(first, second, strict=True)
    )
    return tn(arrived, d_pre, bf16).reshape(count, arrived.shape[1] // count, -1)


def up_grad(up):
    each = EXPERTS // 2
    count = up.shape[0]
    cut = up.shape[2] // each
    return jnp.stack(
        [
            jnp.concatenate([up[k, :, e * cut : (e + 1) * cut] for k in range(count)], 1)
            for e in range(each)
        ],
        0,
    ).astype(f32)


def shards(
    tokens, cotangent, routes, slots, drops, norm_gain, w_in, conv_w, conv_b, x_proj, dt_proj, dt_bias,
    a_log, skip, w_out, moe_gain, router, w_up, w_down,
):
    count = lax.axis_size("dp")
    section = lax.axis_index("section")
    top = section == 1
    weights, sizes = gather_weights(
        norm_gain, w_in, conv_w, conv_b, x_proj, dt_proj, dt_bias, a_log, skip, w_out, moe_gain,
        router, w_up, w_down,
    )
    micro = tokens.shape[0]
    blocks = ("dp", "expert")
    steps = micro + 1

    def pick(which):
        return [lax.dynamic_index_in_dim(v[0], which, 0, False) for v in (routes, slots, drops)]

    halos = jnp.stack(
        [from_behind(tokens[m, -HALO:], blocks, 1) for m in range(micro)], 0
    )
    incoming, incoming_halo = jnp.zeros_like(tokens[0]), jnp.zeros_like(halos[0])
    results, bank, grads, found, last = [], [], [], [], []
    below = None

    def micro_of(step, first):
        return jnp.clip(step - first, 0, micro - 1)

    def back_parts(step):
        if step == 1:
            kept = jax.tree.map(lambda a, b: jnp.where(top, a, b), bank[2], bank[0])
        else:
            kept = bank[1]
        routed = backward_routing(kept, *pick(micro_of(step, 1 - section)), weights)
        above = cotangent[step] if step < micro else jnp.zeros_like(cotangent[0])
        above = jnp.where(top, above, jnp.zeros_like(above))
        crossing = () if below is None else (below,)
        return kept, routed, crossing + (above, routed[5].T, routed[4][:, None], kept["arrived"])

    for step in range(2 * steps - 1):
        ahead = behind = None
        if step < steps:
            fresh = min(step, micro - 1)
            rows = jnp.where(top, incoming, tokens[fresh])
            halo = jnp.where(top, incoming_halo, halos[fresh])
            ahead, fresh_kept = forward(rows, halo, *pick(micro_of(step, section)), weights)
        if step >= steps - 1:
            kept, routed, behind = back_parts(step - steps + 1)
        cross = (ahead is None) != (behind is None)
        if cross or count <= 8:
            done = experts(weights["w_up"], weights["w_down"], ahead, behind, cross)
        else:
            done = experts(weights["w_up"], weights["w_down"], ahead, None, False)
            done = [*done, *experts(weights["w_up"], weights["w_down"], None, behind, False)]
        if ahead is not None:
            fresh_kept["returned"], result = done[:2]
            if cross:
                incoming, incoming_halo = done[2:4]
            number = 5 if cross else 3
            fresh_kept["arrived"] = done[number - 1]
            results.append(result)
            bank.append(fresh_kept)
            done = done[number:]
        if behind is not None:
            upstream, d_sent, d_produced, hidden, d_pre = done
            last.append((hidden, d_produced, kept["arrived"], d_pre))
            upstream, d_normed, d_logits = backward_experts(
                routed, kept["returned"], upstream, d_sent, weights
            )
            if len(last) == steps:
                one = jax.tree.map(lambda a, b: jnp.where(top, a, b), last[0], last[2])
                moving = up_pieces(one[2:], last[1][2:], count)
            below, *pieces = backward_mixer(upstream, kept, d_normed, d_logits, weights)
            grads.append(below)
            found.append(pieces)
    outputs = jnp.stack(
        [jnp.where(top, results[m + 1], results[m]) for m in range(micro)], 0
    )
    backs = jnp.stack([jnp.where(top, grads[m], grads[m + 1]) for m in range(micro)], 0)

    def valid_one(place):
        return jax.tree.map(lambda a, b: jnp.where(top, a, b), found[0][place], found[2][place])

    activations = jax.tree.map(
        lambda a, b: jnp.concatenate([a, b], 0), valid_one(0), found[1][0]
    )
    vectors = jax.tree.map(lambda a, b: a + b, valid_one(1), found[1][1])
    mixer = mixer_grads(activations, vectors, sizes, moving, count)
    down = down_grad(one[:2], last[1][:2])
    return (outputs[None], backs[None]) + tuple(v[None] for v in mixer) + (down[None],)


def solution(mesh):
    both = ("dp", "expert")
    weights = (
        P("section", "dp"),
        P("section", None, None, both),
        P("section", None, both),
        P("section", both),
        P("section", both, None),
        P("section", None, both),
        P("section", both),
        P("section", None, both),
        P("section", both),
        P("section", both, None),
        P("section", "dp"),
        P("section", "dp", None),
        P("section", "expert", "dp", None),
        P("section", "expert", "dp", None),
    )
    return jax.shard_map(
        shards,
        mesh=mesh,
        in_specs=(P(None, both, None),) * 2 + (P("section", None, both),) * 3 + weights,
        out_specs=(P("section", None, both, None),) * 2 + weights,
        check_vma=False,
    )
```

time: 6540 us -> 1190 us (0.18); the launches traced: 6440 us -> 1170 us
  waiting for transfers between devices: 2330 us -> 0.58 us
  local copies, waits for them, and re-layouts: 1470 us -> 95.4 us
  other arithmetic: 1370 us -> 82.5 us
  Pallas kernels: 0 us -> 818 us
  blocking collectives: 760 us -> 0 us
  matrix products: 427 us -> 156 us
    reduce_scatter x5 -> x0, waiting for transfers between devices: 1090 us -> none  [the longest x1 450 us: shards(): lax.psum_scatter(grad_up.astype(jnp.bfloat16), 'dp', scatter_dimension=1,...]
    all_gather x4 -> x0, waiting for transfers between devices: 979 us -> none  [the longest x1 523 us: shards(): lax.all_gather(low_down, 'dp', axis=1, tiled=True)]
    pallas_call x0 -> x13, Pallas kernels: none -> 818 us  [the longest x5 327 us: experts(): pl.pallas_call(functools.partial(experts_kernel, count, bool(ahead), bool...]
    all_gather x29 -> x0, blocking collectives: 624 us -> none  [the longest x6 199 us: entering(): everything = jax.tree.map(lambda part: lax.all_gather(part, axis), shard)]
    reduce_sum x891 -> x23, other arithmetic: 619 us -> 27.4 us  [the longest x4 13.7 us: sums(): return jnp.sum(value, 0)]
    slice x307 -> x17, local copies, waits for them, and re-layouts: 536 us -> 12.3 us  [the longest x7 3.62 us: selective(): out_map = projected[:, rank + states:rank + 2 * states]]
    another operation x1885 -> x9, local copies, waits for them, and re-layouts: 381 us -> 1.83 us  [the longest x1632 81.4 us: advance(): return (state, (jnp.stack(outputs, 0), first))]
    mul x2409 -> x5, other arithmetic: 295 us -> 0.64 us  [the longest x4 0.61 us: routing(): gate = jnp.sum(probs * pick, -1) * keep]
where the time goes in v1:
time: 1190 us; the launch traced here: 1170 us
  Pallas kernels  818 us (69%)
  matrix products  156 us (13%)
  local copies, waits for them, and re-layouts  95.4 us (8%)
  other arithmetic  82.5 us (7%)
  starting transfers between devices  14.2 us (1%)
    pallas_call x5, Pallas kernels, experts(): pl.pallas_call(functools.partial(experts_kernel, count, bool(ahead), bool...  327 us
    pallas_call x1, Pallas kernels, grads_reduce(): pl.pallas_call(functools.partial(grads_reduce_kernel, count, number), in_...  156 us
    pallas_call x1, Pallas kernels, weights_gather(): pl.pallas_call(functools.partial(weights_gather_kernel, count, parts), in...  145 us
    dot_general x41, matrix products, dot(): lax.dot_general(a, b, (dims, ((), ())), preferred_element_type=f32)  145 us
    pallas_call x3, Pallas kernels, mixer_backward(): pl.pallas_call(functools.partial(mixer_backward_kernel, count), in_specs=...  115 us
    pallas_call x3, Pallas kernels, mixer_forward(): pl.pallas_call(functools.partial(mixer_forward_kernel, count), in_specs=[...  75.6 us
    unnamed x658, local copies, waits for them, and re-layouts  52.1 us
  transfers between devices with their start and end apart: 12, of which 1 were waited for; matrix products, arithmetic and copies ran while one was open for 12% of the time, Pallas kernels for 28%

profile of v1, /device:TPU:0, one launch (start us, length us, event | category | flops | bytes accessed | tf_op | source)
XLA Modules:
  0.0 1172.6 jit_solution(1969790633884106145)
XLA Ops:
  12.8 144.7 %weights_gather.1 = (bf16[8,144,1536]{2,1,0:T(8,128)(2,1)S(1)}, bf16[4,384,1152]{2,1,0:T(8,128)(2,1)}, bf16[2,8,144,1152]{3,2,1,0:T(8,128)(2,1)}, bf16[2,8,144,1...) custom-call(f32[4,144,3072]{2,1,0:T(8,128)} %bitcast.338, ...), custom_call_target="tpu_custom_call" | custom-call | tf_op jit(solution)/shard_map/weights_gather/pallas_call | solution.py:817
  169.4 6.6 fusion.163
  183.9 25.6 %mixer_forward.3 = (f32[128,2304]{1,0:T(8,128)S(1)}, f32[16,16,2304]{2,1,0:T(8,128)}) custom-call(f32[128,2304]{1,0:T(8,128)S(1)} %get-tuple-element.389.step_ref, f32[128,2304]{1,0:T(8,128)S(1)} %get-tuple-element.388.drive_ref, f32[128,16,128]{2,1,0:T(8,128)S(1)} %broadcast_in_dim.42.bb_ref, f32[128,16,128]{2,1,0:T(8,128)S(1)} %broadcast_in_dim.43.cb_ref, ...), custom_call_target="tpu_custom_call" | custom-call | tf_op jit(solution)/shard_map/mixer_forward/pallas_call | solution.py:1059
  216.4 58.7 %experts_forward.2 = (bf16[2,48,1152]{2,1,0:T(8,128)(2,1)}, bf16[128,1152]{1,0:T(8,128)(2,1)}, bf16[128,1152]{1,0:T(8,128)(2,1)}, bf16[16,1152]{1,0:T(8,128)(2,1)}, bf16[8,2,48,1152]{3,2,1,0:T(8,128)(2,1)}) custom-call(bf16[2,48,1152]{2,1,0:T(8,128)(2,1)} %bitcast.364, f32[128,1152]{1,0:T(8,128)} %copy-done.63, bf16[128,96]{1,0:T(8,128)(2,1)} %get-tuple-element.418.refs_2_, ...), custom_call_target="tpu_custom_call" | custom-call | tf_op jit(solution)/shard_map/experts_forward/pallas_call | solution.py:632
  276.6 6.7 fusion.161
  292.8 25.0 %mixer_forward.4 = (f32[128,2304]{1,0:T(8,128)S(1)}, f32[16,16,2304]{2,1,0:T(8,128)}) custom-call(f32[128,2304]{1,0:T(8,128)S(1)} %get-tuple-element.313.step_ref, f32[128,2304]{1,0:T(8,128)S(1)} %get-tuple-element.312.drive_ref, f32[128,16,128]{2,1,0:T(8,128)S(1)} %broadcast_in_dim.44.bb_ref, f32[128,16,128]{2,1,0:T(8,128)S(1)} %broadcast_in_dim.45.cb_ref, ...), custom_call_target="tpu_custom_call" | custom-call | tf_op jit(solution)/shard_map/mixer_forward/pallas_call | solution.py:1059
  327.5 60.1 %experts_forward.3 = (bf16[2,48,1152]{2,1,0:T(8,128)(2,1)}, bf16[128,1152]{1,0:T(8,128)(2,1)}, bf16[128,1152]{1,0:T(8,128)(2,1)}, bf16[16,1152]{1,0:T(8,128)(2,1)}, bf16[8,2,48,1152]{3,2,1,0:T(8,128)(2,1)}) custom-call(bf16[2,48,1152]{2,1,0:T(8,128)(2,1)} %bitcast.363, f32[128,1152]{1,0:T(8,128)} %copy-done.34, bf16[128,96]{1,0:T(8,128)(2,1)} %get-tuple-element.417.refs_2_, ...), custom_call_target="tpu_custom_call" | custom-call | tf_op jit(solution)/shard_map/experts_forward/pallas_call | solution.py:632
  389.3 9.4 broadcast_select_fusion.4
  408.3 25.0 %mixer_forward.5 = (f32[128,2304]{1,0:T(8,128)S(1)}, f32[16,16,2304]{2,1,0:T(8,128)}) custom-call(f32[128,2304]{1,0:T(8,128)S(1)} %copy-done.8, f32[128,2304]{1,0:T(8,128)S(1)} %copy-done.7, f32[128,16,128]{2,1,0:T(8,128)S(1)} %broadcast_in_dim.46.bb_ref, f32[128,16,128]{2,1,0:T(8,128)S(1)} %broadcast_in_dim.47.cb_ref, f32[16,2304]{1,0:T(8,128)S(1)} %fusion.214.a_ref), custom_call_target="tpu_custom_call" | custom-call | tf_op jit(solution)/shard_map/mixer_forward/pallas_call | solution.py:1059
  444.5 83.0 %experts_both.1 = (bf16[2,48,1152]{2,1,0:T(8,128)(2,1)}, bf16[128,1152]{1,0:T(8,128)(2,1)}, bf16[8,2,48,1152]{3,2,1,0:T(8,128)(2,1)}, bf16[128,1152]{1,0:T(8,128...) custom-call(bf16[2,48,1152]{2,1,0:T(8,128)(2,1)} %bitcast.362, ...), custom_call_target="tpu_custom_call" | custom-call | tf_op jit(solution)/shard_map/experts_both/pallas_call | solution.py:632
  535.1 6.0 fusion.371
  541.0 38.6 %mixer_backward.3 = (f32[128,2304]{1,0:T(8,128)S(1)}, f32[128,2304]{1,0:T(8,128)}, f32[128,16,128]{2,1,0:T(8,128)S(1)}, f32[128,16,128]{2,1,0:T(8,128)S(1)}, f32[16,2304]{1,0:T(8,128)S(1)}) custom-call(f32[128,2304]{1,0:T(8,128)} %copy-done.2, f32[128,2304]{1,0:T(8,128)} %copy-done.1, f32[128,2304]{1,0:T(8,128)} %get-tuple-element.273.dy_ref, ...), custom_call_target="tpu_custom_call" | custom-call | tf_op jit(solution)/shard_map/mixer_backward/pallas_call | solution.py:1089
  614.3 7.3 fusion.135
  622.7 62.9 %experts_backward.2 = (bf16[128,1152]{1,0:T(8,128)(2,1)}, bf16[2,48,1152]{2,1,0:T(8,128)(2,1)}, bf16[8,2,48,1152]{3,2,1,0:T(8,128)(2,1)}, bf16[8,96,1536]{2,1,0:T(8,128)(2,1)}, bf16[8,96,1536]{2,1,0:T(8,128)(2,1)}) custom-call(bf16[128,1152]{1,0:T(8,128)(2,1)} %fusion.128.refs_0_, bf16[128,1152]{1,0:T(8,128)(2,1)} %get-tuple-element.347.refs_1_, ...), custom_call_target="tpu_custom_call" | custom-call | tf_op jit(solution)/shard_map/experts_backward/pallas_call | solution.py:632
  690.3 9.1 fusion.52
  704.0 38.4 %mixer_backward.4 = (f32[128,2304]{1,0:T(8,128)S(1)}, f32[128,2304]{1,0:T(8,128)}, f32[128,16,128]{2,1,0:T(8,128)S(1)}, f32[128,16,128]{2,1,0:T(8,128)S(1)}, f32[16,2304]{1,0:T(8,128)S(1)}) custom-call(f32[128,2304]{1,0:T(8,128)} %get-tuple-element.311.step_ref, f32[128,2304]{1,0:T(8,128)} %get-tuple-element.310.drive_ref, ...), custom_call_target="tpu_custom_call" | custom-call | tf_op jit(solution)/shard_map/mixer_backward/pallas_call | solution.py:1089
  755.3 7.1 multiply_reduce_fusion
  775.3 7.2 fusion.122
  784.5 62.7 %experts_backward.3 = (bf16[128,1152]{1,0:T(8,128)(2,1)}, bf16[2,48,1152]{2,1,0:T(8,128)(2,1)}, bf16[8,2,48,1152]{3,2,1,0:T(8,128)(2,1)}, bf16[8,96,1536]{2,1,0:T(8,128)(2,1)}, bf16[8,96,1536]{2,1,0:T(8,128)(2,1)}) custom-call(bf16[128,1152]{1,0:T(8,128)(2,1)} %get-tuple-element.247.refs_0_, bf16[128,1152]{1,0:T(8,128)(2,1)} %broadcast.457.refs_1_, ...), custom_call_target="tpu_custom_call" | custom-call | tf_op jit(solution)/shard_map/experts_backward/pallas_call | solution.py:632
  852.7 6.6 fusion.59
  859.3 38.0 %mixer_backward.5 = (f32[128,2304]{1,0:T(8,128)S(1)}, f32[128,2304]{1,0:T(8,128)}, f32[128,16,128]{2,1,0:T(8,128)S(1)}, f32[128,16,128]{2,1,0:T(8,128)S(1)}, f32[16,2304]{1,0:T(8,128)S(1)}) custom-call(f32[128,2304]{1,0:T(8,128)} %copy-done.2, f32[128,2304]{1,0:T(8,128)} %copy-done.1, f32[128,2304]{1,0:T(8,128)} %get-tuple-element.235.dy_ref, ...), custom_call_target="tpu_custom_call" | custom-call | tf_op jit(solution)/shard_map/mixer_backward/pallas_call | solution.py:1089
  927.0 7.6 convolution_convert_fusion.3
  934.6 8.6 fusion.3
  991.4 155.7 %grads_reduce.1 = (bf16[8,144,1536]{2,1,0:T(8,128)(2,1)}, f32[144,1152]{1,0:T(8,128)}, f32[144,1152]{1,0:T(8,128)}, f32[144,1152]{1,0:T(8,128)}, f32[144,256]{1,0:T(8,128)}) custom-call(bf16[8,144,1536]{2,1,0:T(8,128)(2,1)} %bitcast.348, bf16[8,144,1152]{2,1,0:T(8,128)(2,1)} %bitcast.349, bf16[8,144,1152]{2,1,0:T(8,128)(2,1)} %bitcast.350, ...), custom_call_target="tpu_custom_call" | custom-call | tf_op jit(solution)/shard_map/grads_reduce/pallas_call | solution.py:935
  (913 shorter events, 267.1 us)
Async XLA Ops:
  2.1 166.4 %collective-permute-start = (bf16[16,1152]{1,0:T(8,128)(2,1)S(1)}, bf16[16,1152]{1,0:T(8,128)(2,1)}, u32[]{:S(2)}, u32[]{:S(2)}) collective-permute-start(bf16[16,1152]{1,0:T(8,128)(2,1)S(1)} %get-tuple-element.350), channel_id=1, source_target_pairs={{0,1},{1,2},{2,3},{3,4},{4,5},{5,6},{6,7},{7,8},{8,9},{9,10},{10,1... | collective-permute-start | bytes 110600 | tf_op jit(solution)/shard_map/ppermute | solution.py:1137
  5.0 270.8 %collective-permute-start.1 = (bf16[16,1152]{1,0:T(8,128)(2,1)}, bf16[16,1152]{1,0:T(8,128)(2,1)S(1)}, u32[]{:S(2)}, u32[]{:S(2)}) collective-permute-start(bf16[16,1152]{1,0:T(8,128)(2,1)} %get-tuple-element.349), channel_id=1, source_target_pairs={{0,1},{1,2},{2,3},{3,4},{4,5},{5,6},{6,7},{7,8},{8,9},{9,10},{10,1... | collective-permute-start | bytes 110600 | tf_op jit(solution)/shard_map/ppermute | solution.py:1137
  159.4 125.8 %copy-start.5 = (bf16[2,8,144,256]{3,2,1,0:T(8,128)(2,1)}, bf16[2,8,144,256]{3,2,1,0:T(8,128)(2,1)S(1)}, u32[]{:S(2)}) copy-start(bf16[2,8,144,256]{3,2,1,0:T(8,128)(2,1)S(1)} %get-tuple-element.76) | copy-start | bytes 3538948
  161.7 121.5 %copy-start.139 = (f32[2304]{0:T(1024)}, f32[2304]{0:T(1024)S(1)}, u32[]{:S(2)}) copy-start(f32[2304]{0:T(1024)S(1)} %get-tuple-element.202) | copy-start | bytes 27652
  161.7 121.5 %copy-start.141 = (f32[2304]{0:T(1024)}, f32[2304]{0:T(1024)S(1)}, u32[]{:S(2)}) copy-start(f32[2304]{0:T(1024)S(1)} %get-tuple-element.203) | copy-start | bytes 27652
  161.7 121.5 %copy-start.143 = (f32[2304]{0:T(1024)}, f32[2304]{0:T(1024)S(1)}, u32[]{:S(2)}) copy-start(f32[2304]{0:T(1024)S(1)} %get-tuple-element.204) | copy-start | bytes 27652
  161.7 121.5 %copy-start.145 = (f32[2304]{0:T(1024)}, f32[2304]{0:T(1024)S(1)}, u32[]{:S(2)}) copy-start(f32[2304]{0:T(1024)S(1)} %get-tuple-element.205) | copy-start | bytes 27652
  161.7 121.5 %copy-start.173 = (f32[2304]{0:T(1024)}, f32[2304]{0:T(1024)S(1)}, u32[]{:S(2)}) copy-start(f32[2304]{0:T(1024)S(1)} %get-tuple-element.206) | copy-start | bytes 27652
  323.8 209.6 %copy-start.202 = (f32[128]{0:T(128)}, f32[128]{0:T(128)S(1)}, u32[]{:S(2)}) copy-start(f32[128]{0:T(128)S(1)} %add_rsqrt_fusion.7) | copy-start | bytes 1540
  444.5 83.1 %copy-start.263 = (pred[128]{0:T(512)(128)(4,1)S(1)}, pred[128]{0:T(512)(128)(4,1)}, u32[]{:S(2)}) copy-start(pred[128]{0:T(512)(128)(4,1)} %copy-done.262) | copy-start | bytes 388
  444.5 83.1 %copy-start.265 = (s32[128]{0:T(128)S(1)}, s32[128]{0:T(128)}, u32[]{:S(2)}) copy-start(s32[128]{0:T(128)} %copy-done.264) | copy-start | bytes 1540
  444.5 83.1 %copy-start.317 = (bf16[2,48,1152]{2,1,0:T(8,128)(2,1)S(1)}, bf16[2,48,1152]{2,1,0:T(8,128)(2,1)}, u32[]{:S(2)}) copy-start(bf16[2,48,1152]{2,1,0:T(8,128)(2,1)} %get-tuple-element.95) | copy-start | bytes 663556
  444.5 84.5 %copy-start.230 = (s32[128]{0:T(128)S(1)}, s32[128]{0:T(128)}, u32[]{:S(2)}) copy-start(s32[128]{0:T(128)} %get-tuple-element.374) | copy-start | bytes 1540
  444.5 84.5 %copy-start.255 = (f32[128]{0:T(128)S(1)}, f32[128]{0:T(128)}, u32[]{:S(2)}) copy-start(f32[128]{0:T(128)} %get-tuple-element.385) | copy-start | bytes 1540
  593.5 17.1 %collective-permute-start.2 = (f32[8,2304]{1,0:T(8,128)}, f32[8,2304]{1,0:T(8,128)}, u32[]{:S(2)}, u32[]{:S(2)}) collective-permute-start(f32[8,2304]{1,0:T(8,128)} %slice.748), channel_id=1, source_target_pairs={{1,0},{2,1},{3,2},{4,3},{5,4},{6,5},{7,6},{8,7},{9,8},{10,9},{11,1... | collective-permute-start | bytes 221192 | tf_op jit(solution)/shard_map/ppermute | solution.py:1137
  764.1 8.6 collective-permute-start.3
  767.5 203.2 %collective-permute-start.8 = (bf16[128,2560]{1,0:T(8,128)(2,1)}, bf16[128,2560]{1,0:T(8,128)(2,1)}, u32[]{:S(2)}, u32[]{:S(2)}) collective-permute-start(bf16[128,2560]{1,0:T(8,128)(2,1)} %concatenate.176), channel_id=1, source_target_pairs={{0,1},{1,0},{2,3},{3,2},{4,5},{5,4},{6,7},{7,6},{8,9},{9,8},{10,11... | collective-permute-start | bytes 1966088 | tf_op jit(solution)/shard_map/ppermute | solution.py:1141
  913.6 33.5 %collective-permute-start.4 = (f32[8,2304]{1,0:T(8,128)}, f32[8,2304]{1,0:T(8,128)}, u32[]{:S(2)}, u32[]{:S(2)}) collective-permute-start(f32[8,2304]{1,0:T(8,128)} %slice.766), channel_id=1, source_target_pairs={{1,0},{2,1},{3,2},{4,3},{5,4},{6,5},{7,6},{8,7},{9,8},{10,9},{11,1... | collective-permute-start | bytes 221192 | tf_op jit(solution)/shard_map/ppermute | solution.py:1137
  914.8 56.0 %collective-permute-start.9 = (bf16[128,2560]{1,0:T(8,128)(2,1)}, bf16[128,2560]{1,0:T(8,128)(2,1)}, u32[]{:S(2)}, u32[]{:S(2)}) collective-permute-start(bf16[128,2560]{1,0:T(8,128)(2,1)} %concatenate.178), channel_id=1, source_target_pairs={{0,1},{1,0},{2,3},{3,2},{4,5},{5,4},{6,7},{7,6},{8,9},{9,8},{10,11... | collective-permute-start | bytes 1966088 | tf_op jit(solution)/shard_map/ppermute | solution.py:1141
  963.7 9.2 collective-permute-start.5
  965.8 7.1 collective-permute-start.6
  966.9 2.5 collective-permute-start.11
  969.4 3.3 collective-permute-start.10
  970.7 6.1 collective-permute-start.7
  (308 other events, 2270.0 us)

commit v2 on v1

--- a/solution.py
+++ b/solution.py
@@ -651,18 +651,25 @@
     return a, b, core, at(a + 1), at(a - 1), (section, 2 * a + 1 - b, core), (section, dp, 1 - core)
 
 
-def greet_lines(count):
-    greet_all(count)
-
-
-def weights_gather_kernel(count, parts, wide_up, wide_down, *refs):
+def weights_gather_kernel(count, parts, tokens, wide_up, wide_down, *refs):
     own, refs = refs[:parts], refs[parts:]
-    (up_out, low_down), out, refs = refs[:2], refs[2 : parts + 2], refs[parts + 2 :]
+    (halos, up_out, low_down), out, refs = refs[:3], refs[3 : parts + 3], refs[parts + 3 :]
     buffer_up, buffer_down, rounded_up, rounded_down, load_sems, up_sems = refs[:6]
-    after_sems, before_sems, side_sems, pair_sems, local_sems = refs[6:]
+    after_sems, before_sems, side_sems, pair_sems, local_sems, halo_sems = refs[6:]
     a, b, core, after, before, beside, partner = grid_here(count)
     line = count // 2
-    greet_lines(count)
+    section, block = lax.axis_index("section"), 2 * (2 * a + b) + core
+    greet(dp_peers(count) + [partner, block_at(section, block - 1, count)])
+    micro, length = tokens.shape[:2]
+    ends = [
+        remote(
+            tokens.at[m, length - HALO : length], halos.at[m], halo_sems.at[0, m], halo_sems.at[1, m],
+            block_at(section, block + 1, count),
+        )
+        for m in range(micro)
+    ]
+    for copy in ends:
+        copy.start()
 
     def slot(p, place, which):
         return out[p].at[core, 2 * place + which]
@@ -726,7 +733,9 @@
             rounded_up[piece, :, e * cut : (e + 1) * cut] = buffer_up[
                 e, :, piece * cut : (piece + 1) * cut
             ].astype(bf16)
-    end = exchange(count, rounded_up, up_out, up_sems, load_sems.at[3])
+    start, end = exchange(count, rounded_up, up_out, up_sems, load_sems.at[3])
+    start(0)
+    start(1)
     loads[1].wait()
 
     def rounding(e, unused):
@@ -807,18 +816,21 @@
     lax.fori_loop(0, line, sent, 0)
     save.wait()
     end()
-
-
-def weights_gather(up, down, own):
+    for copy in ends:
+        copy.wait()
+
+
+def weights_gather(tokens, up, down, own):
     count = lax.axis_size("dp")
     reach = count // 2
     parts = len(own)
     pieces = (count, up.shape[1], up.shape[0] * up.shape[2] // count)
     return pl.pallas_call(
         functools.partial(weights_gather_kernel, count, parts),
-        in_specs=[anywhere] * (parts + 2),
-        out_specs=[anywhere] * (parts + 2),
-        out_shape=[shape_of(*pieces, dtype=bf16), shape_of(*down.shape, dtype=bf16)]
+        in_specs=[anywhere] * (parts + 3),
+        out_specs=[anywhere] * (parts + 3),
+        out_shape=[shape_of(tokens.shape[0], HALO, tokens.shape[2], dtype=bf16)]
+        + [shape_of(*pieces, dtype=bf16), shape_of(*down.shape, dtype=bf16)]
         + [shape_of(2, count, *part.shape, dtype=part.dtype) for part in own],
         scratch_shapes=[
             pltpu.VMEM(up.shape, f32),
@@ -832,22 +844,73 @@
             dma((2, reach, parts)),
             dma((2, count, parts)),
             dma((parts,)),
+            dma((2, tokens.shape[0])),
         ],
         compiler_params=comm_params(3),
         name="weights_gather",
-    )(up, down, *own)
-
-
-def grads_reduce_kernel(count, parts, pieces, *refs):
-    part, pieces_out, refs = refs[:parts], refs[parts], refs[parts + 1 :]
-    out, refs = refs[:parts], refs[parts:]
-    sides, refs = refs[:parts], refs[parts:]
-    outs = (refs[:parts], refs[parts : 2 * parts])
-    ins = (refs[2 * parts : 3 * parts], refs[3 * parts : 4 * parts])
-    after_sems, before_sems, side_sems, piece_sems, local_sem = refs[4 * parts :]
+    )(tokens, up, down, *own)
+
+
+def grads_reduce_kernel(count, micro, vec, pieces, *refs):
+    refs = list(refs)
+
+    def take(number):
+        taken = refs[:number]
+        del refs[:number]
+        return taken
+
+    given = [take(8) for _ in range(micro)]
+    (up_out,), out = take(1), take(4)
+    wholes, halves, (vecs, landed) = take(4), take(5), take(2)
+    part, sides, ins = take(4), take(4), (take(4), take(4))
+    whole_sems, half_sems, vec_sems, after_sems, before_sems, side_sems, piece_sems, local_sem = refs
     a, b, core, after, before, beside, partner = grid_here(count)
     line = count // 2
-    greet(dp_peers(count))
+    parts = len(part)
+    half = halves[0].shape[1]
+    length = given[0][0].shape[0]
+    greet_all(count)
+
+    def lanes(side, begin):
+        return pl.ds(pl.multiple_of(begin + side * half, LANES), half)
+
+    def moves_of(i, n, which):
+        place, there = pl.ds(i * length, length), pl.ds((micro + i) * length, length)
+        if n < 4:
+            src, dst = given[i][n], wholes[n]
+            if which == 0:
+                return pltpu.make_async_copy(src, dst.at[place], whole_sems.at[2, i, n])
+            return remote(src, dst.at[there], whole_sems.at[0, i, n], whole_sems.at[1, i, n], partner)
+        n -= 4
+        src, begin = (given[i][4], n * 2 * half) if n < 2 else (given[i][3 + n], 0)
+        dst = halves[n]
+        if which == 0:
+            return pltpu.make_async_copy(
+                src.at[:, lanes(core, begin)], dst.at[place], half_sems.at[2, i, n]
+            )
+        return remote(
+            src.at[:, lanes(1 - core, begin)], dst.at[there], half_sems.at[0, i, n], half_sems.at[1, i, n],
+            partner,
+        )
+
+    order = (0, 4, 5, 1, 6, 2, 7, 3, 8)
+    for n in order:
+        for i in range(micro):
+            for which in range(2):
+                moves_of(i, n, which).start()
+    vec_copies = (
+        pltpu.make_async_copy(vec.at[core], vecs.at[0], vec_sems.at[2]),
+        remote(vec.at[1 - core], vecs.at[1], vec_sems.at[0], vec_sems.at[1], partner),
+    )
+    for copy in vec_copies:
+        copy.start()
+    start, end = exchange(count, pieces, landed, piece_sems, local_sem)
+    start(0)
+
+    def ready(n):
+        for i in range(micro):
+            moves_of(i, n, 0).wait()
+            moves_of(i, n, 1).wait_recv()
 
     def aside(place, p):
         return remote(
@@ -858,51 +921,78 @@
     def along(way, place, p):
         sems = after_sems if way == 0 else before_sems
         return remote(
-            outs[way][p].at[place], ins[way][p].at[place], sems.at[0, place, p], sems.at[1, place, p],
+            part[p].at[2 * place + b], ins[way][p].at[place], sems.at[0, place, p], sems.at[1, place, p],
             after if way == 0 else before,
         )
 
     def far(way, k):
         return line - 1 - k if way == 0 else k
 
-    def starts(k, unused):
-        for p in range(parts):
+    def put(p, value):
+        share = part[p].shape[1]
+        for index in range(count):
+            part[p][index] = value[index * share : (index + 1) * share].astype(bf16)
+
+        def starts(k, unused):
             for way in range(2):
 
                 @pl.when((way == 0) | (far(0, k) != far(1, k)))
-                def _(way=way, p=p):
+                def _(way=way):
                     aside(far(way, k), p).start()
 
-        return unused
-
-    lax.fori_loop(0, (line + 1) // 2, starts, 0)
-    end = exchange(count, pieces, pieces_out, piece_sems, local_sem)
+            return unused
+
+        lax.fori_loop(0, (line + 1) // 2, starts, 0)
 
     def both_lines(place, p):
         aside(place, p).wait_recv()
         return part[p][2 * place + b].astype(f32) + sides[p][place].astype(f32)
 
-    def passing(k, unused):
-        for p in range(parts):
-            for way in range(2):
-                place = far(way, k)
-
-                @pl.when(place > a if way == 0 else place < a)
-                def _(way=way, place=place, p=p):
-                    value = both_lines(place, p)
-                    outs[way][p][place] = value.astype(bf16)
-
-                    @pl.when(a > 0 if way == 0 else a < line - 1)
-                    def _():
-                        along(way, place, p).wait_recv()
-                        value = outs[way][p][place].astype(f32) + ins[way][p][place].astype(f32)
-                        outs[way][p][place] = value.astype(bf16)
-
-                    along(way, place, p).start()
-
-        return unused
-
-    lax.fori_loop(0, line - 1, passing, 0)
+    def passing(k, p):
+        for way in range(2):
+            place = far(way, k)
+
+            @pl.when(place > a if way == 0 else place < a)
+            def _(way=way, place=place):
+                index = 2 * place + b
+                part[p][index] = both_lines(place, p).astype(bf16)
+
+                @pl.when(a > 0 if way == 0 else a < line - 1)
+                def _():
+                    along(way, place, p).wait_recv()
+                    value = part[p][index].astype(f32) + ins[way][p][place].astype(f32)
+                    part[p][index] = value.astype(bf16)
+
+                along(way, place, p).start()
+
+    over = ((0,), (0,))
+    ready(0)
+    ready(4)
+    put(0, mm(halves[0][...], wholes[0][...], over))
+    ready(5)
+    put(1, mm(halves[1][...], wholes[0][...], over))
+    ready(1)
+    ready(6)
+    put(2, mm(halves[2][...], wholes[1][...], over))
+    start(1)
+    for n in (2, 7, 3, 8):
+        ready(n)
+    vec_copies[0].wait()
+    vec_copies[1].wait_recv()
+    put(
+        3,
+        mm(halves[3][...], wholes[2][...], over)
+        + mm(halves[4][...], wholes[3][...], over)
+        + vecs[0].astype(f32)
+        + vecs[1].astype(f32),
+    )
+    for p in range(parts):
+
+        def passing_on(k, unused, p=p):
+            passing(k, p)
+            return unused
+
+        lax.fori_loop(0, line - 1, passing_on, 0)
     for p in range(parts):
         out[p][...] = both_lines(a, p)
         for way in range(2):
@@ -924,26 +1014,48 @@
         return unused
 
     lax.fori_loop(0, line, finish, 0)
+    for n in order:
+        for i in range(micro):
+            moves_of(i, n, 1).wait_send()
+    vec_copies[1].wait_send()
     end()
-
-
-def grads_reduce(pieces, parts):
+    each, depth, hidden = up_out.shape
+    cut = hidden // count
+    for piece in range(count):
+        for e in range(each):
+            up_out[e, :, piece * cut : (piece + 1) * cut] = landed[
+                piece, :, e * cut : (e + 1) * cut
+            ]
+
+
+def grads_reduce(vec, pieces, given):
     count = lax.axis_size("dp")
-    reach = count // 2
-    number = len(parts)
-    slots = [pltpu.VMEM((reach,) + part.shape[1:], bf16) for part in parts]
+    line = count // 2
+    micro = len(given)
+    length, model = given[0][0].shape
+    half, lanes = vec.shape[1:]
+    share = half // count
+    each = EXPERTS // 2
+    rows = 2 * micro * length
+    shares = [(share, model)] * 3 + [(share, lanes)]
+    wholes = [model, model, lanes, lanes]
     return pl.pallas_call(
-        functools.partial(grads_reduce_kernel, count, number),
-        in_specs=[anywhere] + [in_vmem] * number,
-        out_specs=[anywhere] + [in_vmem] * number,
-        out_shape=[shape_of(*pieces.shape, dtype=bf16)]
-        + [shape_of(*part.shape[1:]) for part in parts],
-        scratch_shapes=slots * 5
-        + [dma((2, reach, number))] * 3
+        functools.partial(grads_reduce_kernel, count, micro),
+        in_specs=[anywhere] * (2 + 8 * micro),
+        out_specs=[in_vmem] * 5,
+        out_shape=[shape_of(each, pieces.shape[1], count * pieces.shape[2] // each, dtype=bf16)]
+        + [shape_of(*shape) for shape in shares],
+        scratch_shapes=[pltpu.VMEM((rows, width), bf16) for width in wholes]
+        + [pltpu.VMEM((rows, half), bf16)] * 5
+        + [pltpu.VMEM((2, half, lanes), bf16), pltpu.VMEM(pieces.shape, bf16)]
+        + [pltpu.VMEM((count,) + shape, bf16) for shape in shares]
+        + [pltpu.VMEM((line,) + shape, bf16) for shape in shares] * 3
+        + [dma((3, micro, 4)), dma((3, micro, 5)), dma((3,))]
+        + [dma((2, line, 4))] * 3
         + [dma((2, count - 1)), dma(())],
         compiler_params=comm_params(4, 60),
         name="grads_reduce",
-    )(pieces, *parts)
+    )(vec, pieces, *[value for one in given for value in one])
 
 
 def join(
@@ -1030,16 +1142,20 @@
     keep.start()
     copies = []
     for by, peer in enumerate(dp_peers(count)):
-        copy = remote(pieces_ref.at[peer[1]], out_ref.at[dp], sems.at[0, by], sems.at[1, by], peer)
-        copy.start()
-        copies.append(copy)
+        copies.append(
+            remote(pieces_ref.at[peer[1]], out_ref.at[dp], sems.at[0, by], sems.at[1, by], peer)
+        )
+
+    def start(beside):
+        for copy in copies[1 - beside :: 2]:
+            copy.start()
 
     def end():
         keep.wait()
         for copy in copies:
             copy.wait()
 
-    return end
+    return start, end
 
 
 def mixer_forward_kernel(
@@ -1283,34 +1399,27 @@
     d_normed_in = nn(d_xz, weights["w_in"])
     d_inputs, grad_norm = normalize_back(inputs, weights["norm_gain"], d_normed_in)
     result = (d_resid + d_inputs).astype(bf16)
-    half = signal.shape[1] // 2
-
-    def sides(value):
-        return value[:, :half], value[:, half:]
-
-    lanes = (-(d_projected.shape[1] + dt_low.shape[1])) % LANES
-    common = jnp.concatenate(
-        [normed, d_mixer, d_projected, dt_low, jnp.zeros((length, lanes), bf16)], 1
-    )
-    width = signal.shape[1]
-    cut = [sides(v) for v in (d_xz[:, :width], d_xz[:, width:], gated, signal, d_raw_low)]
-    core = lax.axis_index("expert")
-    own, theirs = (
-        jnp.concatenate([jnp.where(core == side, a, b) for a, b in cut], 1) for side in (0, 1)
-    )
-    got_common, got = swap_pair(common), swap_pair(theirs)
-    activations = (
-        jnp.concatenate([common, got_common], 0), jnp.concatenate([own, got], 0),
+    low, rank = d_projected.shape[1], dt_low.shape[1]
+    lanes = (-sum(weights["sizes"])) % LANES + sum(weights["sizes"])
+    given = (
+        normed,
+        d_mixer,
+        jnp.pad(d_projected, ((0, 0), (0, lanes - low))),
+        jnp.pad(dt_low, ((0, 0), (low, lanes - low - rank))),
+        d_xz,
+        gated,
+        signal,
+        d_raw_low,
     )
     vectors = (
         grad_conv + [sums(d_summed), grad_dt_bias, grad_skip], d_rates * weights["rates"],
         [grad_norm, grad_moe], grad_router,
     )
-    return result, activations, vectors
+    return result, given, vectors
 
 
 def gather_weights(
-    norm_gain, w_in, conv_w, conv_b, x_proj, dt_proj, dt_bias, a_log, skip, w_out, moe_gain, router,
+    tokens, norm_gain, w_in, conv_w, conv_b, x_proj, dt_proj, dt_bias, a_log, skip, w_out, moe_gain, router,
     w_up, w_down,
 ):
     count = lax.axis_size("dp")
@@ -1324,8 +1433,8 @@
     sizes = [piece.shape[1] for piece in pieces]
     pad = (-sum(sizes)) % LANES
     small = jnp.concatenate(pieces + [jnp.zeros((share, pad), f32)], 1).astype(bf16)
-    up, low_down, in_x, in_z, out, small = weights_gather(
-        w_up[0], w_down[0], [low_in[0], low_in[1], w_out[0].astype(bf16), small]
+    halos, up, low_down, in_x, in_z, out, small = weights_gather(
+        tokens, w_up[0], w_down[0], [low_in[0], low_in[1], w_out[0].astype(bf16), small]
     )
     width = 2 * count * share
     w_in_all = jnp.concatenate([in_x.reshape(width, model), in_z.reshape(width, model)], 0)
@@ -1338,6 +1447,7 @@
         at += size
     unused, dt_proj, conv_w, conv_b, dt_bias, a_skip, a_log, norm_gain, moe_gain, router = found
     weights = dict(
+        sizes=sizes,
         w_in=w_in_all,
         w_out=out.reshape(width, model),
         x_proj=table[:, : sizes[0]],
@@ -1353,43 +1463,20 @@
         w_up=up.reshape(-1, up.shape[2]),
         w_down=low_down.reshape(-1, model),
     )
-    return weights, sizes
-
-
-def mixer_grads(activations, vectors, sizes, up, count):
-    common, own = activations
+    return weights, sizes, halos
+
+
+def mixer_grads(given, vectors, sizes, up, count):
     channel, d_rates, feature, grad_router = vectors
-
-    def added(pieces):
-        return [piece[None] for piece in pieces]
-
-    channel = jnp.concatenate(added(channel) + [d_rates], 0)
-    feature = jnp.concatenate(added(feature) + [grad_router.T], 0)
-    half = own.shape[1] // 5
-    share = half // count
-    model = feature.shape[1]
-    core = lax.axis_index("expert")
-    normed, d_mixer = common[:, :model], common[:, model : 2 * model]
-    d_projected = common[:, 2 * model : 2 * model + sizes[0]]
-    dt_low = common[:, 2 * model + sizes[0] : 2 * model + sizes[0] + sizes[1]]
-    d_x, d_z, gated, signal, d_raw = (own[:, i * half : (i + 1) * half] for i in range(5))
-    grad_x = tn(d_x, normed, bf16).reshape(count, share, model)
-    grad_z = tn(d_z, normed, bf16).reshape(count, share, model)
-    grad_out = tn(gated, d_mixer, bf16).reshape(count, share, model)
-    grad_proj = tn(signal, d_projected)
-    grad_dt = tn(d_raw, dt_low)
-    sides = (channel[:, :half], channel[:, half:])
-
-    def packed(which):
-        return jnp.concatenate([which, feature], 0)
-
-    own_vectors = packed(jnp.where(core == 0, sides[0], sides[1]))
-    got = swap_pair(packed(jnp.where(core == 0, sides[1], sides[0])))
-    total = (own_vectors + got).T
-    pad = (-sum(sizes)) % LANES
-    small = jnp.concatenate([grad_proj, grad_dt, total, jnp.zeros((half, pad), f32)], 1)
-    small = small.astype(bf16).reshape(count, share, -1)
-    up, grad_x, grad_z, grad_out, small = grads_reduce(up, [grad_x, grad_z, grad_out, small])
+    feature = jnp.concatenate([piece[None] for piece in feature] + [grad_router.T], 0)
+    rows = jnp.concatenate(
+        [piece[None] for piece in channel] + [d_rates, jnp.concatenate([feature, feature], 1)], 0
+    )
+    begin = sizes[0] + sizes[1]
+    lanes = -(-sum(sizes) // LANES) * LANES
+    vec = jnp.pad(rows.T.astype(bf16), ((0, 0), (begin, lanes - begin - rows.shape[0])))
+    vec = vec.reshape(2, -1, lanes)
+    up, grad_x, grad_z, grad_out, small = grads_reduce(vec, up, given)
     at = 0
     found = []
     for size in sizes:
@@ -1409,7 +1496,7 @@
         grad_out,
         moe_gain[:, 0],
         router,
-        up_grad(up),
+        up.astype(f32),
     )
 
 
@@ -1431,19 +1518,6 @@
         for a, b in zip(first, second, strict=True)
     )
     return tn(arrived, d_pre, bf16).reshape(count, arrived.shape[1] // count, -1)
-
-
-def up_grad(up):
-    each = EXPERTS // 2
-    count = up.shape[0]
-    cut = up.shape[2] // each
-    return jnp.stack(
-        [
-            jnp.concatenate([up[k, :, e * cut : (e + 1) * cut] for k in range(count)], 1)
-            for e in range(each)
-        ],
-        0,
-    ).astype(f32)
 
 
 def shards(
@@ -1453,8 +1527,8 @@
     count = lax.axis_size("dp")
     section = lax.axis_index("section")
     top = section == 1
-    weights, sizes = gather_weights(
-        norm_gain, w_in, conv_w, conv_b, x_proj, dt_proj, dt_bias, a_log, skip, w_out, moe_gain,
+    weights, sizes, halos = gather_weights(
+        tokens, norm_gain, w_in, conv_w, conv_b, x_proj, dt_proj, dt_bias, a_log, skip, w_out, moe_gain,
         router, w_up, w_down,
     )
     micro = tokens.shape[0]
@@ -1464,9 +1538,8 @@
     def pick(which):
         return [lax.dynamic_index_in_dim(v[0], which, 0, False) for v in (routes, slots, drops)]
 
-    halos = jnp.stack(
-        [from_behind(tokens[m, -HALO:], blocks, 1) for m in range(micro)], 0
-    )
+    begins = (lax.axis_index("dp") == 0) & (lax.axis_index("expert") == 0)
+    halos = jnp.where(begins, jnp.zeros_like(halos), halos)
     incoming, incoming_halo = jnp.zeros_like(tokens[0]), jnp.zeros_like(halos[0])
     results, bank, grads, found, last = [], [], [], [], []
     below = None
@@ -1529,11 +1602,8 @@
     def valid_one(place):
         return jax.tree.map(lambda a, b: jnp.where(top, a, b), found[0][place], found[2][place])
 
-    activations = jax.tree.map(
-        lambda a, b: jnp.concatenate([a, b], 0), valid_one(0), found[1][0]
-    )
     vectors = jax.tree.map(lambda a, b: a + b, valid_one(1), found[1][1])
-    mixer = mixer_grads(activations, vectors, sizes, moving, count)
+    mixer = mixer_grads([valid_one(0), found[1][0]], vectors, sizes, moving, count)
     down = down_grad(one[:2], last[1][:2])
     return (outputs[None], backs[None]) + tuple(v[None] for v in mixer) + (down[None],)
 

time: 1190 us -> 1130 us (0.950)
  local copies, waits for them, and re-layouts: 95.4 us -> 70.7 us
  matrix products: 156 us -> 139 us
    unnamed x658 -> x572, local copies, waits for them, and re-layouts: 52.1 us -> 33.4 us
    dot_general x41 -> x36, matrix products: 145 us -> 128 us  [dot(): lax.dot_general(a, b, (dims, ((), ())), preferred_element_type=f32)]
  transfers between devices with their start and end apart: 12 -> 3, of which waited for: 1 -> 0; matrix products, arithmetic and copies ran while one was open for 12% -> 4% of each run, Pallas kernels for 28% -> 0%
where the time goes in v2:
time: 1130 us; the launch traced here: 1120 us
  Pallas kernels  827 us (73%)
  matrix products  139 us (12%)
  other arithmetic  75.8 us (7%)
  local copies, waits for them, and re-layouts  70.7 us (6%)
    pallas_call x5, Pallas kernels, experts(): pl.pallas_call(functools.partial(experts_kernel, count, bool(ahead), bool...  330 us
    pallas_call x1, Pallas kernels, grads_reduce(): pl.pallas_call(functools.partial(grads_reduce_kernel, count, micro), in_s...  156 us
    pallas_call x1, Pallas kernels, weights_gather(): pl.pallas_call(functools.partial(weights_gather_kernel, count, parts), in...  150 us
    dot_general x36, matrix products, dot(): lax.dot_general(a, b, (dims, ((), ())), preferred_element_type=f32)  128 us
    pallas_call x3, Pallas kernels, mixer_backward(): pl.pallas_call(functools.partial(mixer_backward_kernel, count), in_specs=...  115 us
    pallas_call x3, Pallas kernels, mixer_forward(): pl.pallas_call(functools.partial(mixer_forward_kernel, count), in_specs=[...  75.3 us
    unnamed x572, local copies, waits for them, and re-layouts  33.4 us
  transfers between devices with their start and end apart: 3, of which 0 were waited for; matrix products, arithmetic and copies ran while one was open for 4% of the time, Pallas kernels for 0%

profile of v2, /device:TPU:0, one launch (start us, length us, event | category | flops | bytes accessed | tf_op | source)
XLA Modules:
  0.0 1121.0 jit_solution(873369018649412193)
XLA Ops:
  4.5 149.9 %weights_gather.1 = (bf16[2,16,1152]{2,1,0:T(8,128)(2,1)S(1)}, bf16[8,144,1536]{2,1,0:T(8,128)(2,1)}, bf16[4,384,1152]{2,1,0:T(8,128)(2,1)}, bf16[2,8,144,1152]{...) custom-call(bf16[2,128,1152]{2,1,0:T(8,128)(2,1)S(1)} %copy-done.6, ...), custom_call_target="tpu_custom_call" | custom-call | tf_op jit(solution)/shard_map/weights_gather/pallas_call | solution.py:828
  160.1 6.6 fusion.145
  171.4 25.4 %mixer_forward.3 = (f32[128,2304]{1,0:T(8,128)S(1)}, f32[16,16,2304]{2,1,0:T(8,128)}) custom-call(f32[128,2304]{1,0:T(8,128)S(1)} %get-tuple-element.329.step_ref, f32[128,2304]{1,0:T(8,128)S(1)} %get-tuple-element.328.drive_ref, f32[128,16,128]{2,1,0:T(8,128)S(1)} %broadcast_in_dim.48.bb_ref, f32[128,16,128]{2,1,0:T(8,128)S(1)} %broadcast_in_dim.49.cb_ref, ...), custom_call_target="tpu_custom_call" | custom-call | tf_op jit(solution)/shard_map/mixer_forward/pallas_call | solution.py:1175
  206.7 58.1 %experts_forward.2 = (bf16[2,48,1152]{2,1,0:T(8,128)(2,1)}, bf16[128,1152]{1,0:T(8,128)(2,1)}, bf16[128,1152]{1,0:T(8,128)(2,1)}, bf16[16,1152]{1,0:T(8,128)(2,1)}, bf16[8,2,48,1152]{3,2,1,0:T(8,128)(2,1)}) custom-call(bf16[2,48,1152]{2,1,0:T(8,128)(2,1)} %bitcast.286, f32[128,1152]{1,0:T(8,128)} %copy-done.61, bf16[128,96]{1,0:T(8,128)(2,1)} %get-tuple-element.355.refs_2_, ...), custom_call_target="tpu_custom_call" | custom-call | tf_op jit(solution)/shard_map/experts_forward/pallas_call | solution.py:632
  266.3 6.6 fusion.143
  282.6 24.9 %mixer_forward.4 = (f32[128,2304]{1,0:T(8,128)S(1)}, f32[16,16,2304]{2,1,0:T(8,128)}) custom-call(f32[128,2304]{1,0:T(8,128)S(1)} %get-tuple-element.284.step_ref, f32[128,2304]{1,0:T(8,128)S(1)} %get-tuple-element.283.drive_ref, f32[128,16,128]{2,1,0:T(8,128)S(1)} %broadcast_in_dim.50.bb_ref, f32[128,16,128]{2,1,0:T(8,128)S(1)} %broadcast_in_dim.51.cb_ref, ...), custom_call_target="tpu_custom_call" | custom-call | tf_op jit(solution)/shard_map/mixer_forward/pallas_call | solution.py:1175
  317.9 60.7 %experts_forward.3 = (bf16[2,48,1152]{2,1,0:T(8,128)(2,1)}, bf16[128,1152]{1,0:T(8,128)(2,1)}, bf16[128,1152]{1,0:T(8,128)(2,1)}, bf16[16,1152]{1,0:T(8,128)(2,1)}, bf16[8,2,48,1152]{3,2,1,0:T(8,128)(2,1)}) custom-call(bf16[2,48,1152]{2,1,0:T(8,128)(2,1)} %bitcast.285, f32[128,1152]{1,0:T(8,128)} %copy-done.33, bf16[128,96]{1,0:T(8,128)(2,1)} %get-tuple-element.354.refs_2_, ...), custom_call_target="tpu_custom_call" | custom-call | tf_op jit(solution)/shard_map/experts_forward/pallas_call | solution.py:632
  380.4 9.6 broadcast_select_fusion.4
  401.8 25.0 %mixer_forward.5 = (f32[128,2304]{1,0:T(8,128)S(1)}, f32[16,16,2304]{2,1,0:T(8,128)}) custom-call(f32[128,2304]{1,0:T(8,128)S(1)} %copy-done.14, f32[128,2304]{1,0:T(8,128)S(1)} %get-tuple-element.339.drive_ref, f32[128,16,128]{2,1,0:T(8,128)S(1)} %broadcast_in_dim.52.bb_ref, f32[128,16,128]{2,1,0:T(8,128)S(1)} %broadcast_in_dim.53.cb_ref, ...), custom_call_target="tpu_custom_call" | custom-call | tf_op jit(solution)/shard_map/mixer_forward/pallas_call | solution.py:1175
  438.5 83.0 %experts_both.1 = (bf16[2,48,1152]{2,1,0:T(8,128)(2,1)}, bf16[128,1152]{1,0:T(8,128)(2,1)}, bf16[8,2,48,1152]{3,2,1,0:T(8,128)(2,1)}, bf16[128,1152]{1,0:T(8,128...) custom-call(bf16[2,48,1152]{2,1,0:T(8,128)(2,1)} %bitcast.284, ...), custom_call_target="tpu_custom_call" | custom-call | tf_op jit(solution)/shard_map/experts_both/pallas_call | solution.py:632
  533.2 38.9 %mixer_backward.3 = (f32[128,2304]{1,0:T(8,128)S(1)}, f32[128,2304]{1,0:T(8,128)}, f32[128,16,128]{2,1,0:T(8,128)S(1)}, f32[128,16,128]{2,1,0:T(8,128)S(1)}, f32[16,2304]{1,0:T(8,128)S(1)}) custom-call(f32[128,2304]{1,0:T(8,128)} %copy-done.1, f32[128,2304]{1,0:T(8,128)} %copy-done, f32[128,2304]{1,0:T(8,128)} %get-tuple-element.277.dy_ref, ...), custom_call_target="tpu_custom_call" | custom-call | tf_op jit(solution)/shard_map/mixer_backward/pallas_call | solution.py:1205
  615.7 7.6 multiply_convert_fusion
  623.3 7.3 fusion.116
  631.6 63.6 %experts_backward.2 = (bf16[128,1152]{1,0:T(8,128)(2,1)}, bf16[2,48,1152]{2,1,0:T(8,128)(2,1)}, bf16[8,2,48,1152]{3,2,1,0:T(8,128)(2,1)}, bf16[8,96,1536]{2,1,0:T(8,128)(2,1)}, bf16[8,96,1536]{2,1,0:T(8,128)(2,1)}) custom-call(bf16[128,1152]{1,0:T(8,128)(2,1)} %fusion.110.refs_0_, bf16[128,1152]{1,0:T(8,128)(2,1)} %get-tuple-element.290.refs_1_, ...), custom_call_target="tpu_custom_call" | custom-call | tf_op jit(solution)/shard_map/experts_backward/pallas_call | solution.py:632
  701.8 7.7 fusion.52
  710.2 38.0 %mixer_backward.4 = (f32[128,2304]{1,0:T(8,128)S(1)}, f32[128,2304]{1,0:T(8,128)}, f32[128,16,128]{2,1,0:T(8,128)S(1)}, f32[128,16,128]{2,1,0:T(8,128)S(1)}, f32[16,2304]{1,0:T(8,128)S(1)}) custom-call(f32[128,2304]{1,0:T(8,128)} %get-tuple-element.287.step_ref, f32[128,2304]{1,0:T(8,128)} %get-tuple-element.288.drive_ref, ...), custom_call_target="tpu_custom_call" | custom-call | tf_op jit(solution)/shard_map/mixer_backward/pallas_call | solution.py:1205
  772.4 7.4 fusion.103
  781.8 64.5 %experts_backward.3 = (bf16[128,1152]{1,0:T(8,128)(2,1)}, bf16[2,48,1152]{2,1,0:T(8,128)(2,1)}, bf16[8,2,48,1152]{3,2,1,0:T(8,128)(2,1)}, bf16[8,96,1536]{2,1,0:T(8,128)(2,1)}, bf16[8,96,1536]{2,1,0:T(8,128)(2,1)}) custom-call(bf16[128,1152]{1,0:T(8,128)(2,1)} %get-tuple-element.252.refs_0_, bf16[128,1152]{1,0:T(8,128)(2,1)} %broadcast.467.refs_1_, ...), custom_call_target="tpu_custom_call" | custom-call | tf_op jit(solution)/shard_map/experts_backward/pallas_call | solution.py:632
  852.2 6.4 fusion.59
  858.6 38.1 %mixer_backward.5 = (f32[128,2304]{1,0:T(8,128)S(1)}, f32[128,2304]{1,0:T(8,128)}, f32[128,16,128]{2,1,0:T(8,128)S(1)}, f32[128,16,128]{2,1,0:T(8,128)S(1)}, f32[16,2304]{1,0:T(8,128)S(1)}) custom-call(f32[128,2304]{1,0:T(8,128)} %copy-done.1, f32[128,2304]{1,0:T(8,128)} %copy-done, f32[128,2304]{1,0:T(8,128)} %get-tuple-element.244.dy_ref, ...), custom_call_target="tpu_custom_call" | custom-call | tf_op jit(solution)/shard_map/mixer_backward/pallas_call | solution.py:1205
  918.9 7.8 convolution_convert_fusion
  926.8 8.6 fusion.3
  944.0 156.5 %grads_reduce.1 = (bf16[4,144,3072]{2,1,0:T(8,128)(2,1)}, f32[144,1152]{1,0:T(8,128)}, f32[144,1152]{1,0:T(8,128)}, f32[144,1152]{1,0:T(8,128)}, f32[144,256]{1,0:T(8,128)}) custom-call(bf16[2,1152,256]{2,1,0:T(8,128)(2,1)} %bitcast.279, bf16[8,144,1536]{2,1,0:T(8,128)(2,1)} %bitcast.280, bf16[128,1152]{1,0:T(8,128)(2,1)} %get-tuple-element.293.refs_0_, ...), custom_call_target="tpu_custom_call" | custom-call | tf_op jit(solution)/shard_map/grads_reduce/pallas_call | solution.py:1042
  1110.8 6.0 bitcast_convert_fusion
  (790 shorter events, 208.2 us)
Async XLA Ops:
  154.4 120.5 %copy-start.4 = (bf16[2,8,144,256]{3,2,1,0:T(8,128)(2,1)}, bf16[2,8,144,256]{3,2,1,0:T(8,128)(2,1)S(1)}, u32[]{:S(2)}) copy-start(bf16[2,8,144,256]{3,2,1,0:T(8,128)(2,1)S(1)} %get-tuple-element.77) | copy-start | bytes 3538948
  157.5 108.2 %copy-start.158 = (f32[1152]{0:T(1024)}, f32[1152]{0:T(1024)S(1)}, u32[]{:S(2)}) copy-start(f32[1152]{0:T(1024)S(1)} %get-tuple-element.209) | copy-start | bytes 13828
  158.9 114.1 %copy-start.111 = (f32[2304]{0:T(1024)}, f32[2304]{0:T(1024)S(1)}, u32[]{:S(2)}) copy-start(f32[2304]{0:T(1024)S(1)} %get-tuple-element.204) | copy-start | bytes 27652
  158.9 114.1 %copy-start.115 = (f32[2304]{0:T(1024)}, f32[2304]{0:T(1024)S(1)}, u32[]{:S(2)}) copy-start(f32[2304]{0:T(1024)S(1)} %get-tuple-element.205) | copy-start | bytes 27652
  158.9 114.1 %copy-start.119 = (f32[2304]{0:T(1024)}, f32[2304]{0:T(1024)S(1)}, u32[]{:S(2)}) copy-start(f32[2304]{0:T(1024)S(1)} %get-tuple-element.206) | copy-start | bytes 27652
  158.9 114.1 %copy-start.123 = (f32[2304]{0:T(1024)}, f32[2304]{0:T(1024)S(1)}, u32[]{:S(2)}) copy-start(f32[2304]{0:T(1024)S(1)} %get-tuple-element.207) | copy-start | bytes 27652
  158.9 114.1 %copy-start.134 = (f32[2304]{0:T(1024)}, f32[2304]{0:T(1024)S(1)}, u32[]{:S(2)}) copy-start(f32[2304]{0:T(1024)S(1)} %get-tuple-element.208) | copy-start | bytes 27652
  159.9 105.7 %copy-start.132 = (bf16[2,16,1152]{2,1,0:T(8,128)(2,1)}, bf16[2,16,1152]{2,1,0:T(8,128)(2,1)S(1)}, u32[]{:S(2)}) copy-start(bf16[2,16,1152]{2,1,0:T(8,128)(2,1)S(1)} %broadcast_select_fusion.12) | copy-start | bytes 221188
  436.3 87.3 %copy-start.221 = (f32[128]{0:T(128)}, f32[128]{0:T(128)S(1)}, u32[]{:S(2)}) copy-start(f32[128]{0:T(128)S(1)} %get-tuple-element.325) | copy-start | bytes 1540
  438.5 83.1 %copy-start.273 = (bf16[2,48,1152]{2,1,0:T(8,128)(2,1)S(1)}, bf16[2,48,1152]{2,1,0:T(8,128)(2,1)}, u32[]{:S(2)}) copy-start(bf16[2,48,1152]{2,1,0:T(8,128)(2,1)} %get-tuple-element.97) | copy-start | bytes 663556
  438.5 84.5 %copy-start.154 = (f32[128,8]{0,1:T(8,128)S(1)}, f32[128,8]{0,1:T(8,128)}, u32[]{:S(2)}) copy-start(f32[128,8]{0,1:T(8,128)} %get-tuple-element.268) | copy-start | bytes 12292
  438.5 84.5 %copy-start.200 = (s32[128]{0:T(128)S(1)}, s32[128]{0:T(128)}, u32[]{:S(2)}) copy-start(s32[128]{0:T(128)} %get-tuple-element.314) | copy-start | bytes 1540
  438.5 84.5 %copy-start.206 = (s32[128]{0:T(128)S(1)}, s32[128]{0:T(128)}, u32[]{:S(2)}) copy-start(s32[128]{0:T(128)} %get-tuple-element.306) | copy-start | bytes 1540
  591.1 24.5 %collective-permute-start = (f32[8,2304]{1,0:T(8,128)}, f32[8,2304]{1,0:T(8,128)}, u32[]{:S(2)}, u32[]{:S(2)}) collective-permute-start(f32[8,2304]{1,0:T(8,128)} %slice.441), channel_id=1, source_target_pairs={{1,0},{2,1},{3,2},{4,3},{5,4},{6,5},{7,6},{8,7},{9,8},{10,9},{11,1... | collective-permute-start | bytes 221192 | tf_op jit(solution)/shard_map/ppermute | solution.py:1253
  598.2 102.0 %copy-start.198 = (f32[128]{0:T(128)}, f32[128]{0:T(128)S(1)}, u32[]{:S(2)}) copy-start(f32[128]{0:T(128)S(1)} %add_rsqrt_fusion.4) | copy-start | bytes 1540
  601.3 95.4 %copy-start.195 = (f32[128]{0:T(128)}, f32[128]{0:T(128)S(1)}, u32[]{:S(2)}) copy-start(f32[128]{0:T(128)S(1)} %get-tuple-element.348) | copy-start | bytes 1540
  631.6 65.1 %copy-start.204 = (s32[128]{0:T(128)S(1)}, s32[128]{0:T(128)}, u32[]{:S(2)}) copy-start(s32[128]{0:T(128)} %get-tuple-element.261) | copy-start | bytes 1540
  631.6 65.1 %copy-start.209 = (f32[128]{0:T(128)S(1)}, f32[128]{0:T(128)}, u32[]{:S(2)}) copy-start(f32[128]{0:T(128)} %copy-done.208) | copy-start | bytes 1540
  631.6 65.1 %copy-start.219 = (f32[128]{0:T(128)S(1)}, f32[128]{0:T(128)}, u32[]{:S(2)}) copy-start(f32[128]{0:T(128)} %get-tuple-element.324) | copy-start | bytes 1540
  767.0 3.2 collective-permute-start.1
  781.8 64.6 %copy-start.274 = (bf16[2,48,1152]{2,1,0:T(8,128)(2,1)S(1)}, bf16[2,48,1152]{2,1,0:T(8,128)(2,1)}, u32[]{:S(2)}) copy-start(bf16[2,48,1152]{2,1,0:T(8,128)(2,1)} %get-tuple-element.97) | copy-start | bytes 663556
  781.8 66.1 %copy-start.201 = (s32[128]{0:T(128)S(1)}, s32[128]{0:T(128)}, u32[]{:S(2)}) copy-start(s32[128]{0:T(128)} %get-tuple-element.314) | copy-start | bytes 1540
  781.8 66.1 %copy-start.223 = (f32[128]{0:T(128)S(1)}, f32[128]{0:T(128)}, u32[]{:S(2)}) copy-start(f32[128]{0:T(128)} %get-tuple-element.323) | copy-start | bytes 1540
  910.0 26.0 %collective-permute-start.2 = (f32[8,2304]{1,0:T(8,128)S(1)}, f32[8,2304]{1,0:T(8,128)S(1)}, u32[]{:S(2)}, u32[]{:S(2)}) collective-permute-start(f32[8,2304]{1,0:T(8,128)S(1)} %slice.459), channel_id=1, source_target_pairs={{1,0},{2,1},{3,2},{4,3},{5,4},{6,5},{7,6},{8,7},{9,8},{10,9},{11,1... | collective-permute-start | bytes 221192 | tf_op jit(solution)/shard_map/ppermute | solution.py:1253
  (259 other events, 1927.4 us)

commit v3 on v2

--- a/solution.py
+++ b/solution.py
@@ -981,8 +981,13 @@
     vec_copies[1].wait_recv()
     put(
         3,
-        mm(halves[3][...], wholes[2][...], over)
-        + mm(halves[4][...], wholes[3][...], over)
+        jnp.concatenate(
+            [
+                mm(halves[3][...], wholes[2][...], over),
+                mm(halves[4][...], wholes[3][...], over),
+            ],
+            1,
+        )
         + vecs[0].astype(f32)
         + vecs[1].astype(f32),
     )
@@ -1038,7 +1043,7 @@
     each = EXPERTS // 2
     rows = 2 * micro * length
     shares = [(share, model)] * 3 + [(share, lanes)]
-    wholes = [model, model, lanes, lanes]
+    wholes = [value.shape[1] for value in given[0][:4]]
     return pl.pallas_call(
         functools.partial(grads_reduce_kernel, count, micro),
         in_specs=[anywhere] * (2 + 8 * micro),
@@ -1290,9 +1295,9 @@
 
 
 def selective(projected, weights):
-    rank = weights["dt_proj"].shape[0]
+    rank = weights["rank"]
     states = weights["rates"].shape[0]
-    dt_low = projected[:, :rank].astype(bf16)
+    dt_low = jnp.where(jnp.arange(projected.shape[1])[None] < rank, projected, 0.0).astype(bf16)
     dt_raw = nn(dt_low, weights["dt_proj"]) + weights["dt_bias"]
     in_map = projected[:, rank : rank + states]
     out_map = projected[:, rank + states : rank + 2 * states]
@@ -1379,9 +1384,10 @@
     grad_dt_bias = sums(d_raw)
     d_raw_low = d_raw.astype(bf16)
     d_low = nt(d_raw_low, weights["dt_proj"])
-    d_projected = jnp.concatenate(
-        [d_low, jnp.sum(d_in_map, -1), jnp.sum(d_out_map, -1)], 1
-    ).astype(bf16)
+    rank, states = weights["rank"], weights["rates"].shape[0]
+    d_maps = jnp.concatenate([jnp.sum(d_in_map, -1), jnp.sum(d_out_map, -1)], 1)
+    d_maps = jnp.pad(d_maps, ((0, 0), (rank, d_low.shape[1] - rank - 2 * states)))
+    d_projected = (d_low + d_maps).astype(bf16)
     d_signal = d_signal + nt(d_projected, weights["x_proj"])
     d_summed = signal_back(d_signal)[0]
     taps = weights["conv_w"].shape[0]
@@ -1399,13 +1405,11 @@
     d_normed_in = nn(d_xz, weights["w_in"])
     d_inputs, grad_norm = normalize_back(inputs, weights["norm_gain"], d_normed_in)
     result = (d_resid + d_inputs).astype(bf16)
-    low, rank = d_projected.shape[1], dt_low.shape[1]
-    lanes = (-sum(weights["sizes"])) % LANES + sum(weights["sizes"])
     given = (
         normed,
         d_mixer,
-        jnp.pad(d_projected, ((0, 0), (0, lanes - low))),
-        jnp.pad(dt_low, ((0, 0), (low, lanes - low - rank))),
+        d_projected,
+        dt_low,
         d_xz,
         gated,
         signal,
@@ -1431,7 +1435,11 @@
         skip[0][:, None], a_log[0].T, norm_gain[0][:, None], moe_gain[0][:, None], router[0],
     ]
     sizes = [piece.shape[1] for piece in pieces]
-    pad = (-sum(sizes)) % LANES
+    lead = -(-sizes[0] // LANES) * LANES
+    begins = [0] + [lead + sum(sizes[1:n]) for n in range(1, len(sizes))]
+    places = list(zip(begins, sizes, strict=True))
+    pieces.insert(1, jnp.zeros((share, lead - sizes[0]), f32))
+    pad = (-sum(sizes[1:])) % LANES
     small = jnp.concatenate(pieces + [jnp.zeros((share, pad), f32)], 1).astype(bf16)
     halos, up, low_down, in_x, in_z, out, small = weights_gather(
         tokens, w_up[0], w_down[0], [low_in[0], low_in[1], w_out[0].astype(bf16), small]
@@ -1440,18 +1448,14 @@
     w_in_all = jnp.concatenate([in_x.reshape(width, model), in_z.reshape(width, model)], 0)
     table = small.reshape(width, -1)
     rows = table.astype(f32).T
-    at = 0
-    found = []
-    for size in sizes:
-        found.append(rows[at : at + size])
-        at += size
+    found = [rows[begin : begin + size] for begin, size in places]
     unused, dt_proj, conv_w, conv_b, dt_bias, a_skip, a_log, norm_gain, moe_gain, router = found
     weights = dict(
-        sizes=sizes,
+        rank=sizes[1],
         w_in=w_in_all,
         w_out=out.reshape(width, model),
-        x_proj=table[:, : sizes[0]],
-        dt_proj=dt_proj.astype(bf16),
+        x_proj=table[:, :lead],
+        dt_proj=jnp.pad(dt_proj, ((0, lead - sizes[1]), (0, 0))).astype(bf16),
         conv_w=conv_w,
         conv_b=conv_b,
         dt_bias=dt_bias,
@@ -1463,25 +1467,21 @@
         w_up=up.reshape(-1, up.shape[2]),
         w_down=low_down.reshape(-1, model),
     )
-    return weights, sizes, halos
-
-
-def mixer_grads(given, vectors, sizes, up, count):
+    return weights, places, halos
+
+
+def mixer_grads(given, vectors, places, up, count):
     channel, d_rates, feature, grad_router = vectors
     feature = jnp.concatenate([piece[None] for piece in feature] + [grad_router.T], 0)
     rows = jnp.concatenate(
         [piece[None] for piece in channel] + [d_rates, jnp.concatenate([feature, feature], 1)], 0
     )
-    begin = sizes[0] + sizes[1]
-    lanes = -(-sum(sizes) // LANES) * LANES
+    begin = places[2][0]
+    lanes = -(-sum(places[-1]) // LANES) * LANES
     vec = jnp.pad(rows.T.astype(bf16), ((0, 0), (begin, lanes - begin - rows.shape[0])))
     vec = vec.reshape(2, -1, lanes)
     up, grad_x, grad_z, grad_out, small = grads_reduce(vec, up, given)
-    at = 0
-    found = []
-    for size in sizes:
-        found.append(small[:, at : at + size])
-        at += size
+    found = [small[:, begin : begin + size] for begin, size in places]
     x_proj, dt_proj, conv_w, conv_b, dt_bias, skip, a_log, norm_gain, moe_gain, router = found
     return (
         norm_gain[:, 0],
@@ -1527,7 +1527,7 @@
     count = lax.axis_size("dp")
     section = lax.axis_index("section")
     top = section == 1
-    weights, sizes, halos = gather_weights(
+    weights, places, halos = gather_weights(
         tokens, norm_gain, w_in, conv_w, conv_b, x_proj, dt_proj, dt_bias, a_log, skip, w_out, moe_gain,
         router, w_up, w_down,
     )
@@ -1603,7 +1603,7 @@
         return jax.tree.map(lambda a, b: jnp.where(top, a, b), found[0][place], found[2][place])
 
     vectors = jax.tree.map(lambda a, b: a + b, valid_one(1), found[1][1])
-    mixer = mixer_grads([valid_one(0), found[1][0]], vectors, sizes, moving, count)
+    mixer = mixer_grads([valid_one(0), found[1][0]], vectors, places, moving, count)
     down = down_grad(one[:2], last[1][:2])
     return (outputs[None], backs[None]) + tuple(v[None] for v in mixer) + (down[None],)
 

time: 1130 us -> 1120 us (level)
    unnamed x572 -> x552, local copies, waits for them, and re-layouts: 33.4 us -> 32.9 us
  transfers between devices with their start and end apart: 3 -> 3, of which waited for: 0 -> 1; matrix products, arithmetic and copies ran while one was open for 4% -> 3% of each run, Pallas kernels for 0% -> 0%
where the time goes in v3:
time: 1120 us; the launch traced here: 1110 us
  Pallas kernels  827 us (74%)
  matrix products  132 us (12%)
  other arithmetic  78.6 us (7%)
  local copies, waits for them, and re-layouts  66.1 us (6%)
    pallas_call x5, Pallas kernels, experts(): pl.pallas_call(functools.partial(experts_kernel, count, bool(ahead), bool...  329 us
    pallas_call x1, Pallas kernels, grads_reduce(): pl.pallas_call(functools.partial(grads_reduce_kernel, count, micro), in_s...  158 us
    pallas_call x1, Pallas kernels, weights_gather(): pl.pallas_call(functools.partial(weights_gather_kernel, count, parts), in...  150 us
    dot_general x36, matrix products, dot(): lax.dot_general(a, b, (dims, ((), ())), preferred_element_type=f32)  121 us
    pallas_call x3, Pallas kernels, mixer_backward(): pl.pallas_call(functools.partial(mixer_backward_kernel, count), in_specs=...  115 us
    pallas_call x3, Pallas kernels, mixer_forward(): pl.pallas_call(functools.partial(mixer_forward_kernel, count), in_specs=[...  75.5 us
    unnamed x552, local copies, waits for them, and re-layouts  32.9 us
  transfers between devices with their start and end apart: 3, of which 1 were waited for; matrix products, arithmetic and copies ran while one was open for 3% of the time, Pallas kernels for 0%

profile of v3, /device:TPU:0, one launch (start us, length us, event | category | flops | bytes accessed | tf_op | source)
XLA Modules:
  0.0 1112.8 jit_solution(11392004875752608171)
XLA Ops:
  4.5 149.9 %weights_gather.1 = (bf16[2,16,1152]{2,1,0:T(8,128)(2,1)S(1)}, bf16[8,144,1536]{2,1,0:T(8,128)(2,1)}, bf16[4,384,1152]{2,1,0:T(8,128)(2,1)}, bf16[2,8,144,1152]{...) custom-call(bf16[2,128,1152]{2,1,0:T(8,128)(2,1)S(1)} %copy-done.6, ...), custom_call_target="tpu_custom_call" | custom-call | tf_op jit(solution)/shard_map/weights_gather/pallas_call | solution.py:828
  159.9 6.7 fusion.155
  175.3 25.5 %mixer_forward.3 = (f32[128,2304]{1,0:T(8,128)S(1)}, f32[16,16,2304]{2,1,0:T(8,128)}) custom-call(f32[128,2304]{1,0:T(8,128)S(1)} %get-tuple-element.379.step_ref, f32[128,2304]{1,0:T(8,128)S(1)} %get-tuple-element.378.drive_ref, f32[128,16,128]{2,1,0:T(8,128)S(1)} %broadcast_in_dim.91.bb_ref, f32[128,16,128]{2,1,0:T(8,128)S(1)} %broadcast_in_dim.92.cb_ref, ...), custom_call_target="tpu_custom_call" | custom-call | tf_op jit(solution)/shard_map/mixer_forward/pallas_call | solution.py:1180
  210.9 58.1 %experts_forward.2 = (bf16[2,48,1152]{2,1,0:T(8,128)(2,1)}, bf16[128,1152]{1,0:T(8,128)(2,1)}, bf16[128,1152]{1,0:T(8,128)(2,1)}, bf16[16,1152]{1,0:T(8,128)(2,1)}, bf16[8,2,48,1152]{3,2,1,0:T(8,128)(2,1)}) custom-call(bf16[2,48,1152]{2,1,0:T(8,128)(2,1)} %bitcast.282, f32[128,1152]{1,0:T(8,128)} %copy-done.63, bf16[128,96]{1,0:T(8,128)(2,1)} %get-tuple-element.407.refs_2_, ...), custom_call_target="tpu_custom_call" | custom-call | tf_op jit(solution)/shard_map/experts_forward/pallas_call | solution.py:632
  269.9 6.6 fusion.153
  285.9 25.0 %mixer_forward.4 = (f32[128,2304]{1,0:T(8,128)S(1)}, f32[16,16,2304]{2,1,0:T(8,128)}) custom-call(f32[128,2304]{1,0:T(8,128)S(1)} %get-tuple-element.334.step_ref, f32[128,2304]{1,0:T(8,128)S(1)} %get-tuple-element.333.drive_ref, f32[128,16,128]{2,1,0:T(8,128)S(1)} %broadcast_in_dim.93.bb_ref, f32[128,16,128]{2,1,0:T(8,128)S(1)} %broadcast_in_dim.94.cb_ref, ...), custom_call_target="tpu_custom_call" | custom-call | tf_op jit(solution)/shard_map/mixer_forward/pallas_call | solution.py:1180
  321.3 60.8 %experts_forward.3 = (bf16[2,48,1152]{2,1,0:T(8,128)(2,1)}, bf16[128,1152]{1,0:T(8,128)(2,1)}, bf16[128,1152]{1,0:T(8,128)(2,1)}, bf16[16,1152]{1,0:T(8,128)(2,1)}, bf16[8,2,48,1152]{3,2,1,0:T(8,128)(2,1)}) custom-call(bf16[2,48,1152]{2,1,0:T(8,128)(2,1)} %bitcast.281, f32[128,1152]{1,0:T(8,128)} %copy-done.34, bf16[128,96]{1,0:T(8,128)(2,1)} %get-tuple-element.406.refs_2_, ...), custom_call_target="tpu_custom_call" | custom-call | tf_op jit(solution)/shard_map/experts_forward/pallas_call | solution.py:632
  383.8 9.6 broadcast_select_fusion.4
  405.9 25.0 %mixer_forward.5 = (f32[128,2304]{1,0:T(8,128)S(1)}, f32[16,16,2304]{2,1,0:T(8,128)}) custom-call(f32[128,2304]{1,0:T(8,128)S(1)} %copy-done.14, f32[128,2304]{1,0:T(8,128)S(1)} %get-tuple-element.389.drive_ref, f32[128,16,128]{2,1,0:T(8,128)S(1)} %broadcast_in_dim.95.bb_ref, f32[128,16,128]{2,1,0:T(8,128)S(1)} %broadcast_in_dim.96.cb_ref, ...), custom_call_target="tpu_custom_call" | custom-call | tf_op jit(solution)/shard_map/mixer_forward/pallas_call | solution.py:1180
  441.6 83.0 %experts_both.1 = (bf16[2,48,1152]{2,1,0:T(8,128)(2,1)}, bf16[128,1152]{1,0:T(8,128)(2,1)}, bf16[8,2,48,1152]{3,2,1,0:T(8,128)(2,1)}, bf16[128,1152]{1,0:T(8,128...) custom-call(bf16[2,48,1152]{2,1,0:T(8,128)(2,1)} %bitcast.280, ...), custom_call_target="tpu_custom_call" | custom-call | tf_op jit(solution)/shard_map/experts_both/pallas_call | solution.py:632
  529.8 5.9 fusion.342
  535.7 38.6 %mixer_backward.3 = (f32[128,2304]{1,0:T(8,128)S(1)}, f32[128,2304]{1,0:T(8,128)}, f32[128,16,128]{2,1,0:T(8,128)S(1)}, f32[128,16,128]{2,1,0:T(8,128)S(1)}, f32[16,2304]{1,0:T(8,128)S(1)}) custom-call(f32[128,2304]{1,0:T(8,128)} %copy-done.1, f32[128,2304]{1,0:T(8,128)} %copy-done, f32[128,2304]{1,0:T(8,128)} %get-tuple-element.327.dy_ref, ...), custom_call_target="tpu_custom_call" | custom-call | tf_op jit(solution)/shard_map/mixer_backward/pallas_call | solution.py:1210
  606.7 7.9 multiply_convert_fusion
  614.6 7.3 fusion.126
  622.9 62.9 %experts_backward.2 = (bf16[128,1152]{1,0:T(8,128)(2,1)}, bf16[2,48,1152]{2,1,0:T(8,128)(2,1)}, bf16[8,2,48,1152]{3,2,1,0:T(8,128)(2,1)}, bf16[8,96,1536]{2,1,0:T(8,128)(2,1)}, bf16[8,96,1536]{2,1,0:T(8,128)(2,1)}) custom-call(bf16[128,1152]{1,0:T(8,128)(2,1)} %fusion.120.refs_0_, bf16[128,1152]{1,0:T(8,128)(2,1)} %get-tuple-element.340.refs_1_, ...), custom_call_target="tpu_custom_call" | custom-call | tf_op jit(solution)/shard_map/experts_backward/pallas_call | solution.py:632
  692.4 7.7 fusion.52
  700.7 38.0 %mixer_backward.4 = (f32[128,2304]{1,0:T(8,128)S(1)}, f32[128,2304]{1,0:T(8,128)}, f32[128,16,128]{2,1,0:T(8,128)S(1)}, f32[128,16,128]{2,1,0:T(8,128)S(1)}, f32[16,2304]{1,0:T(8,128)S(1)}) custom-call(f32[128,2304]{1,0:T(8,128)} %get-tuple-element.337.step_ref, f32[128,2304]{1,0:T(8,128)} %get-tuple-element.338.drive_ref, ...), custom_call_target="tpu_custom_call" | custom-call | tf_op jit(solution)/shard_map/mixer_backward/pallas_call | solution.py:1210
  768.1 64.4 %experts_backward.3 = (bf16[128,1152]{1,0:T(8,128)(2,1)}, bf16[2,48,1152]{2,1,0:T(8,128)(2,1)}, bf16[8,2,48,1152]{3,2,1,0:T(8,128)(2,1)}, bf16[8,96,1536]{2,1,0:T(8,128)(2,1)}, bf16[8,96,1536]{2,1,0:T(8,128)(2,1)}) custom-call(bf16[128,1152]{1,0:T(8,128)(2,1)} %get-tuple-element.300.refs_0_, bf16[128,1152]{1,0:T(8,128)(2,1)} %broadcast.476.refs_1_, ...), custom_call_target="tpu_custom_call" | custom-call | tf_op jit(solution)/shard_map/experts_backward/pallas_call | solution.py:632
  838.2 6.4 fusion.59
  844.6 38.0 %mixer_backward.5 = (f32[128,2304]{1,0:T(8,128)S(1)}, f32[128,2304]{1,0:T(8,128)}, f32[128,16,128]{2,1,0:T(8,128)S(1)}, f32[128,16,128]{2,1,0:T(8,128)S(1)}, f32[16,2304]{1,0:T(8,128)S(1)}) custom-call(f32[128,2304]{1,0:T(8,128)} %copy-done.1, f32[128,2304]{1,0:T(8,128)} %copy-done, f32[128,2304]{1,0:T(8,128)} %get-tuple-element.292.dy_ref, ...), custom_call_target="tpu_custom_call" | custom-call | tf_op jit(solution)/shard_map/mixer_backward/pallas_call | solution.py:1210
  910.2 7.5 convolution_convert_fusion
  917.8 8.5 fusion.3
  934.3 157.8 %grads_reduce.1 = (bf16[4,144,3072]{2,1,0:T(8,128)(2,1)}, f32[144,1152]{1,0:T(8,128)}, f32[144,1152]{1,0:T(8,128)}, f32[144,1152]{1,0:T(8,128)}, f32[144,256]{1,0:T(8,128)}) custom-call(bf16[2,1152,256]{2,1,0:T(8,128)(2,1)} %bitcast.275, bf16[8,144,1536]{2,1,0:T(8,128)(2,1)} %bitcast.276, bf16[128,1152]{1,0:T(8,128)(2,1)} %get-tuple-element.343.refs_0_, ...), custom_call_target="tpu_custom_call" | custom-call | tf_op jit(solution)/shard_map/grads_reduce/pallas_call | solution.py:1047
  1102.3 6.0 bitcast_convert_fusion
  (765 shorter events, 201.1 us)
Async XLA Ops:
  154.5 124.0 %copy-start.4 = (bf16[2,8,144,256]{3,2,1,0:T(8,128)(2,1)}, bf16[2,8,144,256]{3,2,1,0:T(8,128)(2,1)S(1)}, u32[]{:S(2)}) copy-start(bf16[2,8,144,256]{3,2,1,0:T(8,128)(2,1)S(1)} %get-tuple-element.77) | copy-start | bytes 3538948
  156.9 112.9 %copy-start.173 = (f32[1152]{0:T(1024)}, f32[1152]{0:T(1024)S(1)}, u32[]{:S(2)}) copy-start(f32[1152]{0:T(1024)S(1)} %get-tuple-element.257) | copy-start | bytes 13828
  157.1 119.4 %copy-start.125 = (f32[2304]{0:T(1024)}, f32[2304]{0:T(1024)S(1)}, u32[]{:S(2)}) copy-start(f32[2304]{0:T(1024)S(1)} %get-tuple-element.252) | copy-start | bytes 27652
  157.1 119.4 %copy-start.129 = (f32[2304]{0:T(1024)}, f32[2304]{0:T(1024)S(1)}, u32[]{:S(2)}) copy-start(f32[2304]{0:T(1024)S(1)} %get-tuple-element.253) | copy-start | bytes 27652
  157.2 119.4 %copy-start.133 = (f32[2304]{0:T(1024)}, f32[2304]{0:T(1024)S(1)}, u32[]{:S(2)}) copy-start(f32[2304]{0:T(1024)S(1)} %get-tuple-element.254) | copy-start | bytes 27652
  157.2 119.4 %copy-start.137 = (f32[2304]{0:T(1024)}, f32[2304]{0:T(1024)S(1)}, u32[]{:S(2)}) copy-start(f32[2304]{0:T(1024)S(1)} %get-tuple-element.255) | copy-start | bytes 27652
  157.2 119.4 %copy-start.148 = (f32[2304]{0:T(1024)}, f32[2304]{0:T(1024)S(1)}, u32[]{:S(2)}) copy-start(f32[2304]{0:T(1024)S(1)} %get-tuple-element.256) | copy-start | bytes 27652
  157.2 121.8 %copy-start.245 = (pred[128]{0:T(512)(128)(4,1)}, pred[128]{0:T(512)(128)(4,1)S(1)}, u32[]{:S(2)}) copy-start(pred[128]{0:T(512)(128)(4,1)S(1)} %iota_compare_fusion.17) | copy-start | bytes 388
  206.0 62.9 %copy-start.236 = (pred[128]{0:T(512)(128)(4,1)}, pred[128]{0:T(512)(128)(4,1)S(1)}, u32[]{:S(2)}) copy-start(pred[128]{0:T(512)(128)(4,1)S(1)} %get-tuple-element.371) | copy-start | bytes 388
  206.7 62.3 %copy-start.238 = (s32[128]{0:T(128)}, s32[128]{0:T(128)S(1)}, u32[]{:S(2)}) copy-start(s32[128]{0:T(128)S(1)} %get-tuple-element.361) | copy-start | bytes 1540
  439.4 394.6 %copy-start.220 = (f32[128]{0:T(128)}, f32[128]{0:T(128)S(1)}, u32[]{:S(2)}) copy-start(f32[128]{0:T(128)S(1)} %get-tuple-element.373) | copy-start | bytes 1540
  441.6 83.0 %copy-start.263 = (bf16[2,48,1152]{2,1,0:T(8,128)(2,1)S(1)}, bf16[2,48,1152]{2,1,0:T(8,128)(2,1)}, u32[]{:S(2)}) copy-start(bf16[2,48,1152]{2,1,0:T(8,128)(2,1)} %get-tuple-element.97) | copy-start | bytes 663556
  441.6 84.5 %copy-start.169 = (f32[128,8]{0,1:T(8,128)S(1)}, f32[128,8]{0,1:T(8,128)}, u32[]{:S(2)}) copy-start(f32[128,8]{0,1:T(8,128)} %get-tuple-element.318) | copy-start | bytes 12292
  441.6 84.5 %copy-start.207 = (s32[128]{0:T(128)S(1)}, s32[128]{0:T(128)}, u32[]{:S(2)}) copy-start(s32[128]{0:T(128)} %get-tuple-element.364) | copy-start | bytes 1540
  441.6 84.5 %copy-start.211 = (s32[128]{0:T(128)S(1)}, s32[128]{0:T(128)}, u32[]{:S(2)}) copy-start(s32[128]{0:T(128)} %get-tuple-element.356) | copy-start | bytes 1540
  589.2 17.4 %collective-permute-start = (f32[8,2304]{1,0:T(8,128)}, f32[8,2304]{1,0:T(8,128)}, u32[]{:S(2)}, u32[]{:S(2)}) collective-permute-start(f32[8,2304]{1,0:T(8,128)} %slice.416), channel_id=1, source_target_pairs={{1,0},{2,1},{3,2},{4,3},{5,4},{6,5},{7,6},{8,7},{9,8},{10,9},{11,1... | collective-permute-start | bytes 221192 | tf_op jit(solution)/shard_map/ppermute | solution.py:1258
  622.9 62.9 %copy-start.168 = (bf16[2,48,1152]{2,1,0:T(8,128)(2,1)S(1)}, bf16[2,48,1152]{2,1,0:T(8,128)(2,1)}, u32[]{:S(2)}) copy-start(bf16[2,48,1152]{2,1,0:T(8,128)(2,1)} %broadcast_select_fusion.11) | copy-start | bytes 663556
  622.9 62.9 %copy-start.223 = (pred[128]{0:T(512)(128)(4,1)S(1)}, pred[128]{0:T(512)(128)(4,1)}, u32[]{:S(2)}) copy-start(pred[128]{0:T(512)(128)(4,1)} %get-tuple-element.372) | copy-start | bytes 388
  622.9 62.9 %copy-start.225 = (s32[128]{0:T(128)S(1)}, s32[128]{0:T(128)}, u32[]{:S(2)}) copy-start(s32[128]{0:T(128)} %get-tuple-element.310) | copy-start | bytes 1540
  753.6 3.3 collective-permute-start.1
  768.1 64.4 %copy-start.229 = (pred[128]{0:T(512)(128)(4,1)S(1)}, pred[128]{0:T(512)(128)(4,1)}, u32[]{:S(2)}) copy-start(pred[128]{0:T(512)(128)(4,1)} %get-tuple-element.367) | copy-start | bytes 388
  768.1 64.4 %copy-start.231 = (s32[128]{0:T(128)S(1)}, s32[128]{0:T(128)}, u32[]{:S(2)}) copy-start(s32[128]{0:T(128)} %get-tuple-element.363) | copy-start | bytes 1540
  768.1 64.4 %copy-start.264 = (bf16[2,48,1152]{2,1,0:T(8,128)(2,1)S(1)}, bf16[2,48,1152]{2,1,0:T(8,128)(2,1)}, u32[]{:S(2)}) copy-start(bf16[2,48,1152]{2,1,0:T(8,128)(2,1)} %get-tuple-element.97) | copy-start | bytes 663556
  901.4 25.1 %collective-permute-start.2 = (f32[8,2304]{1,0:T(8,128)S(1)}, f32[8,2304]{1,0:T(8,128)S(1)}, u32[]{:S(2)}, u32[]{:S(2)}) collective-permute-start(f32[8,2304]{1,0:T(8,128)S(1)} %slice.433), channel_id=1, source_target_pairs={{1,0},{2,1},{3,2},{4,3},{5,4},{6,5},{7,6},{8,7},{9,8},{10,9},{11,1... | collective-permute-start | bytes 221192 | tf_op jit(solution)/shard_map/ppermute | solution.py:1258
  (250 other events, 1462.9 us)

commit v4 on v3

--- a/solution.py
+++ b/solution.py
@@ -635,7 +635,7 @@
         out_specs=out_specs,
         out_shape=[shape_of(*shape, dtype=bf16) for shape in shapes],
         scratch_shapes=[pltpu.VMEM(up.shape, bf16), pltpu.VMEM(down.shape, bf16), dma((2,))] + scratch,
-        compiler_params=comm_params(number, 60),
+        compiler_params=comm_params(number, 40 if number == 2 and count <= 8 else 60),
         name="experts_both" if number == 7 else "experts_forward" if ahead else "experts_backward",
     )(*(ahead or ()), *(behind or ()), up, down)
 

time: 1120 us -> 1100 us (0.982)
    unnamed x552 -> x678, local copies, waits for them, and re-layouts: 32.9 us -> 41 us
where the time goes in v4:
time: 1100 us; the launch traced here: 1090 us
  Pallas kernels  818 us (74%)
  matrix products  126 us (11%)
  other arithmetic  72.2 us (7%)
  local copies, waits for them, and re-layouts  67.2 us (6%)
    pallas_call x5, Pallas kernels, experts(): pl.pallas_call(functools.partial(experts_kernel, count, bool(ahead), bool...  322 us
    pallas_call x1, Pallas kernels, grads_reduce(): pl.pallas_call(functools.partial(grads_reduce_kernel, count, micro), in_s...  156 us
    pallas_call x1, Pallas kernels, weights_gather(): pl.pallas_call(functools.partial(weights_gather_kernel, count, parts), in...  150 us
    pallas_call x3, Pallas kernels, mixer_backward(): pl.pallas_call(functools.partial(mixer_backward_kernel, count), in_specs=...  115 us
    dot_general x36, matrix products, dot(): lax.dot_general(a, b, (dims, ((), ())), preferred_element_type=f32)  114 us
    pallas_call x3, Pallas kernels, mixer_forward(): pl.pallas_call(functools.partial(mixer_forward_kernel, count), in_specs=[...  75.4 us
    unnamed x678, local copies, waits for them, and re-layouts  41 us
  transfers between devices with their start and end apart: 3, of which 1 were waited for; matrix products, arithmetic and copies ran while one was open for 3% of the time, Pallas kernels for 0%

profile of v4, /device:TPU:0, one launch (start us, length us, event | category | flops | bytes accessed | tf_op | source)
XLA Modules:
  0.0 1093.0 jit_solution(1961694136101078452)
XLA Ops:
  4.5 149.9 %weights_gather.1 = (bf16[2,16,1152]{2,1,0:T(8,128)(2,1)S(1)}, bf16[8,144,1536]{2,1,0:T(8,128)(2,1)}, bf16[4,384,1152]{2,1,0:T(8,128)(2,1)}, bf16[2,8,144,1152]{...) custom-call(bf16[2,128,1152]{2,1,0:T(8,128)(2,1)S(1)} %copy-done.19,, ...), custom_call_target="tpu_custom_call" | custom-call | tf_op jit(solution)/shard_map/weights_gather/pallas_call | solution.py:828
  160.0 6.7 fusion.155
  175.4 25.4 %mixer_forward.3 = (f32[128,2304]{1,0:T(8,128)S(1)}, f32[16,16,2304]{2,1,0:T(8,128)}) custom-call(f32[128,2304]{1,0:T(8,128)S(1)} %get-tuple-element.379.step_ref, f32[128,2304]{1,0:T(8,128)S(1)} %get-tuple-element.378.drive_ref, f32[128,16,128]{2,1,0:T(8,128)S(1)} %broadcast_in_dim.91.bb_ref, f32[128,16,128]{2,1,0:T(8,128)S(1)} %broadcast_in_dim.92.cb_ref, ...), custom_call_target="tpu_custom_call" | custom-call | tf_op jit(solution)/shard_map/mixer_forward/pallas_call | solution.py:1180
  210.9 58.1 %experts_forward.2 = (bf16[2,48,1152]{2,1,0:T(8,128)(2,1)}, bf16[128,1152]{1,0:T(8,128)(2,1)}, bf16[128,1152]{1,0:T(8,128)(2,1)}, bf16[16,1152]{1,0:T(8,128)(2,1)}, bf16[8,2,48,1152]{3,2,1,0:T(8,128)(2,1)}) custom-call(bf16[2,48,1152]{2,1,0:T(8,128)(2,1)} %bitcast.291, f32[128,1152]{1,0:T(8,128)} %copy-done.93, bf16[128,96]{1,0:T(8,128)(2,1)} %get-tuple-element.407.refs_2_, ...), custom_call_target="tpu_custom_call" | custom-call | tf_op jit(solution)/shard_map/experts_forward/pallas_call | solution.py:632
  269.9 6.6 fusion.153
  286.7 24.9 %mixer_forward.4 = (f32[128,2304]{1,0:T(8,128)S(1)}, f32[16,16,2304]{2,1,0:T(8,128)}) custom-call(f32[128,2304]{1,0:T(8,128)S(1)} %get-tuple-element.334.step_ref, f32[128,2304]{1,0:T(8,128)S(1)} %get-tuple-element.333.drive_ref, f32[128,16,128]{2,1,0:T(8,128)S(1)} %broadcast_in_dim.93.bb_ref, f32[128,16,128]{2,1,0:T(8,128)S(1)} %broadcast_in_dim.94.cb_ref, ...), custom_call_target="tpu_custom_call" | custom-call | tf_op jit(solution)/shard_map/mixer_forward/pallas_call | solution.py:1180
  322.0 61.2 %experts_forward.3 = (bf16[2,48,1152]{2,1,0:T(8,128)(2,1)}, bf16[128,1152]{1,0:T(8,128)(2,1)}, bf16[128,1152]{1,0:T(8,128)(2,1)}, bf16[16,1152]{1,0:T(8,128)(2,1)}, bf16[8,2,48,1152]{3,2,1,0:T(8,128)(2,1)}) custom-call(bf16[2,48,1152]{2,1,0:T(8,128)(2,1)} %bitcast.290, f32[128,1152]{1,0:T(8,128)} %copy-done.67, bf16[128,96]{1,0:T(8,128)(2,1)} %get-tuple-element.406.refs_2_, ...), custom_call_target="tpu_custom_call" | custom-call | tf_op jit(solution)/shard_map/experts_forward/pallas_call | solution.py:632
  384.9 9.6 broadcast_select_fusion.4
  403.6 25.0 %mixer_forward.5 = (f32[128,2304]{1,0:T(8,128)S(1)}, f32[16,16,2304]{2,1,0:T(8,128)}) custom-call(f32[128,2304]{1,0:T(8,128)S(1)} %copy-done.37, f32[128,2304]{1,0:T(8,128)S(1)} %copy-done.36, f32[128,16,128]{2,1,0:T(8,128)S(1)} %broadcast_in_dim.95.bb_ref, f32[128,16,128]{2,1,0:T(8,128)S(1)} %broadcast_in_dim.96.cb_ref, f32[16,2304]{1,0:T(8,128)S(1)} %fusion.200.a_ref), custom_call_target="tpu_custom_call" | custom-call | tf_op jit(solution)/shard_map/mixer_forward/pallas_call | solution.py:1180
  428.7 5.7 multiply_reduce_fusion.17
  442.8 83.0 %experts_both.1 = (bf16[2,48,1152]{2,1,0:T(8,128)(2,1)}, bf16[128,1152]{1,0:T(8,128)(2,1)}, bf16[8,2,48,1152]{3,2,1,0:T(8,128)(2,1)}, bf16[128,1152]{1,0:T(8,128...) custom-call(bf16[2,48,1152]{2,1,0:T(8,128)(2,1)} %bitcast.289, ...), custom_call_target="tpu_custom_call" | custom-call | tf_op jit(solution)/shard_map/experts_both/pallas_call | solution.py:632
  531.6 5.9 fusion.342
  537.6 38.8 %mixer_backward.3 = (f32[128,2304]{1,0:T(8,128)S(1)}, f32[128,2304]{1,0:T(8,128)}, f32[128,16,128]{2,1,0:T(8,128)S(1)}, f32[128,16,128]{2,1,0:T(8,128)S(1)}, f32[16,2304]{1,0:T(8,128)S(1)}) custom-call(f32[128,2304]{1,0:T(8,128)} %copy-done.2, f32[128,2304]{1,0:T(8,128)} %copy-done.1, f32[128,2304]{1,0:T(8,128)} %get-tuple-element.327.dy_ref, ...), custom_call_target="tpu_custom_call" | custom-call | tf_op jit(solution)/shard_map/mixer_backward/pallas_call | solution.py:1210
  604.7 6.6 multiply_convert_fusion
  611.5 6.2 fusion.126
  619.3 58.7 %experts_backward.2 = (bf16[128,1152]{1,0:T(8,128)(2,1)S(1)}, bf16[2,48,1152]{2,1,0:T(8,128)(2,1)S(1)}, bf16[8,2,48,1152]{3,2,1,0:T(8,128)(2,1)S(1)}, bf16[8,96,...) custom-call(bf16[128,1152]{1,0:T(8,128)(2,1)S(1)} %fusion.120.refs_0_, bf16[128,1152]{1,0:T(8,128)(2,1)S(1)} %copy-done.38, ...), custom_call_target="tpu_custom_call" | custom-call | tf_op jit(solution)/shard_map/experts_backward/pallas_call | solution.py:632
  685.3 6.1 fusion.52
  692.4 38.0 %mixer_backward.4 = (f32[128,2304]{1,0:T(8,128)S(1)}, f32[128,2304]{1,0:T(8,128)}, f32[128,16,128]{2,1,0:T(8,128)S(1)}, f32[128,16,128]{2,1,0:T(8,128)S(1)}, f32[16,2304]{1,0:T(8,128)S(1)}) custom-call(f32[128,2304]{1,0:T(8,128)} %get-tuple-element.337.step_ref, f32[128,2304]{1,0:T(8,128)} %get-tuple-element.338.drive_ref, ...), custom_call_target="tpu_custom_call" | custom-call | tf_op jit(solution)/shard_map/mixer_backward/pallas_call | solution.py:1210
  761.1 60.5 %experts_backward.3 = (bf16[128,1152]{1,0:T(8,128)(2,1)S(1)}, bf16[2,48,1152]{2,1,0:T(8,128)(2,1)S(1)}, bf16[8,2,48,1152]{3,2,1,0:T(8,128)(2,1)S(1)}, bf16[8,96,...) custom-call(bf16[128,1152]{1,0:T(8,128)(2,1)S(1)} %get-tuple-element.300.refs_0_, ...), custom_call_target="tpu_custom_call" | custom-call | tf_op jit(solution)/shard_map/experts_backward/pallas_call | solution.py:632
  833.6 38.0 %mixer_backward.5 = (f32[128,2304]{1,0:T(8,128)S(1)}, f32[128,2304]{1,0:T(8,128)}, f32[128,16,128]{2,1,0:T(8,128)S(1)}, f32[128,16,128]{2,1,0:T(8,128)S(1)}, f32[16,2304]{1,0:T(8,128)S(1)}) custom-call(f32[128,2304]{1,0:T(8,128)} %copy-done.2, f32[128,2304]{1,0:T(8,128)} %copy-done.1, f32[128,2304]{1,0:T(8,128)} %get-tuple-element.292.dy_ref, ...), custom_call_target="tpu_custom_call" | custom-call | tf_op jit(solution)/shard_map/mixer_backward/pallas_call | solution.py:1210
  892.0 7.5 convolution_convert_fusion
  899.6 8.6 fusion.3
  916.0 156.3 %grads_reduce.1 = (bf16[4,144,3072]{2,1,0:T(8,128)(2,1)}, f32[144,1152]{1,0:T(8,128)}, f32[144,1152]{1,0:T(8,128)}, f32[144,1152]{1,0:T(8,128)}, f32[144,256]{1,0:T(8,128)}) custom-call(bf16[2,1152,256]{2,1,0:T(8,128)(2,1)} %bitcast.284, bf16[8,144,1536]{2,1,0:T(8,128)(2,1)} %bitcast.285, bf16[128,1152]{1,0:T(8,128)(2,1)} %get-tuple-element.343.refs_0_, ...), custom_call_target="tpu_custom_call" | custom-call | tf_op jit(solution)/shard_map/grads_reduce/pallas_call | solution.py:1047
  1082.6 6.0 bitcast_convert_fusion
  (893 shorter events, 194.0 us)
Async XLA Ops:
  154.5 124.1 %copy-start.8 = (bf16[2,8,144,256]{3,2,1,0:T(8,128)(2,1)}, bf16[2,8,144,256]{3,2,1,0:T(8,128)(2,1)S(1)}, u32[]{:S(2)}) copy-start(bf16[2,8,144,256]{3,2,1,0:T(8,128)(2,1)S(1)} %get-tuple-element.77) | copy-start | bytes 3538948
  157.0 112.9 %copy-start.204 = (f32[1152]{0:T(1024)}, f32[1152]{0:T(1024)S(1)}, u32[]{:S(2)}) copy-start(f32[1152]{0:T(1024)S(1)} %get-tuple-element.257) | copy-start | bytes 13828
  157.2 119.4 %copy-start.152 = (f32[2304]{0:T(1024)}, f32[2304]{0:T(1024)S(1)}, u32[]{:S(2)}) copy-start(f32[2304]{0:T(1024)S(1)} %get-tuple-element.252) | copy-start | bytes 27652
  157.2 119.4 %copy-start.157 = (f32[2304]{0:T(1024)}, f32[2304]{0:T(1024)S(1)}, u32[]{:S(2)}) copy-start(f32[2304]{0:T(1024)S(1)} %get-tuple-element.253) | copy-start | bytes 27652
  157.2 119.4 %copy-start.162 = (f32[2304]{0:T(1024)}, f32[2304]{0:T(1024)S(1)}, u32[]{:S(2)}) copy-start(f32[2304]{0:T(1024)S(1)} %get-tuple-element.254) | copy-start | bytes 27652
  157.2 119.4 %copy-start.167 = (f32[2304]{0:T(1024)}, f32[2304]{0:T(1024)S(1)}, u32[]{:S(2)}) copy-start(f32[2304]{0:T(1024)S(1)} %get-tuple-element.255) | copy-start | bytes 27652
  157.3 119.4 %copy-start.179 = (f32[2304]{0:T(1024)}, f32[2304]{0:T(1024)S(1)}, u32[]{:S(2)}) copy-start(f32[2304]{0:T(1024)S(1)} %get-tuple-element.256) | copy-start | bytes 27652
  157.3 121.8 %copy-start.301 = (pred[128]{0:T(512)(128)(4,1)}, pred[128]{0:T(512)(128)(4,1)S(1)}, u32[]{:S(2)}) copy-start(pred[128]{0:T(512)(128)(4,1)S(1)} %iota_compare_fusion.17) | copy-start | bytes 388
  171.1 366.5 %copy-start.12 = (f32[16,2304]{1,0:T(8,128)}, f32[16,2304]{1,0:T(8,128)S(1)}, u32[]{:S(2)}) copy-start(f32[16,2304]{1,0:T(8,128)S(1)} %fusion.200.a_ref) | copy-start | bytes 442372
  285.4 252.2 %copy-start.3 = (f32[128,16,128]{2,1,0:T(8,128)}, f32[128,16,128]{2,1,0:T(8,128)S(1)}, u32[]{:S(2)}) copy-start(f32[128,16,128]{2,1,0:T(8,128)S(1)} %broadcast_in_dim.93.bb_ref) | copy-start | bytes 3145732
  428.6 176.0 %copy-start.34 = (f32[128,2304]{1,0:T(8,128)}, f32[128,2304]{1,0:T(8,128)S(1)}, u32[]{:S(2)}) copy-start(f32[128,2304]{1,0:T(8,128)S(1)} %get-tuple-element.92) | copy-start | bytes 3538948
  442.8 83.1 %copy-start.276 = (pred[128]{0:T(512)(128)(4,1)S(1)}, pred[128]{0:T(512)(128)(4,1)}, u32[]{:S(2)}) copy-start(pred[128]{0:T(512)(128)(4,1)} %get-tuple-element.368) | copy-start | bytes 388
  442.8 83.1 %copy-start.277 = (s32[128]{0:T(128)S(1)}, s32[128]{0:T(128)}, u32[]{:S(2)}) copy-start(s32[128]{0:T(128)} %get-tuple-element.355) | copy-start | bytes 1540
  442.8 83.1 %copy-start.321 = (bf16[2,48,1152]{2,1,0:T(8,128)(2,1)S(1)}, bf16[2,48,1152]{2,1,0:T(8,128)(2,1)}, u32[]{:S(2)}) copy-start(bf16[2,48,1152]{2,1,0:T(8,128)(2,1)} %get-tuple-element.97) | copy-start | bytes 663556
  442.8 84.6 %copy-start.199 = (f32[128,8]{0,1:T(8,128)S(1)}, f32[128,8]{0,1:T(8,128)}, u32[]{:S(2)}) copy-start(f32[128,8]{0,1:T(8,128)} %get-tuple-element.318) | copy-start | bytes 12292
  442.8 84.6 %copy-start.248 = (s32[128]{0:T(128)S(1)}, s32[128]{0:T(128)}, u32[]{:S(2)}) copy-start(s32[128]{0:T(128)} %get-tuple-element.364) | copy-start | bytes 1540
  442.8 84.6 %copy-start.255 = (s32[128]{0:T(128)S(1)}, s32[128]{0:T(128)}, u32[]{:S(2)}) copy-start(s32[128]{0:T(128)} %get-tuple-element.356) | copy-start | bytes 1540
  442.8 84.6 %copy-start.270 = (f32[128]{0:T(128)S(1)}, f32[128]{0:T(128)}, u32[]{:S(2)}) copy-start(f32[128]{0:T(128)} %get-tuple-element.375) | copy-start | bytes 1540
  588.8 15.9 %collective-permute-start = (f32[8,2304]{1,0:T(8,128)S(1)}, f32[8,2304]{1,0:T(8,128)S(1)}, u32[]{:S(2)}, u32[]{:S(2)}) collective-permute-start(f32[8,2304]{1,0:T(8,128)S(1)} %slice.416), channel_id=1, source_target_pairs={{1,0},{2,1},{3,2},{4,3},{5,4},{6,5},{7,6},{8,7},{9,8},{10,9},{11,1... | collective-permute-start | bytes 221192 | tf_op jit(solution)/shard_map/ppermute | solution.py:1258
  604.7 79.1 %slice-start = ((s8[5308416]{0:T(1024)(128)(4,1)}), s8[4194304]{0:T(1024)(128)(4,1)S(1)}, s32[]{:S(2)}) async-start(s8[5308416]{0:T(1024)(128)(4,1)} %bitcast.278), calls=%async_computation | async-start | bytes 8388608
  746.8 3.2 collective-permute-start.1
  750.0 77.8 %slice-start.2 = ((s8[5308416]{0:T(1024)(128)(4,1)}), s8[4194304]{0:T(1024)(128)(4,1)S(1)}, s32[]{:S(2)}) async-start(s8[5308416]{0:T(1024)(128)(4,1)} %bitcast.281), calls=%async_computation.2 | async-start | bytes 8388608
  753.7 74.0 %slice-start.3 = ((s8[5308416]{0:T(1024)(128)(4,1)}), s8[1114112]{0:T(1024)(128)(4,1)S(1)}, s32[]{:S(2)}) async-start(s8[5308416]{0:T(1024)(128)(4,1)} %bitcast.281), calls=%async_computation.3 | async-start | bytes 2228224
  883.3 25.0 %collective-permute-start.2 = (f32[8,2304]{1,0:T(8,128)S(1)}, f32[8,2304]{1,0:T(8,128)S(1)}, u32[]{:S(2)}, u32[]{:S(2)}) collective-permute-start(f32[8,2304]{1,0:T(8,128)S(1)} %slice.433), channel_id=1, source_target_pairs={{1,0},{2,1},{3,2},{4,3},{5,4},{6,5},{7,6},{8,7},{9,8},{10,9},{11,1... | collective-permute-start | bytes 221192 | tf_op jit(solution)/shard_map/ppermute | solution.py:1258
  (313 other events, 2732.2 us)

commit v5 on v4

--- a/solution.py
+++ b/solution.py
@@ -635,7 +635,7 @@
         out_specs=out_specs,
         out_shape=[shape_of(*shape, dtype=bf16) for shape in shapes],
         scratch_shapes=[pltpu.VMEM(up.shape, bf16), pltpu.VMEM(down.shape, bf16), dma((2,))] + scratch,
-        compiler_params=comm_params(number, 40 if number == 2 and count <= 8 else 60),
+        compiler_params=comm_params(number, {2: 40, 7: 46}.get(number, 60) if count <= 8 else 60),
         name="experts_both" if number == 7 else "experts_forward" if ahead else "experts_backward",
     )(*(ahead or ()), *(behind or ()), up, down)
 

time: 1100 us -> 1110 us (level)
    unnamed x678 -> x668, local copies, waits for them, and re-layouts: 41 us -> 40.6 us
where the time goes in v5:
time: 1110 us; the launch traced here: 1090 us
  Pallas kernels  816 us (74%)
  matrix products  123 us (11%)
  local copies, waits for them, and re-layouts  73.7 us (7%)
  other arithmetic  70.9 us (6%)
    pallas_call x5, Pallas kernels, experts(): pl.pallas_call(functools.partial(experts_kernel, count, bool(ahead), bool...  319 us
    pallas_call x1, Pallas kernels, grads_reduce(): pl.pallas_call(functools.partial(grads_reduce_kernel, count, micro), in_s...  157 us
    pallas_call x1, Pallas kernels, weights_gather(): pl.pallas_call(functools.partial(weights_gather_kernel, count, parts), in...  150 us
    pallas_call x3, Pallas kernels, mixer_backward(): pl.pallas_call(functools.partial(mixer_backward_kernel, count), in_specs=...  115 us
    dot_general x36, matrix products, dot(): lax.dot_general(a, b, (dims, ((), ())), preferred_element_type=f32)  112 us
    pallas_call x3, Pallas kernels, mixer_forward(): pl.pallas_call(functools.partial(mixer_forward_kernel, count), in_specs=[...  75.6 us
    unnamed x668, local copies, waits for them, and re-layouts  40.6 us
  transfers between devices with their start and end apart: 3, of which 1 were waited for; matrix products, arithmetic and copies ran while one was open for 3% of the time, Pallas kernels for 0%

profile of v5, /device:TPU:0, one launch (start us, length us, event | category | flops | bytes accessed | tf_op | source)
XLA Modules:
  0.0 1094.3 jit_solution(1265309921436829189)
XLA Ops:
  4.5 149.9 %weights_gather.1 = (bf16[2,16,1152]{2,1,0:T(8,128)(2,1)S(1)}, bf16[8,144,1536]{2,1,0:T(8,128)(2,1)}, bf16[4,384,1152]{2,1,0:T(8,128)(2,1)}, bf16[2,8,144,1152]{...) custom-call(bf16[2,128,1152]{2,1,0:T(8,128)(2,1)S(1)} %copy-done.20,, ...), custom_call_target="tpu_custom_call" | custom-call | tf_op jit(solution)/shard_map/weights_gather/pallas_call | solution.py:828
  160.0 6.7 fusion.155
  175.4 25.4 %mixer_forward.3 = (f32[128,2304]{1,0:T(8,128)S(1)}, f32[16,16,2304]{2,1,0:T(8,128)}) custom-call(f32[128,2304]{1,0:T(8,128)S(1)} %get-tuple-element.379.step_ref, f32[128,2304]{1,0:T(8,128)S(1)} %get-tuple-element.378.drive_ref, f32[128,16,128]{2,1,0:T(8,128)S(1)} %broadcast_in_dim.91.bb_ref, f32[128,16,128]{2,1,0:T(8,128)S(1)} %broadcast_in_dim.92.cb_ref, ...), custom_call_target="tpu_custom_call" | custom-call | tf_op jit(solution)/shard_map/mixer_forward/pallas_call | solution.py:1180
  210.9 58.0 %experts_forward.2 = (bf16[2,48,1152]{2,1,0:T(8,128)(2,1)}, bf16[128,1152]{1,0:T(8,128)(2,1)}, bf16[128,1152]{1,0:T(8,128)(2,1)}, bf16[16,1152]{1,0:T(8,128)(2,1)}, bf16[8,2,48,1152]{3,2,1,0:T(8,128)(2,1)}) custom-call(bf16[2,48,1152]{2,1,0:T(8,128)(2,1)} %bitcast.292, f32[128,1152]{1,0:T(8,128)} %copy-done.103, bf16[128,96]{1,0:T(8,128)(2,1)} %get-tuple-element.407.refs_2_, ...), custom_call_target="tpu_custom_call" | custom-call | tf_op jit(solution)/shard_map/experts_forward/pallas_call | solution.py:632
  269.9 6.6 fusion.153
  285.9 25.0 %mixer_forward.4 = (f32[128,2304]{1,0:T(8,128)S(1)}, f32[16,16,2304]{2,1,0:T(8,128)}) custom-call(f32[128,2304]{1,0:T(8,128)S(1)} %get-tuple-element.334.step_ref, f32[128,2304]{1,0:T(8,128)S(1)} %get-tuple-element.333.drive_ref, f32[128,16,128]{2,1,0:T(8,128)S(1)} %broadcast_in_dim.93.bb_ref, f32[128,16,128]{2,1,0:T(8,128)S(1)} %broadcast_in_dim.94.cb_ref, ...), custom_call_target="tpu_custom_call" | custom-call | tf_op jit(solution)/shard_map/mixer_forward/pallas_call | solution.py:1180
  321.3 61.4 %experts_forward.3 = (bf16[2,48,1152]{2,1,0:T(8,128)(2,1)}, bf16[128,1152]{1,0:T(8,128)(2,1)}, bf16[128,1152]{1,0:T(8,128)(2,1)}, bf16[16,1152]{1,0:T(8,128)(2,1)}, bf16[8,2,48,1152]{3,2,1,0:T(8,128)(2,1)}) custom-call(bf16[2,48,1152]{2,1,0:T(8,128)(2,1)} %bitcast.291, f32[128,1152]{1,0:T(8,128)} %copy-done.77, bf16[128,96]{1,0:T(8,128)(2,1)} %get-tuple-element.406.refs_2_, ...), custom_call_target="tpu_custom_call" | custom-call | tf_op jit(solution)/shard_map/experts_forward/pallas_call | solution.py:632
  384.3 9.6 broadcast_select_fusion.4
  406.3 25.1 %mixer_forward.5 = (f32[128,2304]{1,0:T(8,128)S(1)}, f32[16,16,2304]{2,1,0:T(8,128)}) custom-call(f32[128,2304]{1,0:T(8,128)S(1)} %copy-done.42, f32[128,2304]{1,0:T(8,128)S(1)} %get-tuple-element.389.drive_ref, f32[128,16,128]{2,1,0:T(8,128)S(1)} %broadcast_in_dim.95.bb_ref, f32[128,16,128]{2,1,0:T(8,128)S(1)} %broadcast_in_dim.96.cb_ref, ...), custom_call_target="tpu_custom_call" | custom-call | tf_op jit(solution)/shard_map/mixer_forward/pallas_call | solution.py:1180
  431.5 5.8 multiply_reduce_fusion.17
  447.4 80.9 %experts_both.1 = (bf16[2,48,1152]{2,1,0:T(8,128)(2,1)S(1)}, bf16[128,1152]{1,0:T(8,128)(2,1)S(1)}, bf16[8,2,48,1152]{3,2,1,0:T(8,128)(2,1)S(1)}, bf16[128,1152]...) custom-call(bf16[2,48,1152]{2,1,0:T(8,128)(2,1)S(1)} %bitcast.254, ...), custom_call_target="tpu_custom_call" | custom-call | tf_op jit(solution)/shard_map/experts_both/pallas_call | solution.py:632
  534.2 5.9 fusion.342
  540.2 38.8 %mixer_backward.3 = (f32[128,2304]{1,0:T(8,128)S(1)}, f32[128,2304]{1,0:T(8,128)}, f32[128,16,128]{2,1,0:T(8,128)S(1)}, f32[128,16,128]{2,1,0:T(8,128)S(1)}, f32[16,2304]{1,0:T(8,128)S(1)}) custom-call(f32[128,2304]{1,0:T(8,128)} %copy-done.2, f32[128,2304]{1,0:T(8,128)} %copy-done.1, f32[128,2304]{1,0:T(8,128)} %get-tuple-element.327.dy_ref, ...), custom_call_target="tpu_custom_call" | custom-call | tf_op jit(solution)/shard_map/mixer_backward/pallas_call | solution.py:1210
  607.0 5.9 multiply_convert_fusion
  612.9 5.9 fusion.126
  620.5 58.7 %experts_backward.2 = (bf16[128,1152]{1,0:T(8,128)(2,1)S(1)}, bf16[2,48,1152]{2,1,0:T(8,128)(2,1)S(1)}, bf16[8,2,48,1152]{3,2,1,0:T(8,128)(2,1)S(1)}, bf16[8,96,...) custom-call(bf16[128,1152]{1,0:T(8,128)(2,1)S(1)} %fusion.120.refs_0_, bf16[128,1152]{1,0:T(8,128)(2,1)S(1)} %copy-done.43, ...), custom_call_target="tpu_custom_call" | custom-call | tf_op jit(solution)/shard_map/experts_backward/pallas_call | solution.py:632
  686.6 6.1 fusion.52
  693.7 38.1 %mixer_backward.4 = (f32[128,2304]{1,0:T(8,128)S(1)}, f32[128,2304]{1,0:T(8,128)}, f32[128,16,128]{2,1,0:T(8,128)S(1)}, f32[128,16,128]{2,1,0:T(8,128)S(1)}, f32[16,2304]{1,0:T(8,128)S(1)}) custom-call(f32[128,2304]{1,0:T(8,128)} %get-tuple-element.337.step_ref, f32[128,2304]{1,0:T(8,128)} %get-tuple-element.338.drive_ref, ...), custom_call_target="tpu_custom_call" | custom-call | tf_op jit(solution)/shard_map/mixer_backward/pallas_call | solution.py:1210
  762.4 60.4 %experts_backward.3 = (bf16[128,1152]{1,0:T(8,128)(2,1)S(1)}, bf16[2,48,1152]{2,1,0:T(8,128)(2,1)S(1)}, bf16[8,2,48,1152]{3,2,1,0:T(8,128)(2,1)S(1)}, bf16[8,96,...) custom-call(bf16[128,1152]{1,0:T(8,128)(2,1)S(1)} %get-tuple-element.300.refs_0_, ...), custom_call_target="tpu_custom_call" | custom-call | tf_op jit(solution)/shard_map/experts_backward/pallas_call | solution.py:632
  834.8 38.1 %mixer_backward.5 = (f32[128,2304]{1,0:T(8,128)S(1)}, f32[128,2304]{1,0:T(8,128)}, f32[128,16,128]{2,1,0:T(8,128)S(1)}, f32[128,16,128]{2,1,0:T(8,128)S(1)}, f32[16,2304]{1,0:T(8,128)S(1)}) custom-call(f32[128,2304]{1,0:T(8,128)} %copy-done.2, f32[128,2304]{1,0:T(8,128)} %copy-done.1, f32[128,2304]{1,0:T(8,128)} %get-tuple-element.292.dy_ref, ...), custom_call_target="tpu_custom_call" | custom-call | tf_op jit(solution)/shard_map/mixer_backward/pallas_call | solution.py:1210
  893.2 7.5 convolution_convert_fusion
  900.8 8.5 fusion.3
  917.2 156.5 %grads_reduce.1 = (bf16[4,144,3072]{2,1,0:T(8,128)(2,1)}, f32[144,1152]{1,0:T(8,128)}, f32[144,1152]{1,0:T(8,128)}, f32[144,1152]{1,0:T(8,128)}, f32[144,256]{1,0:T(8,128)}) custom-call(bf16[2,1152,256]{2,1,0:T(8,128)(2,1)} %bitcast.286, bf16[8,144,1536]{2,1,0:T(8,128)(2,1)} %bitcast.287, bf16[128,1152]{1,0:T(8,128)(2,1)} %get-tuple-element.343.refs_0_, ...), custom_call_target="tpu_custom_call" | custom-call | tf_op jit(solution)/shard_map/grads_reduce/pallas_call | solution.py:1047
  1083.9 6.0 bitcast_convert_fusion
  (883 shorter events, 198.1 us)
Async XLA Ops:
  154.5 124.0 %copy-start.8 = (bf16[2,8,144,256]{3,2,1,0:T(8,128)(2,1)}, bf16[2,8,144,256]{3,2,1,0:T(8,128)(2,1)S(1)}, u32[]{:S(2)}) copy-start(bf16[2,8,144,256]{3,2,1,0:T(8,128)(2,1)S(1)} %get-tuple-element.77) | copy-start | bytes 3538948
  157.1 112.8 %copy-start.200 = (f32[1152]{0:T(1024)}, f32[1152]{0:T(1024)S(1)}, u32[]{:S(2)}) copy-start(f32[1152]{0:T(1024)S(1)} %get-tuple-element.257) | copy-start | bytes 13828
  157.3 119.2 %copy-start.157 = (f32[2304]{0:T(1024)}, f32[2304]{0:T(1024)S(1)}, u32[]{:S(2)}) copy-start(f32[2304]{0:T(1024)S(1)} %get-tuple-element.252) | copy-start | bytes 27652
  157.3 119.2 %copy-start.162 = (f32[2304]{0:T(1024)}, f32[2304]{0:T(1024)S(1)}, u32[]{:S(2)}) copy-start(f32[2304]{0:T(1024)S(1)} %get-tuple-element.253) | copy-start | bytes 27652
  157.3 119.2 %copy-start.166 = (f32[2304]{0:T(1024)}, f32[2304]{0:T(1024)S(1)}, u32[]{:S(2)}) copy-start(f32[2304]{0:T(1024)S(1)} %get-tuple-element.254) | copy-start | bytes 27652
  157.3 119.2 %copy-start.170 = (f32[2304]{0:T(1024)}, f32[2304]{0:T(1024)S(1)}, u32[]{:S(2)}) copy-start(f32[2304]{0:T(1024)S(1)} %get-tuple-element.255) | copy-start | bytes 27652
  157.3 119.2 %copy-start.181 = (f32[2304]{0:T(1024)}, f32[2304]{0:T(1024)S(1)}, u32[]{:S(2)}) copy-start(f32[2304]{0:T(1024)S(1)} %get-tuple-element.256) | copy-start | bytes 27652
  157.3 121.6 %copy-start.297 = (pred[128]{0:T(512)(128)(4,1)}, pred[128]{0:T(512)(128)(4,1)S(1)}, u32[]{:S(2)}) copy-start(pred[128]{0:T(512)(128)(4,1)S(1)} %iota_compare_fusion.17) | copy-start | bytes 388
  171.1 369.0 %copy-start.12 = (f32[16,2304]{1,0:T(8,128)}, f32[16,2304]{1,0:T(8,128)S(1)}, u32[]{:S(2)}) copy-start(f32[16,2304]{1,0:T(8,128)S(1)} %fusion.200.a_ref) | copy-start | bytes 442372
  284.6 255.5 %copy-start.3 = (f32[128,16,128]{2,1,0:T(8,128)}, f32[128,16,128]{2,1,0:T(8,128)S(1)}, u32[]{:S(2)}) copy-start(f32[128,16,128]{2,1,0:T(8,128)S(1)} %broadcast_in_dim.93.bb_ref) | copy-start | bytes 3145732
  447.4 82.2 %copy-start.272 = (pred[128]{0:T(512)(128)(4,1)S(1)}, pred[128]{0:T(512)(128)(4,1)}, u32[]{:S(2)}) copy-start(pred[128]{0:T(512)(128)(4,1)} %get-tuple-element.368) | copy-start | bytes 388
  447.4 82.2 %copy-start.273 = (s32[128]{0:T(128)S(1)}, s32[128]{0:T(128)}, u32[]{:S(2)}) copy-start(s32[128]{0:T(128)} %get-tuple-element.355) | copy-start | bytes 1540
  447.4 82.2 %copy-start.316 = (bf16[2,48,1152]{2,1,0:T(8,128)(2,1)S(1)}, bf16[2,48,1152]{2,1,0:T(8,128)(2,1)}, u32[]{:S(2)}) copy-start(bf16[2,48,1152]{2,1,0:T(8,128)(2,1)} %get-tuple-element.97) | copy-start | bytes 663556
  447.4 82.6 %copy-start.195 = (f32[128,8]{0,1:T(8,128)S(1)}, f32[128,8]{0,1:T(8,128)}, u32[]{:S(2)}) copy-start(f32[128,8]{0,1:T(8,128)} %get-tuple-element.318) | copy-start | bytes 12292
  447.4 82.6 %copy-start.244 = (s32[128]{0:T(128)S(1)}, s32[128]{0:T(128)}, u32[]{:S(2)}) copy-start(s32[128]{0:T(128)} %get-tuple-element.364) | copy-start | bytes 1540
  447.4 82.6 %copy-start.251 = (s32[128]{0:T(128)S(1)}, s32[128]{0:T(128)}, u32[]{:S(2)}) copy-start(s32[128]{0:T(128)} %get-tuple-element.356) | copy-start | bytes 1540
  447.4 82.6 %copy-start.266 = (f32[128]{0:T(128)S(1)}, f32[128]{0:T(128)}, u32[]{:S(2)}) copy-start(f32[128]{0:T(128)} %get-tuple-element.375) | copy-start | bytes 1540
  589.1 17.7 %collective-permute-start = (f32[8,2304]{1,0:T(8,128)}, f32[8,2304]{1,0:T(8,128)}, u32[]{:S(2)}, u32[]{:S(2)}) collective-permute-start(f32[8,2304]{1,0:T(8,128)} %slice.416), channel_id=1, source_target_pairs={{1,0},{2,1},{3,2},{4,3},{5,4},{6,5},{7,6},{8,7},{9,8},{10,9},{11,1... | collective-permute-start | bytes 221192 | tf_op jit(solution)/shard_map/ppermute | solution.py:1258
  606.9 78.2 %slice-start = ((s8[5308416]{0:T(1024)(128)(4,1)}), s8[4194304]{0:T(1024)(128)(4,1)S(1)}, s32[]{:S(2)}) async-start(s8[5308416]{0:T(1024)(128)(4,1)} %bitcast.280), calls=%async_computation | async-start | bytes 8388608
  612.8 72.3 %copy-start.102 = (bf16[128,2304]{1,0:T(8,128)(2,1)}, bf16[128,2304]{1,0:T(8,128)(2,1)S(1)}, u32[]{:S(2)}) copy-start(bf16[128,2304]{1,0:T(8,128)(2,1)S(1)} %get-tuple-element.286.refs_14_) | copy-start | bytes 1769476
  748.1 3.2 collective-permute-start.1
  751.3 77.6 %slice-start.2 = ((s8[5308416]{0:T(1024)(128)(4,1)}), s8[4194304]{0:T(1024)(128)(4,1)S(1)}, s32[]{:S(2)}) async-start(s8[5308416]{0:T(1024)(128)(4,1)} %bitcast.283), calls=%async_computation.2 | async-start | bytes 8388608
  755.1 73.8 %slice-start.3 = ((s8[5308416]{0:T(1024)(128)(4,1)}), s8[1114112]{0:T(1024)(128)(4,1)S(1)}, s32[]{:S(2)}) async-start(s8[5308416]{0:T(1024)(128)(4,1)} %bitcast.283), calls=%async_computation.3 | async-start | bytes 2228224
  884.5 25.0 %collective-permute-start.2 = (f32[8,2304]{1,0:T(8,128)S(1)}, f32[8,2304]{1,0:T(8,128)S(1)}, u32[]{:S(2)}, u32[]{:S(2)}) collective-permute-start(f32[8,2304]{1,0:T(8,128)S(1)} %slice.433), channel_id=1, source_target_pairs={{1,0},{2,1},{3,2},{4,3},{5,4},{6,5},{7,6},{8,7},{9,8},{10,9},{11,1... | collective-permute-start | bytes 221192 | tf_op jit(solution)/shard_map/ppermute | solution.py:1258
  (308 other events, 2712.3 us)
